TPU v7x, 32 devices: a whole 2x2x4 slice. The times are simulated.
32 devices in a mesh: seq: 4 (over y, core), wt: 8 (over z, x).
Axes of the slice: x: 2, y: 2, z: 4, core: 2. Of those that a mesh axis runs over, the one named last changes fastest.
Arguments:
- activations: bfloat16 [16, 512, 768], P('wt', 'seq'), may hold values from -6 to 6
- upstream: bfloat16 [16, 512, 768], P('wt', 'seq'), may hold values from -6 to 6
- first_scale: bfloat16 [2, 768], P(None, 'wt'), may hold values from 0.5 to 1.5
- first_shift: bfloat16 [2, 768], P(None, 'wt'), may hold values from -1 to 1
- query_weight: bfloat16 [2, 768, 768], P(None, 'wt'), may hold values from -0.21875 to 0.21875
- query_bias: bfloat16 [2, 768], P(None, 'wt'), may hold values from -1 to 1
- key_weight: bfloat16 [2, 768, 768], P(None, 'wt'), may hold values from -0.21875 to 0.21875
- value_weight: bfloat16 [2, 768, 768], P(None, 'wt'), may hold values from -0.21875 to 0.21875
- value_bias: bfloat16 [2, 768], P(None, 'wt'), may hold values from -1 to 1
- output_weight: bfloat16 [2, 768, 768], P(None, 'wt'), may hold values from -0.75 to 0.75
- output_bias: bfloat16 [2, 768], P(None, 'wt'), may hold values from -1 to 1
- second_scale: bfloat16 [2, 768], P(None, 'wt'), may hold values from 0.5 to 1.5
- second_shift: bfloat16 [2, 768], P(None, 'wt'), may hold values from -1 to 1
- up_weight: bfloat16 [2, 768, 3072], P(None, 'wt'), may hold values from -0.21875 to 0.21875
- up_bias: bfloat16 [2, 3072], P(None, 'wt'), may hold values from -1 to 1
- down_weight: bfloat16 [2, 3072, 768], P(None, 'wt'), may hold values from -0.109375 to 0.109375
- down_bias: bfloat16 [2, 768], P(None, 'wt'), may hold values from -1 to 1
Outputs:
- result: bfloat16 [16, 512, 768], P('wt', 'seq')
- input_grad: float32 [16, 512, 768], P('wt', 'seq')
- first_scale_grad: float32 [2, 768], P(None, 'wt')
- first_shift_grad: float32 [2, 768], P(None, 'wt')
- query_weight_grad: float32 [2, 768, 768], P(None, 'wt')
- query_bias_grad: float32 [2, 768], P(None, 'wt')
- key_weight_grad: float32 [2, 768, 768], P(None, 'wt')
- value_weight_grad: float32 [2, 768, 768], P(None, 'wt')
- value_bias_grad: float32 [2, 768], P(None, 'wt')
- output_weight_grad: float32 [2, 768, 768], P(None, 'wt')
- output_bias_grad: float32 [2, 768], P(None, 'wt')
- second_scale_grad: float32 [2, 768], P(None, 'wt')
- second_shift_grad: float32 [2, 768], P(None, 'wt')
- up_weight_grad: float32 [2, 768, 3072], P(None, 'wt')
- up_bias_grad: float32 [2, 3072], P(None, 'wt')
- down_weight_grad: float32 [2, 3072, 768], P(None, 'wt')
- down_bias_grad: float32 [2, 768], P(None, 'wt')
All inputs are finite; a program needn't handle non-finite values.
Results may differ from a plain program's by a relative error of at most 0.015.
Values may be sent and summed in bfloat16 or wider, within the bound.
No kernel may reach another device: no remote copies, remote signals or barrier semaphores. Data moves between devices by JAX's collectives and lax.ppermute only.
A program may use at most 256 MiB of HBM per device.

v0:
```python
import math

import jax
import jax.numpy as jnp
from jax import lax
from jax.sharding import PartitionSpec as P

HEAD_DIM = 64
LAYERS = 2


epsilon = 1e-05


def layer_norm(values, scales, shifts):
    centred = values - jnp.mean(values, axis=-1, keepdims=True)
    spread = jnp.mean(centred * centred, axis=-1, keepdims=True)
    return centred * lax.rsqrt(spread + epsilon) * scales + shifts


def exact_gelu(values):
    return jax.nn.gelu(values, approximate=False)


def matmul(left, right):
    return jnp.dot(left, right, preferred_element_type=jnp.float32)


def left_product(left, right):
    return lax.dot_general(
        left, right, (((0,), (0,)), ((), ())), preferred_element_type=jnp.float32
    )


def right_product(left, right):
    return lax.dot_general(
        left, right, (((1,), (1,)), ((), ())), preferred_element_type=jnp.float32
    )


def column_sums(values):
    return jnp.sum(values, axis=0, dtype=jnp.float32)


def fetch_layer(shards, layer_index):
    pieces = tuple((member[layer_index] for member in shards))
    return (
        lax.all_gather(pieces[0], "wt", axis=0, tiled=True),
        lax.all_gather(pieces[1], "wt", axis=0, tiled=True),
        lax.all_gather(pieces[2], "wt", axis=0, tiled=True),
        lax.all_gather(pieces[3], "wt", axis=0, tiled=True),
        lax.all_gather(pieces[4], "wt", axis=0, tiled=True),
        lax.all_gather(pieces[5], "wt", axis=0, tiled=True),
        lax.all_gather(pieces[6], "wt", axis=0, tiled=True),
        lax.all_gather(pieces[7], "wt", axis=0, tiled=True),
        lax.all_gather(pieces[8], "wt", axis=0, tiled=True),
        lax.all_gather(pieces[9], "wt", axis=0, tiled=True),
        lax.all_gather(pieces[10], "wt", axis=0, tiled=True),
        lax.all_gather(pieces[11], "wt", axis=0, tiled=True),
        lax.all_gather(pieces[12], "wt", axis=0, tiled=True),
        lax.all_gather(pieces[13], "wt", axis=0, tiled=True),
        lax.all_gather(pieces[14], "wt", axis=0, tiled=True),
    )


def fetch_again(shards, layer_index):
    pieces = tuple((member[layer_index] for member in shards))
    return (
        lax.all_gather(pieces[0], "wt", axis=0, tiled=True),
        lax.all_gather(pieces[1], "wt", axis=0, tiled=True),
        lax.all_gather(pieces[2], "wt", axis=0, tiled=True),
        lax.all_gather(pieces[3], "wt", axis=0, tiled=True),
        lax.all_gather(pieces[4], "wt", axis=0, tiled=True),
        lax.all_gather(pieces[5], "wt", axis=0, tiled=True),
        lax.all_gather(pieces[6], "wt", axis=0, tiled=True),
        lax.all_gather(pieces[7], "wt", axis=0, tiled=True),
        lax.all_gather(pieces[8], "wt", axis=0, tiled=True),
        lax.all_gather(pieces[9], "wt", axis=0, tiled=True),
        lax.all_gather(pieces[10], "wt", axis=0, tiled=True),
        lax.all_gather(pieces[11], "wt", axis=0, tiled=True),
        lax.all_gather(pieces[12], "wt", axis=0, tiled=True),
        lax.all_gather(pieces[13], "wt", axis=0, tiled=True),
        lax.all_gather(pieces[14], "wt", axis=0, tiled=True),
    )


def scores_of(queries_h, keyset_h):
    factor = 1.0 / math.sqrt(HEAD_DIM)
    return (
        jnp.einsum("cqhd,ckhd->chqk", queries_h, keyset_h, preferred_element_type=jnp.float32)
        * factor
    )


def forward_layer(hidden, weights, clip_count, frames_here):
    (
        first_scale,
        first_shift,
        query_weight,
        query_bias,
        key_weight,
        value_weight,
        value_bias,
        output_weight,
        output_bias,
        second_scale,
        second_shift,
        up_weight,
        up_bias,
        down_weight,
        down_bias,
    ) = weights
    row_count, features = hidden.shape
    groups = lax.axis_size("seq")
    group_width = features // groups
    frames_all = frames_here * groups
    split_shape = (clip_count, frames_here, groups, group_width)
    heads_shape = (clip_count, frames_all, group_width // HEAD_DIM, HEAD_DIM)
    normed = layer_norm(
        hidden, first_scale.astype(jnp.float32), first_shift.astype(jnp.float32)
    ).astype(jnp.bfloat16)
    queries = (matmul(normed, query_weight) + query_bias.astype(jnp.float32)).astype(jnp.bfloat16)
    keyset = matmul(normed, key_weight).astype(jnp.bfloat16)
    valueset = (matmul(normed, value_weight) + value_bias.astype(jnp.float32)).astype(jnp.bfloat16)
    queries_h, keyset_h, valueset_h = (
        lax.all_to_all(
            queries.reshape(split_shape), "seq", split_axis=2, concat_axis=1, tiled=True
        ),
        lax.all_to_all(keyset.reshape(split_shape), "seq", split_axis=2, concat_axis=1, tiled=True),
        lax.all_to_all(
            valueset.reshape(split_shape), "seq", split_axis=2, concat_axis=1, tiled=True
        ),
    )
    queries_h = queries_h.reshape(heads_shape)
    keyset_h = keyset_h.reshape(heads_shape)
    valueset_h = valueset_h.reshape(heads_shape)
    scores = scores_of(queries_h, keyset_h)
    maxima = jnp.max(scores, axis=-1, keepdims=True)
    raised = jnp.exp(scores - maxima)
    totals = jnp.sum(raised, axis=-1, keepdims=True)
    logsum = maxima + jnp.log(totals)
    chances_low = (raised / totals).astype(jnp.bfloat16)
    mixture = jnp.einsum(
        "chqk,ckhd->cqhd", chances_low, valueset_h, preferred_element_type=jnp.float32
    ).astype(jnp.bfloat16)
    merged = lax.all_to_all(
        mixture.reshape(clip_count, frames_all, 1, group_width),
        "seq",
        split_axis=1,
        concat_axis=2,
        tiled=True,
    )
    mixture_rows = merged.reshape(row_count, features)
    middle = hidden + matmul(mixture_rows, output_weight) + output_bias.astype(jnp.float32)
    second = layer_norm(
        middle, second_scale.astype(jnp.float32), second_shift.astype(jnp.float32)
    ).astype(jnp.bfloat16)
    upward = matmul(second, up_weight) + up_bias.astype(jnp.float32)
    activated = exact_gelu(upward).astype(jnp.bfloat16)
    output = middle + matmul(activated, down_weight) + down_bias.astype(jnp.float32)
    stored = (
        hidden,
        normed,
        queries_h,
        keyset_h,
        valueset_h,
        logsum,
        mixture_rows,
        middle,
        second,
        upward,
        activated,
    )
    return (output, stored)


def backward_layer(grad_hidden, stored, weights, clip_count, frames_here):
    (
        first_scale,
        first_shift,
        query_weight,
        query_bias,
        key_weight,
        value_weight,
        value_bias,
        output_weight,
        output_bias,
        second_scale,
        second_shift,
        up_weight,
        up_bias,
        down_weight,
        down_bias,
    ) = weights
    (
        hidden,
        normed,
        queries_h,
        keyset_h,
        valueset_h,
        logsum,
        mixture_rows,
        middle,
        second,
        upward,
        activated,
    ) = stored
    row_count, features = hidden.shape
    groups = lax.axis_size("seq")
    group_width = features // groups
    frames_all = frames_here * groups
    split_shape = (clip_count, frames_here, groups, group_width)
    heads_shape = queries_h.shape
    factor = 1.0 / math.sqrt(HEAD_DIM)
    down_in = grad_hidden.astype(jnp.bfloat16)
    grad_down_weight = left_product(activated, down_in)
    grad_down_bias = column_sums(down_in)
    grad_activated = right_product(down_in, down_weight)
    gelu_value, gelu_pull = jax.vjp(exact_gelu, upward)
    grad_upward = gelu_pull(grad_activated)[0].astype(jnp.bfloat16)
    grad_up_weight = left_product(second, grad_upward)
    grad_up_bias = column_sums(grad_upward)
    grad_second = right_product(grad_upward, up_weight)
    norm_value, norm_pull = jax.vjp(
        layer_norm, middle, second_scale.astype(jnp.float32), second_shift.astype(jnp.float32)
    )
    grad_middle, grad_second_scale, grad_second_shift = norm_pull(grad_second)
    grad_middle = grad_hidden + grad_middle
    branch_in = grad_middle.astype(jnp.bfloat16)
    grad_output_weight = left_product(mixture_rows, branch_in)
    grad_output_bias = column_sums(branch_in)
    grad_mixture = right_product(branch_in, output_weight).astype(jnp.bfloat16)
    grad_mixture_h = lax.all_to_all(
        grad_mixture.reshape(split_shape), "seq", split_axis=2, concat_axis=1, tiled=True
    ).reshape(heads_shape)
    scores = scores_of(queries_h, keyset_h)
    chances = jnp.exp(scores - logsum)
    chances_low = chances.astype(jnp.bfloat16)
    grad_chances = jnp.einsum(
        "cqhd,ckhd->chqk", grad_mixture_h, valueset_h, preferred_element_type=jnp.float32
    )
    grad_valueset = jnp.einsum(
        "chqk,cqhd->ckhd", chances_low, grad_mixture_h, preferred_element_type=jnp.float32
    ).astype(jnp.bfloat16)
    inner = jnp.sum(grad_chances * chances, axis=-1, keepdims=True)
    grad_scores = (chances * (grad_chances - inner)).astype(jnp.bfloat16)
    grad_queries = (
        jnp.einsum("chqk,ckhd->cqhd", grad_scores, keyset_h, preferred_element_type=jnp.float32)
        * factor
    ).astype(jnp.bfloat16)
    grad_keyset = (
        jnp.einsum("chqk,cqhd->ckhd", grad_scores, queries_h, preferred_element_type=jnp.float32)
        * factor
    ).astype(jnp.bfloat16)
    back_shape = (clip_count, frames_all, 1, group_width)
    grad_q, grad_k, grad_v = (
        lax.all_to_all(
            grad_queries.reshape(back_shape), "seq", split_axis=1, concat_axis=2, tiled=True
        ),
        lax.all_to_all(
            grad_keyset.reshape(back_shape), "seq", split_axis=1, concat_axis=2, tiled=True
        ),
        lax.all_to_all(
            grad_valueset.reshape(back_shape), "seq", split_axis=1, concat_axis=2, tiled=True
        ),
    )
    grad_q = grad_q.reshape(row_count, features)
    grad_k = grad_k.reshape(row_count, features)
    grad_v = grad_v.reshape(row_count, features)
    grad_query_weight = left_product(normed, grad_q)
    grad_query_bias = column_sums(grad_q)
    grad_key_weight = left_product(normed, grad_k)
    grad_value_weight = left_product(normed, grad_v)
    grad_value_bias = column_sums(grad_v)
    grad_normed = (
        right_product(grad_q, query_weight)
        + right_product(grad_k, key_weight)
        + right_product(grad_v, value_weight)
    )
    first_value, first_pull = jax.vjp(
        layer_norm, hidden, first_scale.astype(jnp.float32), first_shift.astype(jnp.float32)
    )
    grad_before, grad_first_scale, grad_first_shift = first_pull(grad_normed)
    gradients = (
        grad_first_scale,
        grad_first_shift,
        grad_query_weight,
        grad_query_bias,
        grad_key_weight,
        grad_value_weight,
        grad_value_bias,
        grad_output_weight,
        grad_output_bias,
        grad_second_scale,
        grad_second_shift,
        grad_up_weight,
        grad_up_bias,
        grad_down_weight,
        grad_down_bias,
    )
    return (grad_middle + grad_before, gradients)


def owner_order(values):
    owners = lax.axis_size("wt")
    slices = lax.axis_size("seq")
    rows = values.shape[0]
    piece = rows // (owners * slices)
    rest = values.shape[1:]
    shaped = values.reshape((owners, slices, piece) + rest)
    return jnp.swapaxes(shaped, 0, 1).reshape((rows,) + rest)


def settle_layer(gradients):
    g = tuple((owner_order(member) for member in gradients))
    pieces = (
        lax.psum_scatter(g[0], ("seq", "wt"), scatter_dimension=0, tiled=True),
        lax.psum_scatter(g[1], ("seq", "wt"), scatter_dimension=0, tiled=True),
        lax.psum_scatter(g[2], ("seq", "wt"), scatter_dimension=0, tiled=True),
        lax.psum_scatter(g[3], ("seq", "wt"), scatter_dimension=0, tiled=True),
        lax.psum_scatter(g[4], ("seq", "wt"), scatter_dimension=0, tiled=True),
        lax.psum_scatter(g[5], ("seq", "wt"), scatter_dimension=0, tiled=True),
        lax.psum_scatter(g[6], ("seq", "wt"), scatter_dimension=0, tiled=True),
        lax.psum_scatter(g[7], ("seq", "wt"), scatter_dimension=0, tiled=True),
        lax.psum_scatter(g[8], ("seq", "wt"), scatter_dimension=0, tiled=True),
        lax.psum_scatter(g[9], ("seq", "wt"), scatter_dimension=0, tiled=True),
        lax.psum_scatter(g[10], ("seq", "wt"), scatter_dimension=0, tiled=True),
        lax.psum_scatter(g[11], ("seq", "wt"), scatter_dimension=0, tiled=True),
        lax.psum_scatter(g[12], ("seq", "wt"), scatter_dimension=0, tiled=True),
        lax.psum_scatter(g[13], ("seq", "wt"), scatter_dimension=0, tiled=True),
        lax.psum_scatter(g[14], ("seq", "wt"), scatter_dimension=0, tiled=True),
    )
    return (
        lax.all_gather(pieces[0].astype(jnp.bfloat16), "seq", axis=0, tiled=True).astype(
            jnp.float32
        ),
        lax.all_gather(pieces[1].astype(jnp.bfloat16), "seq", axis=0, tiled=True).astype(
            jnp.float32
        ),
        lax.all_gather(pieces[2].astype(jnp.bfloat16), "seq", axis=0, tiled=True).astype(
            jnp.float32
        ),
        lax.all_gather(pieces[3].astype(jnp.bfloat16), "seq", axis=0, tiled=True).astype(
            jnp.float32
        ),
        lax.all_gather(pieces[4].astype(jnp.bfloat16), "seq", axis=0, tiled=True).astype(
            jnp.float32
        ),
        lax.all_gather(pieces[5].astype(jnp.bfloat16), "seq", axis=0, tiled=True).astype(
            jnp.float32
        ),
        lax.all_gather(pieces[6].astype(jnp.bfloat16), "seq", axis=0, tiled=True).astype(
            jnp.float32
        ),
        lax.all_gather(pieces[7].astype(jnp.bfloat16), "seq", axis=0, tiled=True).astype(
            jnp.float32
        ),
        lax.all_gather(pieces[8].astype(jnp.bfloat16), "seq", axis=0, tiled=True).astype(
            jnp.float32
        ),
        lax.all_gather(pieces[9].astype(jnp.bfloat16), "seq", axis=0, tiled=True).astype(
            jnp.float32
        ),
        lax.all_gather(pieces[10].astype(jnp.bfloat16), "seq", axis=0, tiled=True).astype(
            jnp.float32
        ),
        lax.all_gather(pieces[11].astype(jnp.bfloat16), "seq", axis=0, tiled=True).astype(
            jnp.float32
        ),
        lax.all_gather(pieces[12].astype(jnp.bfloat16), "seq", axis=0, tiled=True).astype(
            jnp.float32
        ),
        lax.all_gather(pieces[13].astype(jnp.bfloat16), "seq", axis=0, tiled=True).astype(
            jnp.float32
        ),
        lax.all_gather(pieces[14].astype(jnp.bfloat16), "seq", axis=0, tiled=True).astype(
            jnp.float32
        ),
    )


def per_device(
    activations,
    upstream,
    first_scale,
    first_shift,
    query_weight,
    query_bias,
    key_weight,
    value_weight,
    value_bias,
    output_weight,
    output_bias,
    second_scale,
    second_shift,
    up_weight,
    up_bias,
    down_weight,
    down_bias,
):
    shards = (
        first_scale,
        first_shift,
        query_weight,
        query_bias,
        key_weight,
        value_weight,
        value_bias,
        output_weight,
        output_bias,
        second_scale,
        second_shift,
        up_weight,
        up_bias,
        down_weight,
        down_bias,
    )
    clip_count, frames_here, features = activations.shape
    row_count = clip_count * frames_here
    hidden = activations.astype(jnp.float32).reshape(row_count, features)
    kept_weights = []
    stored_layers = []
    for layer_index in range(LAYERS):
        weights = fetch_layer(shards, layer_index)
        kept_weights.append(None)
        hidden, stored = forward_layer(hidden, weights, clip_count, frames_here)
        stored_layers.append(stored)
    result = hidden.astype(jnp.bfloat16).reshape(clip_count, frames_here, features)
    grad_hidden = upstream.astype(jnp.float32).reshape(row_count, features)
    layer_grads = [None] * LAYERS
    for layer_index in reversed(range(LAYERS)):
        weights = fetch_again(shards, layer_index)
        grad_hidden, gradients = backward_layer(
            grad_hidden, stored_layers[layer_index], weights, clip_count, frames_here
        )
        layer_grads[layer_index] = settle_layer(gradients)
    final = tuple(
        (
            jnp.stack([layer_grads[layer_index][member] for layer_index in range(LAYERS)])
            for member in range(15)
        )
    )
    input_grad = grad_hidden.reshape(clip_count, frames_here, features)
    return (
        result,
        input_grad,
        final[0],
        final[1],
        final[2],
        final[3],
        final[4],
        final[5],
        final[6],
        final[7],
        final[8],
        final[9],
        final[10],
        final[11],
        final[12],
        final[13],
        final[14],
    )


def solution(mesh):
    in_specs = (
        P("wt", "seq", None),
        P("wt", "seq", None),
        P(None, "wt"),
        P(None, "wt"),
        P(None, "wt", None),
        P(None, "wt"),
        P(None, "wt", None),
        P(None, "wt", None),
        P(None, "wt"),
        P(None, "wt", None),
        P(None, "wt"),
        P(None, "wt"),
        P(None, "wt"),
        P(None, "wt", None),
        P(None, "wt"),
        P(None, "wt", None),
        P(None, "wt"),
    )
    out_specs = (
        P("wt", "seq", None),
        P("wt", "seq", None),
        P(None, "wt"),
        P(None, "wt"),
        P(None, "wt", None),
        P(None, "wt"),
        P(None, "wt", None),
        P(None, "wt", None),
        P(None, "wt"),
        P(None, "wt", None),
        P(None, "wt"),
        P(None, "wt"),
        P(None, "wt"),
        P(None, "wt", None),
        P(None, "wt"),
        P(None, "wt", None),
        P(None, "wt"),
    )
    return jax.shard_map(
        per_device, mesh=mesh, in_specs=in_specs, out_specs=out_specs, check_vma=False
    )
```

profile of v0, /device:TPU:0, one launch (start us, length us, event | category | flops | bytes accessed | tf_op | source)
XLA Modules:
  0.0 2099.1 jit_solution(13761848432321563579)
XLA Ops:
  39.0 39.0 %all-reduce.53 = (bf16[768]{0:T(1024)(128)(2,1)S(1)}, bf16[768]{0:T(1024)(128)(2,1)S(1)}, bf16[768]{0:T(1024)(128)(2,1)S(1)}, bf16[768]{0:T(1024)(128)(2,1)S(1)}...) all-reduce(bf16[768]{0:T(1024)(128)(2,1)} %dynamic-update-slice.4, ...), channel_id=10, replica_groups=mesh['seq'=4,'wt'=8] {'wt'}, use_global_device_ids=true, to_apply=%add.4 | all-reduce | flops 12288 | bytes 49152
  86.3 11.0 all-gather.45.cloned.1.call-done
  103.6 35.8 %all-gather.47.cloned.1.call-done = bf16[1,768,768]{2,1,0:T(8,128)(2,1)} async-done(((bf16[1,96,768]{2,1,0:T(8,128)(2,1)}), bf16[1,768,768]{2,1,0:T(8,128)(2,1)}) %all-gather.47.cloned.1.call-update) | async-done | bytes 1179664 | tf_op jit(solution)/shard_map/all_gather | solution.py:52
  146.9 6.4 all-to-all-done.2
  164.1 26.5 %all-gather.12 = bf16[1,3072]{1,0:T(2,128)(2,1)S(1)} all-gather(bf16[1,384]{1,0:T(2,128)(2,1)S(1)} %get-tuple-element.109), channel_id=14, replica_groups=mesh['seq'=4,'wt'=8] {'wt'}, dimensions={1}, use_global_device_ids=true | all-gather | bytes 6912 | tf_op jit(solution)/shard_map/all_gather | solution.py:60
  193.7 69.5 %all-gather.51.cloned.1.call-done = bf16[1,768,3072]{2,1,0:T(8,128)(2,1)} async-done(((bf16[1,96,3072]{2,1,0:T(8,128)(2,1)}), bf16[1,768,3072]{2,1,0:T(8,128)(2,1)}) %all-gather.51.cloned.1.call-update) | async-done | bytes 4718608 | tf_op jit(solution)/shard_map/all_gather | solution.py:59
  263.2 11.6 multiply_convert_fusion.3
  274.8 69.1 %all-gather.53.cloned.1.call-done = bf16[1,3072,768]{2,1,0:T(8,128)(2,1)} async-done(((bf16[1,384,768]{2,1,0:T(8,128)(2,1)}), bf16[1,3072,768]{2,1,0:T(8,128)(2,1)}) %all-gather.53.cloned.1.call-update) | async-done | bytes 4718608 | tf_op jit(solution)/shard_map/all_gather | solution.py:61
  348.6 36.7 %all-gather.55.cloned.1.call-done = bf16[1,768,768]{2,1,0:T(8,128)(2,1)} async-done(((bf16[1,96,768]{2,1,0:T(8,128)(2,1)}), bf16[1,768,768]{2,1,0:T(8,128)(2,1)}) %all-gather.55.cloned.1.call-update) | async-done | bytes 1179664 | tf_op jit(solution)/shard_map/all_gather | solution.py:53
  391.5 35.8 %all-gather.57.cloned.1.call-done = bf16[1,768,768]{2,1,0:T(8,128)(2,1)} async-done(((bf16[1,96,768]{2,1,0:T(8,128)(2,1)}), bf16[1,768,768]{2,1,0:T(8,128)(2,1)}) %all-gather.57.cloned.1.call-update) | async-done | bytes 1179664 | tf_op jit(solution)/shard_map/all_gather | solution.py:50
  433.6 35.8 %all-gather.59.cloned.1.call-done = bf16[1,768,768]{2,1,0:T(8,128)(2,1)} async-done(((bf16[1,96,768]{2,1,0:T(8,128)(2,1)}), bf16[1,768,768]{2,1,0:T(8,128)(2,1)}) %all-gather.59.cloned.1.call-update) | async-done | bytes 1179664 | tf_op jit(solution)/shard_map/all_gather | solution.py:52
  476.7 6.4 all-to-all-done.6
  493.5 26.1 %all-gather.27 = bf16[1,3072]{1,0:T(2,128)(2,1)S(1)} all-gather(bf16[1,384]{1,0:T(2,128)(2,1)S(1)} %get-tuple-element.108), channel_id=29, replica_groups=mesh['seq'=4,'wt'=8] {'wt'}, dimensions={1}, use_global_device_ids=true | all-gather | bytes 6912 | tf_op jit(solution)/shard_map/all_gather | solution.py:60
  523.3 70.1 %all-gather.63.cloned.1.call-done = bf16[1,768,3072]{2,1,0:T(8,128)(2,1)} async-done(((bf16[1,96,3072]{2,1,0:T(8,128)(2,1)}), bf16[1,768,3072]{2,1,0:T(8,128)(2,1)}) %all-gather.63.cloned.1.call-update) | async-done | bytes 4718608 | tf_op jit(solution)/shard_map/all_gather | solution.py:59
  593.3 11.1 fusion.31
  604.5 69.5 %all-gather.65.cloned.1.call-done = bf16[1,3072,768]{2,1,0:T(8,128)(2,1)} async-done(((bf16[1,384,768]{2,1,0:T(8,128)(2,1)}), bf16[1,3072,768]{2,1,0:T(8,128)(2,1)}) %all-gather.65.cloned.1.call-update) | async-done | bytes 4718608 | tf_op jit(solution)/shard_map/all_gather | solution.py:61
  674.0 7.0 convert_reduce_fusion
  693.0 7.4 all-to-all-done.8
  719.6 8.4 all-to-all-done.9
  735.4 11.9 all_to_all.240
  762.5 6.6 all-to-all-done.11
  778.8 7.2 convert_reduce_fusion.1
  796.9 7.4 all-to-all-done.12
  820.5 8.6 all-to-all-done.13
  838.7 11.6 all_to_all.241
  859.1 12.5 all_to_all.242
  883.6 8.6 fusion.34
  921.2 6.6 fusion.98
  966.8 42.1 %all-reduce.52 = (bf16[768]{0:T(1024)(128)(2,1)S(1)}, bf16[768]{0:T(1024)(128)(2,1)S(1)}, bf16[768]{0:T(1024)(128)(2,1)S(1)}, bf16[768]{0:T(1024)(128)(2,1)S(1)}...) all-reduce(f32[768]{0:T(1024)} %reshape.572, ...), channel_id=33, replica_groups=mesh['seq'=4,'wt'=8] {'seq','wt'}, use_global_device_ids=true, to_apply=%region_25.0.clone | all-reduce | flops 18432 | bytes 110592
  1014.2 10.9 all-reduce.54
  1030.8 5.5 all_gather.241
  1038.0 63.4 %reduce-scatter.23.cloned.1.call-done = f32[24,768]{1,0:T(8,128)} async-done(((f32[768,768]{1,0:T(8,128)}), f32[24,768]{1,0:T(8,128)}) %reduce-scatter.23.cloned.1.call-update) | async-done | bytes 73744 | tf_op jit(solution)/shard_map/reduce_scatter | solution.py:322
  1102.3 102.3 %reduce-scatter.25.cloned.1.call-done = f32[24,768]{1,0:T(8,128)} async-done(((f32[768,768]{1,0:T(8,128)}), f32[24,768]{1,0:T(8,128)}) %reduce-scatter.25.cloned.1.call-update) | async-done | bytes 73744 | tf_op jit(solution)/shard_map/reduce_scatter | solution.py:324
  1205.5 5.5 all_gather.231
  1210.9 5.5 all_gather.235
  1216.4 5.5 all_gather.237
  1221.8 5.5 all_gather.240
  1228.1 81.0 %reduce-scatter.13.cloned.1.call-done = f32[24,768]{1,0:T(8,128)} async-done(((f32[768,768]{1,0:T(8,128)}), f32[24,768]{1,0:T(8,128)}) %reduce-scatter.13.cloned.1.call-update) | async-done | bytes 73744 | tf_op jit(solution)/shard_map/reduce_scatter | solution.py:319
  1310.1 102.5 %reduce-scatter.17.cloned.1.call-done = f32[24,768]{1,0:T(8,128)} async-done(((f32[768,768]{1,0:T(8,128)}), f32[24,768]{1,0:T(8,128)}) %reduce-scatter.17.cloned.1.call-update) | async-done | bytes 73744 | tf_op jit(solution)/shard_map/reduce_scatter | solution.py:321
  1413.4 103.1 %reduce-scatter.21.cloned.1.call-done = f32[24,768]{1,0:T(8,128)} async-done(((f32[768,768]{1,0:T(8,128)}), f32[24,768]{1,0:T(8,128)}) %reduce-scatter.21.cloned.1.call-update) | async-done | bytes 73744 | tf_op jit(solution)/shard_map/reduce_scatter | solution.py:322
  1536.3 120.7 %reduce-scatter.31.cloned.1.call-done = f32[24,3072]{1,0:T(8,128)} async-done(((f32[768,3072]{1,0:T(8,128)}), f32[24,3072]{1,0:T(8,128)}) %reduce-scatter.31.cloned.1.call-update) | async-done | bytes 294928 | tf_op jit(solution)/shard_map/reduce_scatter | solution.py:328
  1658.0 140.6 %reduce-scatter.35.cloned.1.call-done = f32[96,768]{1,0:T(8,128)} async-done(((f32[3072,768]{1,0:T(8,128)}), f32[96,768]{1,0:T(8,128)}) %reduce-scatter.35.cloned.1.call-update) | async-done | bytes 294928 | tf_op jit(solution)/shard_map/reduce_scatter | solution.py:330
  1799.5 7.5 all_gather.249
  1807.0 7.6 all_gather.253
  1814.7 124.6 %reduce-scatter.29.cloned.1.call-done = f32[24,3072]{1,0:T(8,128)} async-done(((f32[768,3072]{1,0:T(8,128)}), f32[24,3072]{1,0:T(8,128)}) %reduce-scatter.29.cloned.1.call-update) | async-done | bytes 294928 | tf_op jit(solution)/shard_map/reduce_scatter | solution.py:328
  1940.2 7.2 all_gather.248
  1947.5 133.2 %reduce-scatter.33.cloned.1.call-done = f32[96,768]{1,0:T(8,128)} async-done(((f32[3072,768]{1,0:T(8,128)}), f32[96,768]{1,0:T(8,128)}) %reduce-scatter.33.cloned.1.call-update) | async-done | bytes 294928 | tf_op jit(solution)/shard_map/reduce_scatter | solution.py:330
  2081.6 7.4 all_gather.252
  (667 shorter events, 334.9 us)
Async XLA Ops:
  7.2 72.7 %all-gather.43.cloned.1.call-start = ((), (), s32[]{:S(2)}) async-start(), calls=%async_computation.40 | async-start | bytes 1327104 | tf_op jit(solution)/shard_map/all_gather | solution.py:53
  9.1 88.2 %all-gather.45.cloned.1.call-start = ((), (), s32[]{:S(2)}) async-start(), calls=%async_computation.41 | async-start | bytes 1327104 | tf_op jit(solution)/shard_map/all_gather | solution.py:50
  10.9 128.4 %all-gather.47.cloned.1.call-start = ((), (), s32[]{:S(2)}) async-start(), calls=%async_computation.42 | async-start | bytes 1327104 | tf_op jit(solution)/shard_map/all_gather | solution.py:52
  12.7 178.6 %all-gather.49.cloned.1.call-start = ((), (), s32[]{:S(2)}) async-start(), calls=%async_computation.43 | async-start | bytes 1327104 | tf_op jit(solution)/shard_map/all_gather | solution.py:55
  14.6 248.6 %all-gather.51.cloned.1.call-start = ((), (), s32[]{:S(2)}) async-start(), calls=%async_computation.44 | async-start | bytes 5308416 | tf_op jit(solution)/shard_map/all_gather | solution.py:59
  15.8 328.1 %all-gather.53.cloned.1.call-start = ((), (), s32[]{:S(2)}) async-start(), calls=%async_computation.45 | async-start | bytes 5308416 | tf_op jit(solution)/shard_map/all_gather | solution.py:61
  17.0 368.3 %all-gather.55.cloned.1.call-start = ((), (), s32[]{:S(2)}) async-start(), calls=%async_computation.46 | async-start | bytes 1327104 | tf_op jit(solution)/shard_map/all_gather | solution.py:53
  17.7 409.6 %all-gather.57.cloned.1.call-start = ((), (), s32[]{:S(2)}) async-start(), calls=%async_computation.47 | async-start | bytes 1327104 | tf_op jit(solution)/shard_map/all_gather | solution.py:50
  18.5 450.9 %all-gather.59.cloned.1.call-start = ((), (), s32[]{:S(2)}) async-start(), calls=%async_computation.48 | async-start | bytes 1327104 | tf_op jit(solution)/shard_map/all_gather | solution.py:52
  19.2 501.9 %all-gather.61.cloned.1.call-start = ((), (), s32[]{:S(2)}) async-start(), calls=%async_computation.49 | async-start | bytes 1327104 | tf_op jit(solution)/shard_map/all_gather | solution.py:55
  19.8 573.5 %all-gather.63.cloned.1.call-start = ((), (), s32[]{:S(2)}) async-start(), calls=%async_computation.50 | async-start | bytes 5308416 | tf_op jit(solution)/shard_map/all_gather | solution.py:59
  82.8 17.3 all-to-all-start
  100.1 42.0 %all-to-all-start.1 = ((bf16[2,128,4,192]{1,0,3,2:T(2,128)(2,1)}), bf16[2,128,4,192]{1,0,3,2:T(2,128)(2,1)S(1)}, u32[]{:S(2)}, u32[]{:S(2)}) async-start(bf16[2,128,4,192]{1,0,3,2:T(2,128)(2,1)} %reshape.536), calls=%async_computation.1 | async-start | bytes 786432 | tf_op jit(solution)/shard_map/all_to_all | solution.py:126
  142.1 11.2 all-to-all-start.2
  160.0 30.7 %all-to-all-start.3 = ((bf16[2,512,1,192]{3,0,2,1:T(2,128)(2,1)}), bf16[2,512,1,192]{3,0,2,1:T(2,128)(2,1)S(1)}, u32[]{:S(2)}, u32[]{:S(2)}) async-start(bf16[2,512,1,192]{3,0,2,1:T(2,128)(2,1)} %copy.193), calls=%async_computation.3 | async-start | bytes 1048576 | tf_op jit(solution)/shard_map/all_to_all | solution.py:146
  163.4 510.6 %all-gather.65.cloned.1.call-start = ((), (), s32[]{:S(2)}) async-start(), calls=%async_computation.51 | async-start | bytes 5308416 | tf_op jit(solution)/shard_map/all_gather | solution.py:61
  190.6 84.2 %copy-start.68 = (f32[768]{0:T(1024)}, f32[768]{0:T(1024)S(1)}, u32[]{:S(2)}) copy-start(f32[768]{0:T(1024)S(1)} %convert_element_type.481) | copy-start | bytes 9220
  190.7 597.6 %copy-start.64 = (f32[768]{0:T(1024)}, f32[768]{0:T(1024)S(1)}, u32[]{:S(2)}) copy-start(f32[768]{0:T(1024)S(1)} %convert_element_type.480) | copy-start | bytes 9220
  191.3 83.5 %copy-start.51 = (bf16[2,128,4,1,192]{1,0,4,2,3:T(2,128)(2,1)}, bf16[2,128,4,1,192]{1,0,4,2,3:T(2,128)(2,1)S(1)}, u32[]{:S(2)}) copy-start(bf16[2,128,4,1,192]{1,0,4,2,3:T(2,128)(2,1)S(1)} %copy.194) | copy-start | bytes 1179652
  193.4 150.5 %copy-start.15 = (f32[256,768]{1,0:T(8,128)}, f32[256,768]{1,0:T(8,128)S(1)}, u32[]{:S(2)}) copy-start(f32[256,768]{1,0:T(8,128)S(1)} %get-tuple-element.131) | copy-start | bytes 2359300
  193.4 594.9 %copy-start.76 = (f32[256]{0:T(256)}, f32[256]{0:T(256)S(1)}, u32[]{:S(2)}) copy-start(f32[256]{0:T(256)S(1)} %broadcast_multiply_fusion.2) | copy-start | bytes 3076
  193.7 594.6 %copy-start.84 = (f32[256]{0:T(256)}, f32[256]{0:T(256)S(1)}, u32[]{:S(2)}) copy-start(f32[256]{0:T(256)S(1)} %fusion.143) | copy-start | bytes 3076
  388.0 42.0 %all-to-all-start.4 = ((bf16[2,128,4,192]{1,0,3,2:T(2,128)(2,1)}), bf16[2,128,4,192]{1,0,3,2:T(2,128)(2,1)S(1)}, u32[]{:S(2)}, u32[]{:S(2)}) async-start(bf16[2,128,4,192]{1,0,3,2:T(2,128)(2,1)} %reshape.542), calls=%async_computation.4 | async-start | bytes 786432 | tf_op jit(solution)/shard_map/all_to_all | solution.py:130
  430.1 42.0 %all-to-all-start.5 = ((bf16[2,128,4,192]{1,0,3,2:T(2,128)(2,1)}), bf16[2,128,4,192]{1,0,3,2:T(2,128)(2,1)S(1)}, u32[]{:S(2)}, u32[]{:S(2)}) async-start(bf16[2,128,4,192]{1,0,3,2:T(2,128)(2,1)} %reshape.544), calls=%async_computation.5 | async-start | bytes 786432 | tf_op jit(solution)/shard_map/all_to_all | solution.py:126
  472.1 11.0 all-to-all-start.6
  489.9 29.7 %all-to-all-start.7 = ((bf16[2,512,1,192]{3,0,2,1:T(2,128)(2,1)}), bf16[2,512,1,192]{3,0,2,1:T(2,128)(2,1)S(1)}, u32[]{:S(2)}, u32[]{:S(2)}) async-start(bf16[2,512,1,192]{3,0,2,1:T(2,128)(2,1)} %copy.202), calls=%async_computation.7 | async-start | bytes 1048576 | tf_op jit(solution)/shard_map/all_to_all | solution.py:146
  493.4 536.5 %reduce-scatter.27.cloned.1.call-start = ((), (), s32[]{:S(2)}) async-start(), calls=%async_computation.35 | async-start | bytes 2433024 | tf_op jit(solution)/shard_map/reduce_scatter | solution.py:324
  519.6 73.8 %copy-start.70 = (f32[768]{0:T(1024)}, f32[768]{0:T(1024)S(1)}, u32[]{:S(2)}) copy-start(f32[768]{0:T(1024)S(1)} %convert_element_type.489) | copy-start | bytes 9220
  519.6 163.6 %copy-start.66 = (f32[768]{0:T(1024)}, f32[768]{0:T(1024)S(1)}, u32[]{:S(2)}) copy-start(f32[768]{0:T(1024)S(1)} %convert_element_type.488) | copy-start | bytes 9220
  523.0 160.2 %copy-start.4 = (f32[256,768]{1,0:T(8,128)}, f32[256,768]{1,0:T(8,128)S(1)}, u32[]{:S(2)}) copy-start(f32[256,768]{1,0:T(8,128)S(1)} %get-tuple-element.138) | copy-start | bytes 2359300
  523.0 160.2 %copy-start.78 = (f32[256]{0:T(256)}, f32[256]{0:T(256)S(1)}, u32[]{:S(2)}) copy-start(f32[256]{0:T(256)S(1)} %broadcast_multiply_fusion) | copy-start | bytes 3076
  523.2 160.0 %copy-start.86 = (f32[256]{0:T(256)}, f32[256]{0:T(256)S(1)}, u32[]{:S(2)}) copy-start(f32[256]{0:T(256)S(1)} %fusion.145) | copy-start | bytes 3076
  689.3 11.1 all-to-all-start.8
  715.7 12.3 all-to-all-start.9
  719.2 317.0 %reduce-scatter.15.cloned.1.call-start = ((), (), s32[]{:S(2)}) async-start(), calls=%async_computation.29 | async-start | bytes 2433024 | tf_op jit(solution)/shard_map/reduce_scatter | solution.py:319
  731.6 305.5 %reduce-scatter.19.cloned.1.call-start = ((), (), s32[]{:S(2)}) async-start(), calls=%async_computation.31 | async-start | bytes 2433024 | tf_op jit(solution)/shard_map/reduce_scatter | solution.py:321
  756.8 12.3 all-to-all-start.11
  760.3 341.1 %reduce-scatter.23.cloned.1.call-start = ((), (), s32[]{:S(2)}) async-start(), calls=%async_computation.33 | async-start | bytes 2433024 | tf_op jit(solution)/shard_map/reduce_scatter | solution.py:322
  777.2 427.3 %reduce-scatter.25.cloned.1.call-start = ((), (), s32[]{:S(2)}) async-start(), calls=%async_computation.34 | async-start | bytes 2433024 | tf_op jit(solution)/shard_map/reduce_scatter | solution.py:324
  793.2 11.0 all-to-all-start.12
  816.8 12.3 all-to-all-start.13
  820.2 488.9 %reduce-scatter.13.cloned.1.call-start = ((), (), s32[]{:S(2)}) async-start(), calls=%async_computation.28 | async-start | bytes 2433024 | tf_op jit(solution)/shard_map/reduce_scatter | solution.py:319
  833.4 579.2 %reduce-scatter.17.cloned.1.call-start = ((), (), s32[]{:S(2)}) async-start(), calls=%async_computation.30 | async-start | bytes 2433024 | tf_op jit(solution)/shard_map/reduce_scatter | solution.py:321
  854.6 661.9 %reduce-scatter.21.cloned.1.call-start = ((), (), s32[]{:S(2)}) async-start(), calls=%async_computation.32 | async-start | bytes 2433024 | tf_op jit(solution)/shard_map/reduce_scatter | solution.py:322
  876.3 780.7 %reduce-scatter.31.cloned.1.call-start = ((), (), s32[]{:S(2)}) async-start(), calls=%async_computation.37 | async-start | bytes 9732096 | tf_op jit(solution)/shard_map/reduce_scatter | solution.py:328
  883.6 915.0 %reduce-scatter.35.cloned.1.call-start = ((), (), s32[]{:S(2)}) async-start(), calls=%async_computation.39 | async-start | bytes 9732096 | tf_op jit(solution)/shard_map/reduce_scatter | solution.py:330
  900.0 1039.2 %reduce-scatter.29.cloned.1.call-start = ((), (), s32[]{:S(2)}) async-start(), calls=%async_computation.36 | async-start | bytes 9732096 | tf_op jit(solution)/shard_map/reduce_scatter | solution.py:328
  907.4 1173.2 %reduce-scatter.33.cloned.1.call-start = ((), (), s32[]{:S(2)}) async-start(), calls=%async_computation.38 | async-start | bytes 9732096 | tf_op jit(solution)/shard_map/reduce_scatter | solution.py:330
  (102 other events, 833.7 us)
Sparse Core Ops, SparseCore 0:
  10.8 43.8 all-gather.42
  57.4 39.8 all-gather.44
  99.5 39.8 all-gather.46
  142.0 39.8 all-gather.48
  184.5 78.6 all-gather.50
  265.8 78.0 all-gather.52
  346.0 39.1 all-gather.54
  387.5 39.8 all-gather.56
  429.5 39.8 all-gather.58
  472.0 39.8 all-gather.60
  514.7 78.6 all-gather.62
  595.9 78.0 all-gather.64
  686.6 98.0 reduce-scatter.26
  791.3 102.6 reduce-scatter.14
  899.1 98.1 reduce-scatter.18
  1003.2 98.1 reduce-scatter.22
  1106.5 97.9 reduce-scatter.24
  1211.1 97.9 reduce-scatter.12
  1314.5 98.0 reduce-scatter.16
  1418.5 97.9 reduce-scatter.20
  1522.4 134.5 reduce-scatter.30
  1663.9 134.6 reduce-scatter.34
  1804.5 134.7 reduce-scatter.28
  1946.0 134.5 reduce-scatter.32
where the time goes:
time: 2110 us; the launch traced here: 2100 us
  waiting for transfers between devices  1460 us (69%)
  blocking collectives  254 us (12%)
  local copies, waits for them, and re-layouts  153 us (7%)
  matrix products  117 us (6%)
  other arithmetic  48.1 us (2%)
  starting transfers between devices  47.9 us (2%)
    reduce_scatter x2, waiting for transfers between devices, settle_layer(): lax.psum_scatter(g[13], ('seq', 'wt'), scatter_dimension=0, tiled=True)  274 us
    reduce_scatter x2, waiting for transfers between devices, settle_layer(): lax.psum_scatter(g[11], ('seq', 'wt'), scatter_dimension=0, tiled=True)  245 us
    reduce_scatter x2, waiting for transfers between devices, settle_layer(): lax.psum_scatter(g[5], ('seq', 'wt'), scatter_dimension=0, tiled=True)  166 us
    all_gather x2, waiting for transfers between devices, fetch_layer(): lax.all_gather(pieces[11], 'wt', axis=0, tiled=True)  140 us
    all_gather x2, waiting for transfers between devices, fetch_layer(): lax.all_gather(pieces[13], 'wt', axis=0, tiled=True)  139 us
    reduce_scatter x2, waiting for transfers between devices, settle_layer(): lax.psum_scatter(g[4], ('seq', 'wt'), scatter_dimension=0, tiled=True)  102 us
    reduce_scatter x2, waiting for transfers between devices, settle_layer(): lax.psum_scatter(g[7], ('seq', 'wt'), scatter_dimension=0, tiled=True)  102 us
    unnamed x3, blocking collectives  92 us
  transfers between devices with their start and end apart: 37, of which 25 were waited for; matrix products, arithmetic and copies ran while one was open for 14% of the time, Pallas kernels for 0%

commit v1 on v0

v1 whole, which is shorter than its diff:
```python
import math

import jax
import jax.numpy as jnp
from jax import lax
from jax.experimental import pallas as pl
from jax.experimental.pallas import tpu as pltpu
from jax.sharding import PartitionSpec as P

HEAD_DIM = 64
LAYERS = 2
epsilon = 1e-05
BF = jnp.bfloat16
F32 = jnp.float32
VMEM_BYTES = 48 * 1024 * 1024

VECTORS = (
    "first_scale",
    "first_shift",
    "query_bias",
    "value_bias",
    "output_bias",
    "second_scale",
    "second_shift",
    "up_bias",
    "down_bias",
)


def matmul(left, right):
    return jnp.dot(left, right, preferred_element_type=F32)


def left_product(left, right):
    return lax.dot_general(left, right, (((0,), (0,)), ((), ())), preferred_element_type=F32)


def right_product(left, right):
    return lax.dot_general(left, right, (((1,), (1,)), ((), ())), preferred_element_type=F32)


def column_sums(values):
    return jnp.sum(values, axis=0, dtype=F32)


def swap_core(values):
    pairs = [(i, i ^ 1) for i in range(lax.axis_size("seq"))]
    return lax.ppermute(values, "seq", pairs)


def swap_row(values):
    pairs = [(i, i ^ 2) for i in range(lax.axis_size("seq"))]
    return lax.ppermute(values, "seq", pairs)


def by_core(core, mine, theirs, axis):
    return jnp.where(
        core == 0,
        jnp.concatenate([mine, theirs], axis),
        jnp.concatenate([theirs, mine], axis),
    )


def gather_owners(shard):
    return lax.all_gather(shard, "wt", axis=0, tiled=True)


def sum_to_owner(values):
    mine = lax.psum_scatter(values.astype(BF), "wt", scatter_dimension=0, tiled=True)
    return mine.astype(F32) + swap_row(mine).astype(F32)


def attend_kernel(q_ref, k_ref, v_ref, o_ref):
    factor = 1.0 / math.sqrt(HEAD_DIM)
    for head in range(q_ref.shape[1] // HEAD_DIM):
        part = slice(head * HEAD_DIM, (head + 1) * HEAD_DIM)
        scores = right_product(q_ref[:, part], k_ref[:, part]) * factor
        raised = jnp.exp(scores - jnp.max(scores, axis=1, keepdims=True))
        chances = raised * (1.0 / jnp.sum(raised, axis=1, keepdims=True))
        o_ref[:, part] = matmul(chances.astype(BF), v_ref[:, part]).astype(BF)


def attend(qkv):
    rows, width = qkv.shape
    width //= 3
    block = 2 * HEAD_DIM
    steps = width // block
    return pl.pallas_call(
        attend_kernel,
        grid=(steps,),
        in_specs=[
            pl.BlockSpec((rows, block), lambda i: (0, i)),
            pl.BlockSpec((rows, block), lambda i: (0, steps + i)),
            pl.BlockSpec((rows, block), lambda i: (0, 2 * steps + i)),
        ],
        out_specs=pl.BlockSpec((rows, block), lambda i: (0, i)),
        out_shape=jax.ShapeDtypeStruct((rows, width), BF),
        compiler_params=pltpu.CompilerParams(vmem_limit_bytes=VMEM_BYTES),
        cost_estimate=pl.CostEstimate(
            flops=4 * rows * rows * width,
            bytes_accessed=8 * rows * width,
            transcendentals=rows * rows * width // HEAD_DIM,
        ),
        name="attend",
    )(qkv, qkv, qkv)


def attend_back_kernel(q_ref, k_ref, v_ref, eo_ref, eq_ref, ek_ref, ev_ref):
    factor = 1.0 / math.sqrt(HEAD_DIM)
    for head in range(q_ref.shape[1] // HEAD_DIM):
        part = slice(head * HEAD_DIM, (head + 1) * HEAD_DIM)
        queries, keys, eo = q_ref[:, part], k_ref[:, part], eo_ref[:, part]
        scores = right_product(keys, queries) * factor
        raised = jnp.exp(scores - jnp.max(scores, axis=0, keepdims=True))
        chances = raised * (1.0 / jnp.sum(raised, axis=0, keepdims=True))
        ep = right_product(v_ref[:, part], eo)
        ev_ref[:, part] = matmul(chances.astype(BF), eo).astype(BF)
        inner = jnp.sum(ep * chances, axis=0, keepdims=True)
        es = (chances * (ep - inner)).astype(BF)
        ek_ref[:, part] = (matmul(es, queries) * factor).astype(BF)
        eq_ref[:, part] = (left_product(keys, es) * factor).T.astype(BF)


def attend_back(qkv, eo):
    rows, width = eo.shape
    block = 2 * HEAD_DIM
    steps = width // block
    return pl.pallas_call(
        attend_back_kernel,
        grid=(steps,),
        in_specs=[
            pl.BlockSpec((rows, block), lambda i: (0, i)),
            pl.BlockSpec((rows, block), lambda i: (0, steps + i)),
            pl.BlockSpec((rows, block), lambda i: (0, 2 * steps + i)),
            pl.BlockSpec((rows, block), lambda i: (0, i)),
        ],
        out_specs=[pl.BlockSpec((rows, block), lambda i: (0, i))] * 3,
        out_shape=[jax.ShapeDtypeStruct((rows, width), BF)] * 3,
        compiler_params=pltpu.CompilerParams(vmem_limit_bytes=VMEM_BYTES),
        cost_estimate=pl.CostEstimate(
            flops=10 * rows * rows * width,
            bytes_accessed=14 * rows * width,
            transcendentals=rows * rows * width // HEAD_DIM,
        ),
        name="attend_back",
    )(qkv, qkv, qkv, eo)


def norm_parts(values):
    centred = values - jnp.mean(values, axis=-1, keepdims=True)
    spread = jnp.mean(centred * centred, axis=-1, keepdims=True)
    rate = lax.rsqrt(spread + epsilon)
    return centred * rate, rate


def norm_back(values, scale, grad):
    flat, rate = norm_parts(values)
    inner = grad * scale
    mean_inner = jnp.mean(inner, axis=-1, keepdims=True)
    mean_cross = jnp.mean(inner * flat, axis=-1, keepdims=True)
    before = rate * (inner - mean_inner - flat * mean_cross)
    return before, column_sums(grad * flat), column_sums(grad)


def gelu_parts(values):
    below = 0.5 * (1.0 + lax.erf(values * math.sqrt(0.5)))
    density = jnp.exp(-0.5 * values * values) * (1.0 / math.sqrt(2.0 * math.pi))
    return values * below, below + values * density


def per_device(
    activations,
    upstream,
    first_scale,
    first_shift,
    query_weight,
    query_bias,
    key_weight,
    value_weight,
    value_bias,
    output_weight,
    output_bias,
    second_scale,
    second_shift,
    up_weight,
    up_bias,
    down_weight,
    down_bias,
):
    owners = lax.axis_size("wt")
    place = lax.axis_index("seq")
    core, side = place % 2, place // 2
    frames_here, features = activations.shape[1:]
    half = features // 2
    shard = features // owners
    units = up_weight.shape[2]
    unit_shard = units // owners
    unit_half = unit_shard // 2

    def to_chip(values):
        kept = lax.dynamic_index_in_dim(values, side, 0, keepdims=False)
        sent = lax.dynamic_index_in_dim(values, 1 - side, 0, keepdims=False)
        mine = jnp.concatenate([kept, swap_row(sent)], 0)
        return by_core(core, mine, swap_core(mine), 0)

    def from_chip(mine):
        kept, sent = mine[:frames_here], mine[frames_here:]
        other = swap_row(sent)
        return jnp.where(side == 0, jnp.stack([kept, other]), jnp.stack([other, kept]))

    def own_rows(values):
        return lax.dynamic_slice_in_dim(values, core * 2 * frames_here, 2 * frames_here, 0)

    def half_columns(values):
        return lax.dynamic_slice_in_dim(values, core * half, half, 1)

    members = dict(
        first_scale=first_scale,
        first_shift=first_shift,
        query_bias=query_bias,
        value_bias=value_bias,
        output_bias=output_bias,
        second_scale=second_scale,
        second_shift=second_shift,
        up_bias=up_bias,
        down_bias=down_bias,
    )
    packed = jnp.concatenate([members[name] for name in VECTORS], 1)
    spread = lax.all_gather(packed, "wt", axis=0, tiled=False)
    vectors = []
    for layer in range(LAYERS):
        found, start = {}, 0
        for name in VECTORS:
            size = members[name].shape[1]
            found[name] = spread[:, layer, start : start + size].reshape(-1).astype(F32)
            start += size
        vectors.append(found)

    def unit_part(bias):
        return lax.dynamic_index_in_dim(
            bias.reshape(owners, 2, unit_half), core, 1, keepdims=False
        ).reshape(-1)

    weights = []
    for layer in range(LAYERS):
        branch = gather_owners(
            jnp.concatenate(
                [
                    half_columns(query_weight[layer]),
                    half_columns(key_weight[layer]),
                    half_columns(value_weight[layer]),
                    half_columns(output_weight[layer]),
                ],
                1,
            )
        )
        up = gather_owners(
            lax.dynamic_index_in_dim(
                up_weight[layer].reshape(shard, owners, 2, unit_half), core, 2, keepdims=False
            ).reshape(shard, units // 2)
        )
        down = gather_owners(
            lax.dynamic_slice_in_dim(down_weight[layer], core * unit_half, unit_half, 0)
        )
        out_half = branch[:, 3 * half :]
        out = by_core(core, out_half, swap_core(out_half), 1)
        weights.append((branch[:, : 3 * half], out, up, down))

    hidden = to_chip(activations).astype(F32)
    kept = []
    for layer in range(LAYERS):
        vec = vectors[layer]
        in_weight, out_weight, up, down = weights[layer]
        flat, _ = norm_parts(hidden)
        normed = (flat * vec["first_scale"] + vec["first_shift"]).astype(BF)
        in_bias = jnp.concatenate(
            [
                lax.dynamic_slice_in_dim(vec["query_bias"], core * half, half, 0),
                jnp.zeros((half,), F32),
                lax.dynamic_slice_in_dim(vec["value_bias"], core * half, half, 0),
            ]
        )
        qkv = (matmul(normed, in_weight) + in_bias).astype(BF)
        mixture_half = attend(qkv)
        mixture = by_core(core, mixture_half, swap_core(mixture_half), 1)
        middle = hidden + matmul(mixture, out_weight) + vec["output_bias"]
        flat, _ = norm_parts(middle)
        second = (flat * vec["second_scale"] + vec["second_shift"]).astype(BF)
        upward = matmul(second, up) + unit_part(vec["up_bias"])
        activated, slope = gelu_parts(upward)
        activated = activated.astype(BF)
        slope = slope.astype(BF)
        kept.append((hidden, normed, qkv, mixture, middle, second, activated, slope))
        partial = matmul(activated, down)
        if layer + 1 < LAYERS:
            hidden = middle + vec["down_bias"] + (partial + swap_core(partial.astype(BF)))
        else:
            theirs = lax.dynamic_slice_in_dim(
                partial, (1 - core) * 2 * frames_here, 2 * frames_here, 0
            )
            total = own_rows(partial) + swap_core(theirs.astype(BF))
            result = from_chip((own_rows(middle) + vec["down_bias"] + total).astype(BF))

    grad_hidden = to_chip(upstream).astype(F32)
    settled = [None] * LAYERS
    for layer in reversed(range(LAYERS)):
        vec = vectors[layer]
        in_weight, out_weight, up, down = weights[layer]
        hidden, normed, qkv, mixture, middle, second, activated, slope = kept[layer]
        grads = {}
        down_in = grad_hidden.astype(BF)
        grad_down = sum_to_owner(left_product(activated, down_in))
        grads["down_bias"] = column_sums(down_in)
        grad_upward = (slope.astype(F32) * right_product(down_in, down)).astype(BF)
        grad_up = sum_to_owner(left_product(second, grad_upward))
        grad_up_bias = column_sums(grad_upward)
        partial = right_product(grad_upward, up)
        grad_second = partial + swap_core(partial.astype(BF))
        before, grads["second_scale"], grads["second_shift"] = norm_back(
            middle, vec["second_scale"], grad_second
        )
        grad_middle = grad_hidden + before
        branch_in = grad_middle.astype(BF)
        grads["output_bias"] = column_sums(branch_in)
        grad_out = left_product(mixture, half_columns(branch_in))
        out_rows = lax.dynamic_slice_in_dim(out_weight, core * half, half, 0)
        grad_mixture = right_product(branch_in, out_rows).astype(BF)
        grad_qkv = jnp.concatenate(attend_back(qkv, grad_mixture), 1)
        grad_in = left_product(normed, grad_qkv)
        grad_branch = sum_to_owner(jnp.concatenate([grad_in, grad_out], 1))
        grad_in_bias = column_sums(grad_qkv)
        partial = right_product(grad_qkv, in_weight)
        if layer > 0:
            grad_normed = partial + swap_core(partial.astype(BF))
            before, grads["first_scale"], grads["first_shift"] = norm_back(
                hidden, vec["first_scale"], grad_normed
            )
            grad_hidden = grad_middle + before
        else:
            theirs = lax.dynamic_slice_in_dim(
                partial, (1 - core) * 2 * frames_here, 2 * frames_here, 0
            )
            grad_normed = own_rows(partial) + swap_core(theirs.astype(BF))
            before, grads["first_scale"], grads["first_shift"] = norm_back(
                own_rows(hidden), vec["first_scale"], grad_normed
            )
            input_grad = from_chip(own_rows(grad_middle) + before)

        first = (core == 0).astype(F32)
        for name in ("down_bias", "second_scale", "second_shift", "output_bias"):
            grads[name] = grads[name] * first
        if layer > 0:
            grads["first_scale"] = grads["first_scale"] * first
            grads["first_shift"] = grads["first_shift"] * first
        blank = jnp.zeros((half,), F32)
        grads["query_bias"] = by_core(core, grad_in_bias[:half], blank, 0)
        grads["value_bias"] = by_core(core, grad_in_bias[2 * half :], blank, 0)
        unit_rows = grad_up_bias.reshape(owners, 1, unit_half)
        grads["up_bias"] = by_core(core, unit_rows, jnp.zeros_like(unit_rows), 1).reshape(-1)
        packed = jnp.concatenate([grads[name].reshape(owners, -1) for name in VECTORS], 1)
        packed = lax.psum_scatter(packed, "wt", scatter_dimension=0, tiled=False)
        packed = packed + swap_row(packed)
        packed = packed + swap_core(packed)
        done, start = {}, 0
        for name in VECTORS:
            size = members[name].shape[1]
            done[name] = packed[start : start + size]
            start += size

        def both(mine):
            mine = mine.astype(BF)
            other = swap_core(mine).astype(F32)
            mine = mine.astype(F32)
            return jnp.where(core == 0, mine, other), jnp.where(core == 0, other, mine)

        low, high = both(grad_branch)
        for position, name in enumerate(
            ("query_weight", "key_weight", "value_weight", "output_weight")
        ):
            part = slice(position * half, (position + 1) * half)
            done[name] = jnp.concatenate([low[:, part], high[:, part]], 1)
        low, high = both(grad_up)
        done["up_weight"] = jnp.stack(
            [low.reshape(shard, owners, unit_half), high.reshape(shard, owners, unit_half)], 2
        ).reshape(shard, units)
        low, high = both(grad_down)
        done["down_weight"] = jnp.concatenate([low, high], 0)
        settled[layer] = done

    names = (
        "first_scale",
        "first_shift",
        "query_weight",
        "query_bias",
        "key_weight",
        "value_weight",
        "value_bias",
        "output_weight",
        "output_bias",
        "second_scale",
        "second_shift",
        "up_weight",
        "up_bias",
        "down_weight",
        "down_bias",
    )
    final = tuple(
        jnp.stack([settled[layer][name] for layer in range(LAYERS)]) for name in names
    )
    return (result, input_grad) + final


def solution(mesh):
    rows, vector, matrix = P("wt", "seq", None), P(None, "wt"), P(None, "wt", None)
    parameters = (
        vector,
        vector,
        matrix,
        vector,
        matrix,
        matrix,
        vector,
        matrix,
        vector,
        vector,
        vector,
        matrix,
        vector,
        matrix,
        vector,
    )
    specs = (rows, rows) + parameters
    return jax.shard_map(
        per_device, mesh=mesh, in_specs=specs, out_specs=specs, check_vma=False
    )
```

time: 2110 us -> 948 us (0.45)
  waiting for transfers between devices: 1460 us -> 631 us
  blocking collectives: 254 us -> 31.7 us
  local copies, waits for them, and re-layouts: 153 us -> 69.9 us
  matrix products: 117 us -> 72.1 us
  Pallas kernels: 0 us -> 28.2 us
  starting transfers between devices: 47.9 us -> 22.4 us
    reduce_scatter x12 -> x6, waiting for transfers between devices: 971 us -> 378 us  [sum_to_owner(): lax.psum_scatter(values.astype(BF), 'wt', scatter_dimension=0, tiled=True)]
    all_gather x12 -> x6, waiting for transfers between devices: 433 us -> 196 us  [gather_owners(): return lax.all_gather(shard, 'wt', axis=0, tiled=True)]
    all_gather x14 -> x1, blocking collectives: 126 us -> 31.7 us  [per_device(): spread = lax.all_gather(packed, 'wt', axis=0, tiled=False)]
    unnamed x3 -> x0, blocking collectives: 92 us -> none
    all_to_all x13 -> x0, waiting for transfers between devices: 51.1 us -> none  [the longest x2 16.9 us: backward_layer(): lax.all_to_all(grad_queries.reshape(back_shape), 'seq', split_axis=1, con...]
    dot_general x24 -> x8, matrix products: 80.2 us -> 29.8 us  [matmul(): return jnp.dot(left, right, preferred_element_type=F32)]
    all_to_all x13 -> x0, starting transfers between devices: 45.9 us -> none  [the longest x2 7.39 us: forward_layer(): lax.all_to_all(keyset.reshape(split_shape), 'seq', split_axis=2, concat_a...]
    transpose x30 -> x0, local copies, waits for them, and re-layouts: 38.7 us -> none  [owner_order(): return jnp.swapaxes(shaped, 0, 1).reshape((rows,) + rest)]
  transfers between devices with their start and end apart: 37 -> 45, of which waited for: 25 -> 26; matrix products, arithmetic and copies ran while one was open for 14% -> 16% of each run, Pallas kernels for 0% -> 1%
where the time goes in v1:
time: 948 us; the launch traced here: 940 us
  waiting for transfers between devices  631 us (67%)
  matrix products  72.1 us (8%)
  local copies, waits for them, and re-layouts  69.9 us (7%)
  other arithmetic  68.7 us (7%)
  blocking collectives  31.7 us (3%)
  Pallas kernels  28.2 us (3%)
  starting transfers between devices  22.4 us (2%)
  between operations  16.2 us (2%)
    reduce_scatter x6, waiting for transfers between devices, sum_to_owner(): lax.psum_scatter(values.astype(BF), 'wt', scatter_dimension=0, tiled=True)  378 us
    all_gather x6, waiting for transfers between devices, gather_owners(): return lax.all_gather(shard, 'wt', axis=0, tiled=True)  196 us
    all_gather x1, blocking collectives, per_device(): spread = lax.all_gather(packed, 'wt', axis=0, tiled=False)  31.7 us
    ppermute x12, waiting for transfers between devices, swap_row(): return lax.ppermute(values, 'seq', pairs)  31.2 us
    dot_general x8, matrix products, matmul(): return jnp.dot(left, right, preferred_element_type=F32)  29.8 us
    dot_general x8, matrix products, left_product(): lax.dot_general(left, right, (((0,), (0,)), ((), ())), preferred_element_...  22.5 us
    reduce_sum x10, other arithmetic, column_sums(): return jnp.sum(values, axis=0, dtype=F32)  20.2 us
    dot_general x8, matrix products, right_product(): lax.dot_general(left, right, (((1,), (1,)), ((), ())), preferred_element_...  19.7 us
  transfers between devices with their start and end apart: 45, of which 26 were waited for; matrix products, arithmetic and copies ran while one was open for 16% of the time, Pallas kernels for 1%

profile of v1, /device:TPU:0, one launch (start us, length us, event | category | flops | bytes accessed | tf_op | source)
XLA Modules:
  0.0 940.1 jit_solution(18296709503616754715)
XLA Ops:
  20.0 3.0 collective-permute-start
  23.1 4.9 collective-permute-done
  33.0 31.7 %all-gather.3 = bf16[8,2,1152]{2,1,0:T(2,128)(2,1)S(1)} all-gather(bf16[1,2,1152]{2,1,0:T(2,128)(2,1)S(1)} %bitcast.120), channel_id=2, replica_groups=mesh['seq'=4,'wt'=8] {'wt'}, dimensions={0}, use_global_device_ids=true | all-gather | bytes 41472 | tf_op jit(solution)/shard_map/all_gather | solution.py:229
  70.2 3.0 fusion.12.q_ref.k_ref.v_ref
  73.2 5.7 attend.2
  81.4 3.1 fusion.79
  84.8 36.4 %all-gather.13.cloned.1.call-done = bf16[768,1536]{1,0:T(8,128)(2,1)} async-done(((bf16[96,1536]{1,0:T(8,128)(2,1)}), bf16[768,1536]{1,0:T(8,128)(2,1)}) %all-gather.13.cloned.1.call-update) | async-done | bytes 2359312 | tf_op jit(solution)/shard_map/all_gather | solution.py:65
  121.2 5.0 multiply_convert_fusion.1
  126.2 48.4 %all-gather.19.cloned.1.call-done = bf16[1,1536,768]{2,1,0:T(8,128)(2,1)} async-done(((bf16[1,192,768]{2,1,0:T(8,128)(2,1)}), bf16[1,1536,768]{2,1,0:T(8,128)(2,1)}) %all-gather.19.cloned.1.call-update) | async-done | bytes 2359312 | tf_op jit(solution)/shard_map/all_gather | solution.py:65
  174.6 5.0 fusion.80
  186.4 3.3 collective-permute-done.9
  190.5 36.8 %all-gather.15.cloned.1.call-done = bf16[768,1536]{1,0:T(8,128)(2,1)} async-done(((bf16[96,1536]{1,0:T(8,128)(2,1)}), bf16[768,1536]{1,0:T(8,128)(2,1)}) %all-gather.15.cloned.1.call-update) | async-done | bytes 2359312 | tf_op jit(solution)/shard_map/all_gather | solution.py:65
  234.0 6.2 attend.3
  248.9 2.9 fusion.81
  253.3 27.3 %all-gather.17.cloned.1.call-done = bf16[768,1536]{1,0:T(8,128)(2,1)} async-done(((bf16[96,1536]{1,0:T(8,128)(2,1)}), bf16[768,1536]{1,0:T(8,128)(2,1)}) %all-gather.17.cloned.1.call-update) | async-done | bytes 2359312 | tf_op jit(solution)/shard_map/all_gather | solution.py:65
  280.6 6.0 multiply_convert_fusion
  286.6 46.7 %all-gather.21.cloned.1.call-done = bf16[1,1536,768]{2,1,0:T(8,128)(2,1)} async-done(((bf16[1,192,768]{2,1,0:T(8,128)(2,1)}), bf16[1,1536,768]{2,1,0:T(8,128)(2,1)}) %all-gather.21.cloned.1.call-update) | async-done | bytes 2359312 | tf_op jit(solution)/shard_map/all_gather | solution.py:65
  333.3 5.5 convert_reduce_fusion
  338.9 2.9 fusion.82
  344.4 3.0 maximum_select_fusion.1
  352.3 3.0 multiply_reduce_fusion
  355.4 2.9 convert_reduce_fusion.5
  358.9 8.2 attend_back.2
  377.5 3.2 convert_reduce_fusion.1
  380.7 2.9 fusion.84
  393.6 3.2 multiply_reduce_fusion.2
  396.8 3.6 convert_reduce_fusion.7
  401.1 8.2 attend_back.3
  410.2 2.7 fusion.23
  416.0 3.2 multiply_reduce_fusion.13
  420.1 4.4 convolution_convert_fusion.2
  426.1 4.0 convolution_convert_fusion
  436.7 4.4 convolution_convert_fusion.3
  442.5 4.3 convolution_convert_fusion.1
  447.3 3.6 fusion.15
  457.1 4.9 collective-permute-done.8
  468.1 19.4 %all-reduce.15.cloned.1.call-done = (f32[8,1152]{1,0:T(8,128)}, f32[8,1152]{1,0:T(8,128)}) async-done(((f32[8,1152]{1,0:T(8,128)}, f32[8,1152]{1,0:T(8,128)}), (f32[8,1152]{1,0:T(8,128)}, f32[8,1152]{1,0:T(8,128)})) %all-reduce.15.cloned.1.call-update) | async-done | bytes 73744
  501.7 58.0 %reduce-scatter.13.cloned.1.call-done = bf16[96,1536]{1,0:T(8,128)(2,1)} async-done(((bf16[768,1536]{1,0:T(8,128)(2,1)}), bf16[96,1536]{1,0:T(8,128)(2,1)}) %reduce-scatter.13.cloned.1.call-update) | async-done | bytes 294928 | tf_op jit(solution)/shard_map/reduce_scatter | solution.py:69
  563.0 68.4 %reduce-scatter.17.cloned.1.call-done = bf16[192,768]{1,0:T(8,128)(2,1)} async-done(((bf16[1536,768]{1,0:T(8,128)(2,1)}), bf16[192,768]{1,0:T(8,128)(2,1)}) %reduce-scatter.17.cloned.1.call-update) | async-done | bytes 294928 | tf_op jit(solution)/shard_map/reduce_scatter | solution.py:69
  634.9 4.4 collective-permute-done.30
  639.5 63.9 %reduce-scatter.9.cloned.1.call-done = bf16[96,1536]{1,0:T(8,128)(2,1)} async-done(((bf16[768,1536]{1,0:T(8,128)(2,1)}), bf16[96,1536]{1,0:T(8,128)(2,1)}) %reduce-scatter.9.cloned.1.call-update) | async-done | bytes 294928 | tf_op jit(solution)/shard_map/reduce_scatter | solution.py:69
  706.9 2.6 stack_reshape.23
  713.4 61.6 %reduce-scatter.11.cloned.1.call-done = bf16[96,1536]{1,0:T(8,128)(2,1)} async-done(((bf16[768,1536]{1,0:T(8,128)(2,1)}), bf16[96,1536]{1,0:T(8,128)(2,1)}) %reduce-scatter.11.cloned.1.call-update) | async-done | bytes 294928 | tf_op jit(solution)/shard_map/reduce_scatter | solution.py:69
  778.7 68.1 %reduce-scatter.15.cloned.1.call-done = bf16[192,768]{1,0:T(8,128)(2,1)} async-done(((bf16[1536,768]{1,0:T(8,128)(2,1)}), bf16[192,768]{1,0:T(8,128)(2,1)}) %reduce-scatter.15.cloned.1.call-update) | async-done | bytes 294928 | tf_op jit(solution)/shard_map/reduce_scatter | solution.py:69
  849.2 5.6 collective-permute-done.28
  857.5 2.8 stack_reshape.20
  861.5 57.7 %reduce-scatter.7.cloned.1.call-done = bf16[96,1536]{1,0:T(8,128)(2,1)} async-done(((bf16[768,1536]{1,0:T(8,128)(2,1)}), bf16[96,1536]{1,0:T(8,128)(2,1)}) %reduce-scatter.7.cloned.1.call-update) | async-done | bytes 294928 | tf_op jit(solution)/shard_map/reduce_scatter | solution.py:69
  922.2 4.8 collective-permute-done.20
  (587 shorter events, 153.3 us)
Async XLA Ops:
  7.2 61.7 %all-gather.11.cloned.1.call-start = ((), (), s32[]{:S(2)}) async-start(), calls=%async_computation.6 | async-start | bytes 2654208 | tf_op jit(solution)/shard_map/all_gather | solution.py:65
  12.6 108.6 %all-gather.13.cloned.1.call-start = ((), (), s32[]{:S(2)}) async-start(), calls=%async_computation.7 | async-start | bytes 2654208 | tf_op jit(solution)/shard_map/all_gather | solution.py:65
  17.3 157.4 %all-gather.19.cloned.1.call-start = ((), (), s32[]{:S(2)}) async-start(), calls=%async_computation.16 | async-start | bytes 2654208 | tf_op jit(solution)/shard_map/all_gather | solution.py:65
  19.0 208.3 %all-gather.15.cloned.1.call-start = ((), (), s32[]{:S(2)}) async-start(), calls=%async_computation.8 | async-start | bytes 2654208 | tf_op jit(solution)/shard_map/all_gather | solution.py:65
  19.9 260.7 %all-gather.17.cloned.1.call-start = ((), (), s32[]{:S(2)}) async-start(), calls=%async_computation.9 | async-start | bytes 2654208 | tf_op jit(solution)/shard_map/all_gather | solution.py:65
  20.0 7.9 collective-permute-start
  28.0 38.9 %collective-permute-start.1 = (bf16[256,768]{1,0:T(8,128)(2,1)S(1)}, bf16[256,768]{1,0:T(8,128)(2,1)S(1)}, u32[]{:S(2)}, u32[]{:S(2)}) collective-permute-start(bf16[256,768]{1,0:T(8,128)(2,1)S(1)} %pad_maximum_fusion.10), channel_id=1, source_target_pairs={{0,8},{8,0},{16,24},{24,16},{1,9},{9,1},{17,25},{25,17},{2,10},{10... | collective-permute-start | bytes 1179656 | tf_op jit(solution)/shard_map/ppermute | solution.py:48
  32.7 300.6 %all-gather.21.cloned.1.call-start = ((), (), s32[]{:S(2)}) async-start(), calls=%async_computation.17 | async-start | bytes 2654208 | tf_op jit(solution)/shard_map/all_gather | solution.py:65
  70.1 11.3 %collective-permute-start.3 = (bf16[768,384]{1,0:T(8,128)(2,1)S(1)}, bf16[768,384]{1,0:T(8,128)(2,1)}, u32[]{:S(2)}, u32[]{:S(2)}) collective-permute-start(bf16[768,384]{1,0:T(8,128)(2,1)S(1)} %slice.317), channel_id=1, source_target_pairs={{0,8},{8,0},{16,24},{24,16},{1,9},{9,1},{17,25},{25,17},{2,10},{10... | collective-permute-start | bytes 1769480 | tf_op jit(solution)/shard_map/ppermute | solution.py:48
  78.8 1.8 collective-permute-start.2
  84.5 144.8 %copy-start.4 = (f32[512,768]{1,0:T(8,128)}, f32[512,768]{1,0:T(8,128)S(1)}, u32[]{:S(2)}) copy-start(f32[512,768]{1,0:T(8,128)S(1)} %get-tuple-element.151) | copy-start | bytes 4718596
  179.6 49.6 %collective-permute-start.4 = (bf16[512,768]{1,0:T(8,128)(2,1)}, bf16[512,768]{1,0:T(8,128)(2,1)}, u32[]{:S(2)}, u32[]{:S(2)}) collective-permute-start(bf16[512,768]{1,0:T(8,128)(2,1)} %get-tuple-element.154), channel_id=1, source_target_pairs={{0,8},{8,0},{16,24},{24,16},{1,9},{9,1},{17,25},{25,17},{2,10},{10... | collective-permute-start | bytes 2359304 | tf_op jit(solution)/shard_map/ppermute | solution.py:48
  180.4 307.0 %all-reduce.15.cloned.1.call-start = ((), (), s32[]{:S(2)}) async-start(), calls=%async_computation.18 | async-start | bytes 147456
  182.2 49.2 %copy-start.22 = (bf16[128,768]{1,0:T(8,128)(2,1)}, bf16[128,768]{1,0:T(8,128)(2,1)S(1)}, u32[]{:S(2)}) copy-start(bf16[128,768]{1,0:T(8,128)(2,1)S(1)} %get-tuple-element.112) | copy-start | bytes 589828
  182.2 7.5 collective-permute-start.9
  190.5 57.0 %collective-permute-start.10 = (bf16[256,768]{1,0:T(8,128)(2,1)}, bf16[256,768]{1,0:T(8,128)(2,1)}, u32[]{:S(2)}, u32[]{:S(2)}) collective-permute-start(bf16[256,768]{1,0:T(8,128)(2,1)} %pad_maximum_fusion.11), channel_id=1, source_target_pairs={{0,8},{8,0},{16,24},{24,16},{1,9},{9,1},{17,25},{25,17},{2,10},{10... | collective-permute-start | bytes 1179656 | tf_op jit(solution)/shard_map/ppermute | solution.py:48
  229.3 19.6 %collective-permute-start.6 = (bf16[768,384]{1,0:T(8,128)(2,1)}, bf16[768,384]{1,0:T(8,128)(2,1)}, u32[]{:S(2)}, u32[]{:S(2)}) collective-permute-start(bf16[768,384]{1,0:T(8,128)(2,1)} %slice.328), channel_id=1, source_target_pairs={{0,8},{8,0},{16,24},{24,16},{1,9},{9,1},{17,25},{25,17},{2,10},{10... | collective-permute-start | bytes 1769480 | tf_op jit(solution)/shard_map/ppermute | solution.py:48
  240.2 8.7 collective-permute-start.5
  341.7 10.5 %collective-permute-start.11 = (bf16[512,768]{1,0:T(8,128)(2,1)}, bf16[512,768]{1,0:T(8,128)(2,1)}, u32[]{:S(2)}, u32[]{:S(2)}) collective-permute-start(bf16[512,768]{1,0:T(8,128)(2,1)} %get-tuple-element.160), channel_id=1, source_target_pairs={{0,8},{8,0},{16,24},{24,16},{1,9},{9,1},{17,25},{25,17},{2,10},{10... | collective-permute-start | bytes 2359304 | tf_op jit(solution)/shard_map/ppermute | solution.py:48
  370.5 2.5 collective-permute-start.12
  383.7 9.9 %collective-permute-start.13 = (bf16[512,768]{1,0:T(8,128)(2,1)}, bf16[512,768]{1,0:T(8,128)(2,1)}, u32[]{:S(2)}, u32[]{:S(2)}) collective-permute-start(bf16[512,768]{1,0:T(8,128)(2,1)} %get-tuple-element.164), channel_id=1, source_target_pairs={{0,8},{8,0},{16,24},{24,16},{1,9},{9,1},{17,25},{25,17},{2,10},{10... | collective-permute-start | bytes 2359304 | tf_op jit(solution)/shard_map/ppermute | solution.py:48
  414.2 1.8 collective-permute-start.14
  420.0 139.8 %reduce-scatter.13.cloned.1.call-start = ((), (), s32[]{:S(2)}) async-start(), calls=%async_computation.13 | async-start | bytes 2654208 | tf_op jit(solution)/shard_map/reduce_scatter | solution.py:69
  424.5 206.9 %reduce-scatter.17.cloned.1.call-start = ((), (), s32[]{:S(2)}) async-start(), calls=%async_computation.15 | async-start | bytes 2654208 | tf_op jit(solution)/shard_map/reduce_scatter | solution.py:69
  430.2 273.2 %reduce-scatter.9.cloned.1.call-start = ((), (), s32[]{:S(2)}) async-start(), calls=%async_computation.11 | async-start | bytes 2654208 | tf_op jit(solution)/shard_map/reduce_scatter | solution.py:69
  435.3 339.7 %reduce-scatter.11.cloned.1.call-start = ((), (), s32[]{:S(2)}) async-start(), calls=%async_computation.12 | async-start | bytes 2654208 | tf_op jit(solution)/shard_map/reduce_scatter | solution.py:69
  441.2 405.6 %reduce-scatter.15.cloned.1.call-start = ((), (), s32[]{:S(2)}) async-start(), calls=%async_computation.14 | async-start | bytes 2654208 | tf_op jit(solution)/shard_map/reduce_scatter | solution.py:69
  446.9 472.2 %reduce-scatter.7.cloned.1.call-start = ((), (), s32[]{:S(2)}) async-start(), calls=%async_computation.10 | async-start | bytes 2654208 | tf_op jit(solution)/shard_map/reduce_scatter | solution.py:69
  451.7 2.1 collective-permute-start.7
  454.9 7.0 collective-permute-start.8
  488.8 5.0 collective-permute-start.16
  493.3 3.7 collective-permute-start.18
  493.9 3.1 collective-permute-start.17
  494.0 140.0 %collective-permute-start.15 = (f32[128,768]{1,0:T(8,128)S(1)}, f32[128,768]{1,0:T(8,128)S(1)}, u32[]{:S(2)}, u32[]{:S(2)}) collective-permute-start(f32[128,768]{1,0:T(8,128)S(1)} %get-tuple-element.83), channel_id=1, source_target_pairs={{0,16},{8,24},{16,0},{24,8},{1,17},{9,25},{17,1},{25,9},{2,18},{10... | collective-permute-start | bytes 1179656 | tf_op jit(solution)/shard_map/ppermute | solution.py:53
  497.0 1.2 collective-permute-start.19
  559.8 73.1 %collective-permute-start.26 = (bf16[96,1536]{1,0:T(8,128)(2,1)}, bf16[96,1536]{1,0:T(8,128)(2,1)S(1)}, u32[]{:S(2)}, u32[]{:S(2)}) collective-permute-start(bf16[96,1536]{1,0:T(8,128)(2,1)} %reduce-scatter.13.cloned.1.call-done), channel_id=1, source_target_pairs={{0,16},{8,24},{16,0},{24,8},{1,17},{9,25},{17,1},{25,9},{2,18},{10... | collective-permute-start | bytes 884744 | tf_op jit(solution)/shard_map/ppermute | solution.py:53
  631.4 8.0 collective-permute-start.30
  633.9 71.0 %collective-permute-start.27 = (bf16[96,1536]{1,0:T(8,128)(2,1)S(1)}, bf16[96,1536]{1,0:T(8,128)(2,1)S(1)}, u32[]{:S(2)}, u32[]{:S(2)}) collective-permute-start(bf16[96,1536]{1,0:T(8,128)(2,1)S(1)} %add_convert_fusion.7), channel_id=1, source_target_pairs={{0,8},{8,0},{16,24},{24,16},{1,9},{9,1},{17,25},{25,17},{2,10},{10... | collective-permute-start | bytes 884744 | tf_op jit(solution)/shard_map/ppermute | solution.py:48
  639.4 72.1 %collective-permute-start.31 = (bf16[192,768]{1,0:T(8,128)(2,1)S(1)}, bf16[192,768]{1,0:T(8,128)(2,1)S(1)}, u32[]{:S(2)}, u32[]{:S(2)}) collective-permute-start(bf16[192,768]{1,0:T(8,128)(2,1)S(1)} %add_convert_fusion.5), channel_id=1, source_target_pairs={{0,8},{8,0},{16,24},{24,16},{1,9},{9,1},{17,25},{25,17},{2,10},{10... | collective-permute-start | bytes 884744 | tf_op jit(solution)/shard_map/ppermute | solution.py:48
  703.4 8.0 collective-permute-start.22
  711.5 1.6 collective-permute-start.23
  775.0 73.3 %copy-start.51 = (bf16[96,1536]{1,0:T(8,128)(2,1)S(1)}, bf16[96,1536]{1,0:T(8,128)(2,1)}, u32[]{:S(2)}) copy-start(bf16[96,1536]{1,0:T(8,128)(2,1)} %reduce-scatter.11.cloned.1.call-done) | copy-start | bytes 884740
  775.0 73.3 %collective-permute-start.24 = (bf16[96,1536]{1,0:T(8,128)(2,1)}, bf16[96,1536]{1,0:T(8,128)(2,1)S(1)}, u32[]{:S(2)}, u32[]{:S(2)}) collective-permute-start(bf16[96,1536]{1,0:T(8,128)(2,1)} %reduce-scatter.11.cloned.1.call-done), channel_id=1, source_target_pairs={{0,16},{8,24},{16,0},{24,8},{1,17},{9,25},{17,1},{25,9},{2,18},{10... | collective-permute-start | bytes 884744 | tf_op jit(solution)/shard_map/ppermute | solution.py:53
  846.8 8.0 collective-permute-start.28
  848.4 7.2 collective-permute-start.25
  855.5 4.8 collective-permute-start.29
  919.1 7.9 collective-permute-start.20
  927.1 1.7 collective-permute-start.21
  (141 other events, 945.8 us)
Sparse Core Ops, SparseCore 0:
  12.7 55.0 all-gather.10
  70.6 50.6 all-gather.12
  124.0 50.6 all-gather.18
  176.7 50.5 all-gather.14
  229.9 50.6 all-gather.16
  282.6 50.5 all-gather.20
  420.1 67.2 all-reduce.14
  490.9 68.8 reduce-scatter.12
  563.3 68.0 reduce-scatter.16
  635.3 68.0 reduce-scatter.8
  706.9 68.0 reduce-scatter.10
  778.4 68.3 reduce-scatter.14
  850.9 68.1 reduce-scatter.6

commit v2 on v1

--- a/solution.py
+++ b/solution.py
@@ -13,6 +13,8 @@
 BF = jnp.bfloat16
 F32 = jnp.float32
 VMEM_BYTES = 48 * 1024 * 1024
+
+GATHER_ORDER = (("wide", 0), ("branch", 0), ("wide", 1), ("branch", 1))
 
 VECTORS = (
     "first_scale",
@@ -22,9 +24,9 @@
     "output_bias",
     "second_scale",
     "second_shift",
-    "up_bias",
     "down_bias",
 )
+LINE_STEPS = (1, 2)
 
 
 def matmul(left, right):
@@ -61,13 +63,115 @@
     )
 
 
-def gather_owners(shard):
-    return lax.all_gather(shard, "wt", axis=0, tiled=True)
-
-
-def sum_to_owner(values):
-    mine = lax.psum_scatter(values.astype(BF), "wt", scatter_dimension=0, tiled=True)
-    return mine.astype(F32) + swap_row(mine).astype(F32)
+def swap_pair(values):
+    pairs = [(i, i ^ 1) for i in range(lax.axis_size("wt"))]
+    return lax.ppermute(values, "wt", pairs)
+
+
+def shift_line(values, step):
+    owners = lax.axis_size("wt")
+    pairs = [(i, (i + 2 * step) % owners) for i in range(owners)]
+    return lax.ppermute(values, "wt", pairs)
+
+
+def picked(values, index, axis):
+    return lax.dynamic_index_in_dim(values, index, axis, keepdims=False)
+
+
+def after(values, earlier):
+    return lax.optimization_barrier((values, earlier))[0]
+
+
+def swap_line(values, step):
+    pairs = [(i, i ^ (2 * step)) for i in range(lax.axis_size("wt"))]
+    return lax.ppermute(values, "wt", pairs)
+
+
+def doubled(values, step):
+    return jnp.concatenate([values, swap_line(values, step)], 0)
+
+
+def place_kernel(fill, where_ref, *refs):
+    fill(where_ref, *refs)
+
+
+def place(fill, where, sources, spots, name):
+    depth = sources[0][0].shape[0]
+    rows = sources[0][0].shape[1]
+    size = sum(math.prod(spot) for spot in spots) * depth
+
+    def spot_index(spot):
+        blank = (0,) * len(spot)
+        return lambda k, w: (jnp.bitwise_xor(w[0], k),) + blank
+
+    return pl.pallas_call(
+        lambda *refs: place_kernel(fill, *refs),
+        grid_spec=pltpu.PrefetchScalarGridSpec(
+            num_scalar_prefetch=1,
+            grid=(depth,),
+            in_specs=[
+                pl.BlockSpec((1, rows, width), lambda k, w, block=block: (k, 0, block))
+                for _, width, block in sources
+            ],
+            out_specs=[pl.BlockSpec((1,) + spot, spot_index(spot)) for spot in spots],
+        ),
+        out_shape=[jax.ShapeDtypeStruct((depth,) + spot, BF) for spot in spots],
+        compiler_params=pltpu.CompilerParams(vmem_limit_bytes=VMEM_BYTES),
+        cost_estimate=pl.CostEstimate(flops=0, bytes_accessed=4 * size, transcendentals=0),
+        name=name,
+    )(where, *(array for array, _, _ in sources))
+
+
+def fill_in(where_ref, near_ref, far_ref, target):
+    target[0, where_ref[1]] = near_ref[0]
+    target[0, 1 - where_ref[1]] = far_ref[0]
+
+
+def fill_out(where_ref, near_ref, far_ref, near_there_ref, far_there_ref, target):
+    width = near_ref.shape[-1]
+    here = pl.ds(pl.multiple_of(where_ref[3] * width, 128), width)
+    there = pl.ds(pl.multiple_of((1 - where_ref[3]) * width, 128), width)
+    target[0, where_ref[1], :, here] = near_ref[0]
+    target[0, 1 - where_ref[1], :, here] = far_ref[0]
+    target[0, where_ref[1], :, there] = near_there_ref[0]
+    target[0, 1 - where_ref[1], :, there] = far_there_ref[0]
+
+
+def fill_wide(where_ref, near_ref, far_ref, near_there_ref, far_there_ref, up, down):
+    rows = near_ref.shape[1] // 2
+    features = down.shape[-1]
+    for source, across, over in (
+        (near_ref, where_ref[1], where_ref[2]),
+        (far_ref, 1 - where_ref[1], where_ref[2]),
+        (near_there_ref, where_ref[1], 1 - where_ref[2]),
+        (far_there_ref, 1 - where_ref[1], 1 - where_ref[2]),
+    ):
+        up[0, across, over] = source[0, :rows]
+        down[0, across, over, 0] = source[0, rows:, :features]
+        down[0, across, over, 1] = source[0, rows:, features:]
+
+
+def reduce_line(values, kind):
+    owners = lax.axis_size("wt")
+    depth = owners // 2
+    own = lax.axis_index("wt")
+    line, across = own // 2, own % 2
+    paired = values.reshape((depth, 2) + values.shape[1:])
+    theirs = swap_pair(picked(paired, 1 - across, 1))
+    mine = (picked(paired, across, 1).astype(F32) + theirs.astype(F32)).astype(kind)
+    arrived = [
+        shift_line(picked(mine, lax.rem(line + step, depth), 0), step) for step in range(1, depth)
+    ]
+    total = picked(mine, line, 0).astype(F32)
+    for other in arrived:
+        total = total + other.astype(F32)
+    return total
+
+
+def reduce_owners(values, kind=BF):
+    if lax.axis_size("wt") == 8:
+        return reduce_line(values, kind)
+    return lax.psum_scatter(values, "wt", scatter_dimension=0, tiled=False).astype(F32)
 
 
 def attend_kernel(q_ref, k_ref, v_ref, o_ref):
@@ -188,8 +292,8 @@
     down_bias,
 ):
     owners = lax.axis_size("wt")
-    place = lax.axis_index("seq")
-    core, side = place % 2, place // 2
+    seat = lax.axis_index("seq")
+    core, side = seat % 2, seat // 2
     frames_here, features = activations.shape[1:]
     half = features // 2
     shard = features // owners
@@ -214,6 +318,10 @@
     def half_columns(values):
         return lax.dynamic_slice_in_dim(values, core * half, half, 1)
 
+    direct = owners == 8
+    own = lax.axis_index("wt")
+    line, across = own // 2, own % 2
+    where = jnp.stack([line, across, side, core]).astype(jnp.int32)
     members = dict(
         first_scale=first_scale,
         first_shift=first_shift,
@@ -222,49 +330,132 @@
         output_bias=output_bias,
         second_scale=second_scale,
         second_shift=second_shift,
-        up_bias=up_bias,
         down_bias=down_bias,
     )
-    packed = jnp.concatenate([members[name] for name in VECTORS], 1)
-    spread = lax.all_gather(packed, "wt", axis=0, tiled=False)
-    vectors = []
+    narrow = len(VECTORS) * shard
+    packed = jnp.concatenate([members[name] for name in VECTORS] + [up_bias], 1)
+    if direct:
+        reached = packed[None]
+        for step in LINE_STEPS:
+            reached = doubled(reached, step)
+        other = swap_pair(reached)
+        spread = jnp.stack([reached, other], 1)
+        for bit in LINE_STEPS:
+            turned = spread.reshape((owners // (4 * bit), 2, bit, 2) + packed.shape)
+            spread = jnp.where((line & bit) == 0, turned, turned[:, ::-1]).reshape(spread.shape)
+        spread = jnp.where(across == 0, spread, spread[:, ::-1]).reshape(
+            (owners,) + packed.shape
+        )
+    else:
+        spread = lax.all_gather(packed, "wt", axis=0, tiled=False)
+    vector_rows = (
+        spread[:, :, :narrow]
+        .reshape(owners, LAYERS * len(VECTORS), shard)
+        .swapaxes(0, 1)
+        .reshape(LAYERS * len(VECTORS), features)
+        .astype(F32)
+    )
+    vectors = [
+        {
+            name: vector_rows[layer * len(VECTORS) + position]
+            for position, name in enumerate(VECTORS)
+        }
+        for layer in range(LAYERS)
+    ]
+    unit_rows = (
+        picked(spread[:, :, narrow:].reshape(owners, LAYERS, 2, unit_half), core, 2)
+        .swapaxes(0, 1)
+        .reshape(LAYERS, units // 2)
+        .astype(F32)
+    )
+
+    shards = {}
     for layer in range(LAYERS):
-        found, start = {}, 0
-        for name in VECTORS:
-            size = members[name].shape[1]
-            found[name] = spread[:, layer, start : start + size].reshape(-1).astype(F32)
-            start += size
-        vectors.append(found)
-
-    def unit_part(bias):
-        return lax.dynamic_index_in_dim(
-            bias.reshape(owners, 2, unit_half), core, 1, keepdims=False
-        ).reshape(-1)
-
-    weights = []
-    for layer in range(LAYERS):
-        branch = gather_owners(
-            jnp.concatenate(
-                [
-                    half_columns(query_weight[layer]),
-                    half_columns(key_weight[layer]),
-                    half_columns(value_weight[layer]),
-                    half_columns(output_weight[layer]),
-                ],
-                1,
-            )
+        shards["branch", layer] = jnp.concatenate(
+            [
+                half_columns(query_weight[layer]),
+                half_columns(key_weight[layer]),
+                half_columns(value_weight[layer]),
+                half_columns(output_weight[layer]),
+            ],
+            1,
         )
-        up = gather_owners(
-            lax.dynamic_index_in_dim(
-                up_weight[layer].reshape(shard, owners, 2, unit_half), core, 2, keepdims=False
-            ).reshape(shard, units // 2)
+        shards["up", layer] = picked(
+            up_weight[layer].reshape(shard, owners, 2, unit_half), core, 2
+        ).reshape(shard, units // 2)
+        shards["down", layer] = lax.dynamic_slice_in_dim(
+            down_weight[layer], core * unit_half, unit_half, 0
         )
-        down = gather_owners(
-            lax.dynamic_slice_in_dim(down_weight[layer], core * unit_half, unit_half, 0)
-        )
-        out_half = branch[:, 3 * half :]
-        out = by_core(core, out_half, swap_core(out_half), 1)
-        weights.append((branch[:, : 3 * half], out, up, down))
+    gathered = {}
+    if direct:
+        earlier = [None] * 3
+        for kind, layer in GATHER_ORDER:
+            if kind == "branch":
+                piece = shards["branch", layer]
+            else:
+                up_piece = picked(
+                    shards["up", layer].reshape(2, shard // 2, units // 2), side, 0
+                )
+                down_piece = picked(
+                    shards["down", layer].reshape(2, 2, shard // 2, features), side, 0
+                )
+                down_piece = jnp.concatenate([down_piece[0], down_piece[1]], -1)
+                piece = jnp.concatenate([up_piece, down_piece], 0)
+            near = piece[None]
+            for position, step in enumerate(LINE_STEPS):
+                if earlier[position] is not None:
+                    near = after(near, earlier[position])
+                near = doubled(near, step)
+                earlier[position] = near
+            if earlier[2] is not None:
+                near = after(near, earlier[2])
+            far = swap_pair(near)
+            earlier[2] = far
+            if kind == "branch":
+                (gathered["in", layer],) = place(
+                    fill_in,
+                    where,
+                    ((near, 3 * half, 0), (far, 3 * half, 0)),
+                    ((2, shard, 3 * half),),
+                    "place_in",
+                )
+                gathered["in", layer] = gathered["in", layer].reshape(features, 3 * half)
+                swapped = swap_core(
+                    jnp.concatenate([near[:, :, 3 * half :], far[:, :, 3 * half :]], 2)
+                )
+                (gathered["out", layer],) = place(
+                    fill_out,
+                    where,
+                    ((near, half, 3), (far, half, 3), (swapped, half, 0), (swapped, half, 1)),
+                    ((2, shard, features),),
+                    "place_out",
+                )
+                gathered["out", layer] = gathered["out", layer].reshape(features, features)
+            else:
+                width = 2 * features
+                gathered["up", layer], gathered["down", layer] = place(
+                    fill_wide,
+                    where,
+                    tuple((v, width, 0) for v in (near, far, swap_row(near), swap_row(far))),
+                    ((2, 2, shard // 2, width), (2, 2, 2, shard // 2, features)),
+                    "place_wide",
+                )
+                gathered["up", layer] = gathered["up", layer].reshape(features, units // 2)
+                gathered["down", layer] = gathered["down", layer].reshape(units // 2, features)
+    else:
+        for layer in range(LAYERS):
+            for kind in ("up", "down"):
+                gathered[kind, layer] = lax.all_gather(
+                    shards[kind, layer], "wt", axis=0, tiled=True
+                )
+            branch = lax.all_gather(shards["branch", layer], "wt", axis=0, tiled=True)
+            gathered["in", layer] = branch[:, : 3 * half]
+            out_half = branch[:, 3 * half :]
+            gathered["out", layer] = by_core(core, out_half, swap_core(out_half), 1)
+    weights = [
+        tuple(gathered[kind, layer] for kind in ("in", "out", "up", "down"))
+        for layer in range(LAYERS)
+    ]
 
     hidden = to_chip(activations).astype(F32)
     kept = []
@@ -286,7 +477,7 @@
         middle = hidden + matmul(mixture, out_weight) + vec["output_bias"]
         flat, _ = norm_parts(middle)
         second = (flat * vec["second_scale"] + vec["second_shift"]).astype(BF)
-        upward = matmul(second, up) + unit_part(vec["up_bias"])
+        upward = matmul(second, up) + unit_rows[layer]
         activated, slope = gelu_parts(upward)
         activated = activated.astype(BF)
         slope = slope.astype(BF)
@@ -299,20 +490,37 @@
                 partial, (1 - core) * 2 * frames_here, 2 * frames_here, 0
             )
             total = own_rows(partial) + swap_core(theirs.astype(BF))
-            result = from_chip((own_rows(middle) + vec["down_bias"] + total).astype(BF))
+            result_rows = (own_rows(middle) + vec["down_bias"] + total).astype(BF)
 
     grad_hidden = to_chip(upstream).astype(F32)
     settled = [None] * LAYERS
+    vector_grads = [None] * LAYERS
     for layer in reversed(range(LAYERS)):
         vec = vectors[layer]
         in_weight, out_weight, up, down = weights[layer]
         hidden, normed, qkv, mixture, middle, second, activated, slope = kept[layer]
         grads = {}
         down_in = grad_hidden.astype(BF)
-        grad_down = sum_to_owner(left_product(activated, down_in))
+        grad_down = left_product(activated, down_in).astype(BF)
+        grad_down = grad_down.reshape(owners, 2, 2, unit_half // 4, features)
+        down_sent = picked(grad_down, 1 - side, 1)
+        down_there = swap_row(jnp.concatenate([down_sent[:, 0], down_sent[:, 1]], -1))
         grads["down_bias"] = column_sums(down_in)
         grad_upward = (slope.astype(F32) * right_product(down_in, down)).astype(BF)
-        grad_up = sum_to_owner(left_product(second, grad_upward))
+        grad_up = left_product(second, grad_upward).astype(BF)
+        grad_up = grad_up.reshape(owners, 2, shard // 2, units // 2)
+        up_there = swap_row(picked(grad_up, 1 - side, 1))
+        down_kept = picked(grad_down, side, 1)
+        down_kept = jnp.concatenate([down_kept[:, 0], down_kept[:, 1]], -1)
+        grad_wide = reduce_owners(
+            jnp.concatenate(
+                [
+                    (picked(grad_up, side, 1).astype(F32) + up_there.astype(F32)).astype(BF),
+                    (down_kept.astype(F32) + down_there.astype(F32)).astype(BF),
+                ],
+                1,
+            )
+        )
         grad_up_bias = column_sums(grad_upward)
         partial = right_product(grad_upward, up)
         grad_second = partial + swap_core(partial.astype(BF))
@@ -327,9 +535,13 @@
         grad_mixture = right_product(branch_in, out_rows).astype(BF)
         grad_qkv = jnp.concatenate(attend_back(qkv, grad_mixture), 1)
         grad_in = left_product(normed, grad_qkv)
-        grad_branch = sum_to_owner(jnp.concatenate([grad_in, grad_out], 1))
+        grad_branch = jnp.concatenate([grad_in.astype(BF), grad_out.astype(BF)], 1)
+        grad_branch = reduce_owners(grad_branch.reshape(owners, shard, 2 * features))
         grad_in_bias = column_sums(grad_qkv)
         partial = right_product(grad_qkv, in_weight)
+        if layer == 0:
+            result_rows = after(result_rows, grad_qkv)
+            result = from_chip(result_rows)
         if layer > 0:
             grad_normed = partial + swap_core(partial.astype(BF))
             before, grads["first_scale"], grads["first_shift"] = norm_back(
@@ -346,46 +558,67 @@
             )
             input_grad = from_chip(own_rows(grad_middle) + before)
 
-        first = (core == 0).astype(F32)
-        for name in ("down_bias", "second_scale", "second_shift", "output_bias"):
-            grads[name] = grads[name] * first
-        if layer > 0:
-            grads["first_scale"] = grads["first_scale"] * first
-            grads["first_shift"] = grads["first_shift"] * first
+        grads["query_bias"] = grad_in_bias[:half]
+        grads["value_bias"] = grad_in_bias[2 * half :]
         blank = jnp.zeros((half,), F32)
-        grads["query_bias"] = by_core(core, grad_in_bias[:half], blank, 0)
-        grads["value_bias"] = by_core(core, grad_in_bias[2 * half :], blank, 0)
-        unit_rows = grad_up_bias.reshape(owners, 1, unit_half)
-        grads["up_bias"] = by_core(core, unit_rows, jnp.zeros_like(unit_rows), 1).reshape(-1)
-        packed = jnp.concatenate([grads[name].reshape(owners, -1) for name in VECTORS], 1)
-        packed = lax.psum_scatter(packed, "wt", scatter_dimension=0, tiled=False)
-        packed = packed + swap_row(packed)
-        packed = packed + swap_core(packed)
-        done, start = {}, 0
+        rows = []
         for name in VECTORS:
-            size = members[name].shape[1]
-            done[name] = packed[start : start + size]
-            start += size
-
-        def both(mine):
-            mine = mine.astype(BF)
-            other = swap_core(mine).astype(F32)
-            mine = mine.astype(F32)
-            return jnp.where(core == 0, mine, other), jnp.where(core == 0, other, mine)
-
-        low, high = both(grad_branch)
+            values = grads[name]
+            if name in ("query_bias", "value_bias"):
+                values = jnp.where(
+                    core == 0,
+                    jnp.concatenate([values, blank]),
+                    jnp.concatenate([blank, values]),
+                )
+            elif layer > 0 or name not in ("first_scale", "first_shift"):
+                values = jnp.where(core == 0, values, 0.0)
+            rows.append(values)
+        vector_grads[layer] = (jnp.stack(rows), grad_up_bias)
+        done = {}
+        sent = jnp.concatenate([grad_branch, grad_wide], 0).astype(BF)
+        other = swap_row(sent)
+        grad_branch = (grad_branch + other[:shard].astype(F32)).astype(BF)
+        wide, wide_there = sent[shard:], other[shard:]
+        wide = jnp.where(
+            side == 0, jnp.stack([wide, wide_there]), jnp.stack([wide_there, wide])
+        ).reshape(2 * shard, 2 * features)
+        mine = jnp.concatenate([grad_branch, wide], 0)
+        other = swap_core(mine)
+        low = jnp.where(core == 0, mine, other).astype(F32)
+        high = jnp.where(core == 0, other, mine).astype(F32)
         for position, name in enumerate(
             ("query_weight", "key_weight", "value_weight", "output_weight")
         ):
             part = slice(position * half, (position + 1) * half)
-            done[name] = jnp.concatenate([low[:, part], high[:, part]], 1)
-        low, high = both(grad_up)
-        done["up_weight"] = jnp.stack(
-            [low.reshape(shard, owners, unit_half), high.reshape(shard, owners, unit_half)], 2
-        ).reshape(shard, units)
-        low, high = both(grad_down)
-        done["down_weight"] = jnp.concatenate([low, high], 0)
+            done[name] = jnp.concatenate([low[:shard, part], high[:shard, part]], 1)
+
+        def up_part(values):
+            values = values[shard:].reshape(2, 2, shard // 2, units // 2)[:, 0]
+            return values.reshape(shard, owners, unit_half)
+
+        def down_part(values):
+            values = values[shard:].reshape(2, 2, unit_half // 4, units // 2)[:, 1]
+            values = values.reshape(2, unit_half // 4, 2, features)
+            return jnp.swapaxes(values, 1, 2).reshape(unit_half, features)
+
+        done["up_weight"] = jnp.stack([up_part(low), up_part(high)], 2).reshape(shard, units)
+        done["down_weight"] = jnp.concatenate([down_part(low), down_part(high)], 0)
         settled[layer] = done
+
+    packed = jnp.stack([rows for rows, _ in vector_grads])
+    packed = packed.reshape(LAYERS * len(VECTORS), owners, shard).swapaxes(0, 1)
+    packed = packed.reshape(owners, LAYERS * narrow)
+    from_units = jnp.stack([values for _, values in vector_grads])
+    from_units = from_units.reshape(LAYERS, owners, unit_half).swapaxes(0, 1)
+    from_units = from_units.reshape(owners, LAYERS * unit_half)
+    packed = reduce_owners(jnp.concatenate([packed, from_units], 1), F32)
+    packed = packed + swap_row(packed)
+    other = swap_core(packed)
+    narrow_sum = (packed + other)[: LAYERS * narrow].reshape(LAYERS, len(VECTORS), shard)
+    unit_mine = packed[LAYERS * narrow :].reshape(LAYERS, unit_half)
+    unit_other = other[LAYERS * narrow :].reshape(LAYERS, unit_half)
+    summed = {name: narrow_sum[:, position] for position, name in enumerate(VECTORS)}
+    summed["up_bias"] = by_core(core, unit_mine, unit_other, 1)
 
     names = (
         "first_scale",
@@ -405,7 +638,10 @@
         "down_bias",
     )
     final = tuple(
-        jnp.stack([settled[layer][name] for layer in range(LAYERS)]) for name in names
+        summed[name]
+        if name in summed
+        else jnp.stack([settled[layer][name] for layer in range(LAYERS)])
+        for name in names
     )
     return (result, input_grad) + final
 

time: 948 us -> 582 us (0.61)
  the two profiles are of different devices: /device:TPU:0 before, /device:TPU:15 now
where the time goes in v2:
time: 582 us; the launch traced here: 571 us
  waiting for transfers between devices  212 us (36%)
  local copies, waits for them, and re-layouts  106 us (18%)
  starting transfers between devices  87 us (15%)
  other arithmetic  76.2 us (13%)
  matrix products  46.7 us (8%)
  Pallas kernels  39.9 us (7%)
    ppermute x15, waiting for transfers between devices, swap_row(): return lax.ppermute(values, 'seq', pairs)  64.5 us
    ppermute x15, waiting for transfers between devices, shift_line(): return lax.ppermute(values, 'wt', pairs)  62.6 us
    ppermute x10, waiting for transfers between devices, swap_line(): return lax.ppermute(values, 'wt', pairs)  42.9 us
    ppermute x10, waiting for transfers between devices, swap_pair(): return lax.ppermute(values, 'wt', pairs)  41.9 us
    ppermute x15, starting transfers between devices, swap_core(): return lax.ppermute(values, 'seq', pairs)  35.3 us
    unnamed x369, local copies, waits for them, and re-layouts  21.4 us
    ppermute x10, starting transfers between devices, swap_line(): return lax.ppermute(values, 'wt', pairs)  18.6 us
    dot_general x8, matrix products, right_product(): lax.dot_general(left, right, (((1,), (1,)), ((), ())), preferred_element_...  18.5 us
  transfers between devices with their start and end apart: 65, of which 25 were waited for; matrix products, arithmetic and copies ran while one was open for 28% of the time, Pallas kernels for 7%

profile of v2, /device:TPU:15, one launch (start us, length us, event | category | flops | bytes accessed | tf_op | source)
XLA Modules:
  0.0 571.4 jit_solution(7420658027788379853)
XLA Ops:
  3.9 4.8 dynamic-slice_reduce_fusion
  33.3 4.4 collective-permute-start.1
  37.9 19.1 %collective-permute-done.7 = bf16[2,96,1536]{2,1,0:T(8,128)(2,1)} collective-permute-done((bf16[2,96,1536]{2,1,0:T(8,128)(2,1)S(1)}, bf16[2,96,1536]{2,1,0:T(8,128)(2,1)}, u32[]{:S(2)}, u32[]{:S(2)}) %collective-permute-start.7) | collective-permute-done | bytes 589856 | tf_op jit(solution)/shard_map/ppermute | solution.py:87
  58.6 3.3 collective-permute-start.8
  64.3 19.9 %collective-permute-done.8 = bf16[2,96,1536]{2,1,0:T(8,128)(2,1)S(1)} collective-permute-done((bf16[2,96,1536]{2,1,0:T(8,128)(2,1)S(1)}, bf16[2,96,1536]{2,1,0:T(8,128)(2,1)S(1)}, u32[]{:S(2)}, u32[]{:S(2)}) %collective-permute-start.8) | collective-permute-done | bytes 589856 | tf_op jit(solution)/shard_map/ppermute | solution.py:87
  89.0 2.8 collective-permute-done.17
  91.9 4.0 collective-permute-start.18
  95.9 15.5 %collective-permute-done.10.refs_2_ = bf16[4,96,1536]{2,1,0:T(8,128)(2,1)S(1)} collective-permute-done((bf16[4,96,1536]{2,1,0:T(8,128)(2,1)S(1)}, bf16[4,96,1536]{2,1,0:T(8,128)(2,1)S(1)}, u32[]{:S(2)}, u32[]{:S(2)}) %collective-permute-start.10) | collective-permute-done | bytes 1179680 | tf_op jit(solution)/shard_map/ppermute | solution.py:68
  117.5 5.7 attend.2
  124.0 3.3 collective-permute-start.19
  127.2 10.1 %collective-permute-done.14.refs_4_ = bf16[4,96,1536]{2,1,0:T(8,128)(2,1)S(1)} collective-permute-done((bf16[4,96,1536]{2,1,0:T(8,128)(2,1)S(1)}, bf16[4,96,1536]{2,1,0:T(8,128)(2,1)S(1)}, u32[]{:S(2)}, u32[]{:S(2)}) %collective-permute-start.14) | collective-permute-done | bytes 1179680 | tf_op jit(solution)/shard_map/ppermute | solution.py:55
  137.6 3.3 place_wide.2
  145.5 3.2 multiply_convert_fusion.1
  148.8 2.8 fusion.79
  151.5 4.1 collective-permute-start.15
  168.0 20.3 %collective-permute-done.21.refs_2_ = bf16[4,96,1536]{2,1,0:T(8,128)(2,1)S(1)} collective-permute-done((bf16[4,96,1536]{2,1,0:T(8,128)(2,1)S(1)}, bf16[4,96,1536]{2,1,0:T(8,128)(2,1)S(1)}, u32[]{:S(2)}, u32[]{:S(2)}) %collective-permute-start.21) | collective-permute-done | bytes 1179680 | tf_op jit(solution)/shard_map/ppermute | solution.py:68
  188.3 3.5 collective-permute-start.23
  195.5 5.7 attend.3
  202.7 12.7 %collective-permute-done.25.refs_4_ = bf16[4,96,1536]{2,1,0:T(8,128)(2,1)S(1)} collective-permute-done((bf16[4,96,1536]{2,1,0:T(8,128)(2,1)}, bf16[4,96,1536]{2,1,0:T(8,128)(2,1)S(1)}, u32[]{:S(2)}, u32[]{:S(2)}) %collective-permute-start.25) | collective-permute-done | bytes 1179680 | tf_op jit(solution)/shard_map/ppermute | solution.py:55
  215.4 4.7 place_wide.3
  225.2 4.8 convert_reduce_fusion
  229.9 2.8 fusion.81
  234.4 2.8 collective-permute-start.29
  240.1 3.2 convolution_convert_fusion
  255.9 2.8 convert_reduce_fusion.5
  259.4 8.2 %attend_back.2 = (bf16[512,384]{1,0:T(8,128)(2,1)S(1)}, bf16[512,384]{1,0:T(8,128)(2,1)S(1)}, bf16[512,384]{1,0:T(8,128)(2,1)S(1)}) custom-call(bf16[512,1152]{1,0:T(8,128)(2,1)S(1)} %fusion.13.q_ref.k_ref.v_ref, bf16[512,1152]{1,0:T(8,128)(2,1)S(1)} %fusion.13.q_ref.k_ref.v_ref, bf16[512,1152]{1,0:T(8,128)(2,1)S(1)} %fusion.13.q_ref.k_ref.v_ref, ...), custom_call_target="tpu_custom_call" | custom-call | flops 1006632960 | bytes 2752512 | tf_op jit(solution)/shard_map/attend_back/pallas_call | solution.py:232
  279.5 11.9 %collective-permute-done.58 = bf16[8,48,1536]{2,1,0:T(8,128)(2,1)} collective-permute-done((bf16[8,48,1536]{2,1,0:T(8,128)(2,1)}, bf16[8,48,1536]{2,1,0:T(8,128)(2,1)}, u32[]{:S(2)}, u32[]{:S(2)}) %collective-permute-start.58) | collective-permute-done | bytes 1179680 | tf_op jit(solution)/shard_map/ppermute | solution.py:55
  300.5 3.3 convert_reduce_fusion.1
  303.8 2.8 fusion.83
  312.8 3.0 convolution_convert_fusion.4
  323.7 3.1 collective-permute-start.54
  336.3 14.3 %collective-permute-done.55 = bf16[96,1536]{1,0:T(8,128)(2,1)} collective-permute-done((bf16[96,1536]{1,0:T(8,128)(2,1)}, bf16[96,1536]{1,0:T(8,128)(2,1)}, u32[]{:S(2)}, u32[]{:S(2)}) %collective-permute-start.55) | collective-permute-done | bytes 294944 | tf_op jit(solution)/shard_map/ppermute | solution.py:74
  350.6 2.9 collective-permute-done.56
  363.8 8.4 %attend_back.3 = (bf16[512,384]{1,0:T(8,128)(2,1)S(1)}, bf16[512,384]{1,0:T(8,128)(2,1)S(1)}, bf16[512,384]{1,0:T(8,128)(2,1)S(1)}) custom-call(bf16[512,1152]{1,0:T(8,128)(2,1)S(1)} %fusion.12.q_ref.k_ref.v_ref, bf16[512,1152]{1,0:T(8,128)(2,1)S(1)} %fusion.12.q_ref.k_ref.v_ref, bf16[512,1152]{1,0:T(8,128)(2,1)S(1)} %fusion.12.q_ref.k_ref.v_ref, ...), custom_call_target="tpu_custom_call" | custom-call | flops 1006632960 | bytes 2752512 | tf_op jit(solution)/shard_map/attend_back/pallas_call | solution.py:232
  387.7 4.2 collective-permute-start.33
  397.0 12.9 %collective-permute-done.46 = bf16[8,48,1536]{2,1,0:T(8,128)(2,1)S(1)} collective-permute-done((bf16[8,48,1536]{2,1,0:T(8,128)(2,1)S(1)}, bf16[8,48,1536]{2,1,0:T(8,128)(2,1)S(1)}, u32[]{:S(2)}, u32[]{:S(2)}) %collective-permute-start.46) | collective-permute-done | bytes 1179680 | tf_op jit(solution)/shard_map/ppermute | solution.py:55
  414.6 2.8 collective-permute-done.35
  419.0 3.6 collective-permute-start.37
  428.6 8.1 %collective-permute-start.40 = (f32[1920]{0:T(1024)S(1)}, f32[1920]{0:T(1024)S(1)}, u32[]{:S(2)}, u32[]{:S(2)}) collective-permute-start(f32[1920]{0:T(1024)S(1)} %add.540), channel_id=1, source_target_pairs={{0,8},{8,0},{16,24},{24,16},{1,9},{9,1},{17,25},{25,17},{2,10},{10... | collective-permute-start | bytes 23048 | tf_op jit(solution)/shard_map/ppermute | solution.py:50
  439.1 8.6 %collective-permute-done.34 = f32[128,768]{1,0:T(8,128)S(1)} collective-permute-done((f32[128,768]{1,0:T(8,128)S(1)}, f32[128,768]{1,0:T(8,128)S(1)}, u32[]{:S(2)}, u32[]{:S(2)}) %collective-permute-start.34) | collective-permute-done | bytes 393248 | tf_op jit(solution)/shard_map/ppermute | solution.py:55
  460.9 18.3 %collective-permute-done.43 = bf16[96,1536]{1,0:T(8,128)(2,1)S(1)} collective-permute-done((bf16[96,1536]{1,0:T(8,128)(2,1)S(1)}, bf16[96,1536]{1,0:T(8,128)(2,1)S(1)}, u32[]{:S(2)}, u32[]{:S(2)}) %collective-permute-start.43) | collective-permute-done | bytes 294944 | tf_op jit(solution)/shard_map/ppermute | solution.py:74
  479.2 3.4 collective-permute-done.44
  494.5 17.1 %collective-permute-done.49 = bf16[96,1536]{1,0:T(8,128)(2,1)} collective-permute-done((bf16[96,1536]{1,0:T(8,128)(2,1)}, bf16[96,1536]{1,0:T(8,128)(2,1)}, u32[]{:S(2)}, u32[]{:S(2)}) %collective-permute-start.49) | collective-permute-done | bytes 294944 | tf_op jit(solution)/shard_map/ppermute | solution.py:74
  516.1 3.3 stack_reshape_squeeze.15
  521.5 8.2 %collective-permute-done.51 = bf16[192,1536]{1,0:T(8,128)(2,1)} collective-permute-done((bf16[192,1536]{1,0:T(8,128)(2,1)}, bf16[192,1536]{1,0:T(8,128)(2,1)}, u32[]{:S(2)}, u32[]{:S(2)}) %collective-permute-start.51) | collective-permute-done | bytes 589856 | tf_op jit(solution)/shard_map/ppermute | solution.py:55
  535.2 2.7 pad_maximum_fusion.7
  540.9 3.5 stack_reshape.7
  559.1 2.7 stack_reshape.6
  (757 shorter events, 240.9 us)
Async XLA Ops:
  11.0 18.0 %collective-permute-start.5 = (bf16[1,96,1536]{2,1,0:T(8,128)(2,1)S(1)}, bf16[1,96,1536]{2,1,0:T(8,128)(2,1)S(1)}, u32[]{:S(2)}, u32[]{:S(2)}) collective-permute-start(bf16[1,96,1536]{2,1,0:T(8,128)(2,1)S(1)} %maximum_bitcast_fusion.3), channel_id=1, source_target_pairs={{0,2},{1,3},{2,0},{3,1},{4,6},{5,7},{6,4},{7,5},{8,10},{9,11},{10,... | collective-permute-start | bytes 884744 | tf_op jit(solution)/shard_map/ppermute | solution.py:87
  11.9 21.3 %collective-permute-start = (bf16[128,768]{1,0:T(8,128)(2,1)}, bf16[128,768]{1,0:T(8,128)(2,1)S(1)}, u32[]{:S(2)}, u32[]{:S(2)}) collective-permute-start(bf16[128,768]{1,0:T(8,128)(2,1)} %get-tuple-element.171), channel_id=1, source_target_pairs={{0,16},{8,24},{16,0},{24,8},{1,17},{9,25},{17,1},{25,9},{2,18},{10... | collective-permute-start | bytes 589832 | tf_op jit(solution)/shard_map/ppermute | solution.py:55
  15.4 46.4 %collective-permute-start.27 = (bf16[128,768]{1,0:T(8,128)(2,1)}, bf16[128,768]{1,0:T(8,128)(2,1)S(1)}, u32[]{:S(2)}, u32[]{:S(2)}) collective-permute-start(bf16[128,768]{1,0:T(8,128)(2,1)} %get-tuple-element.169), channel_id=1, source_target_pairs={{0,16},{8,24},{16,0},{24,8},{1,17},{9,25},{17,1},{25,9},{2,18},{10... | collective-permute-start | bytes 589832 | tf_op jit(solution)/shard_map/ppermute | solution.py:55
  29.1 27.9 %collective-permute-start.7 = (bf16[2,96,1536]{2,1,0:T(8,128)(2,1)S(1)}, bf16[2,96,1536]{2,1,0:T(8,128)(2,1)}, u32[]{:S(2)}, u32[]{:S(2)}) collective-permute-start(bf16[2,96,1536]{2,1,0:T(8,128)(2,1)S(1)} %pad_maximum_fusion.14), channel_id=1, source_target_pairs={{0,4},{1,5},{2,6},{3,7},{4,0},{5,1},{6,2},{7,3},{8,12},{9,13},{10,... | collective-permute-start | bytes 1769480 | tf_op jit(solution)/shard_map/ppermute | solution.py:87
  33.3 29.4 %collective-permute-start.1 = (bf16[256,768]{1,0:T(8,128)(2,1)S(1)}, bf16[256,768]{1,0:T(8,128)(2,1)S(1)}, u32[]{:S(2)}, u32[]{:S(2)}) collective-permute-start(bf16[256,768]{1,0:T(8,128)(2,1)S(1)} %pad_maximum_fusion.24), channel_id=1, source_target_pairs={{0,8},{8,0},{16,24},{24,16},{1,9},{9,1},{17,25},{25,17},{2,10},{10... | collective-permute-start | bytes 1179656 | tf_op jit(solution)/shard_map/ppermute | solution.py:50
  37.7 20.8 %collective-permute-start.6 = (bf16[1,96,1536]{2,1,0:T(8,128)(2,1)S(1)}, bf16[1,96,1536]{2,1,0:T(8,128)(2,1)S(1)}, u32[]{:S(2)}, u32[]{:S(2)}) collective-permute-start(bf16[1,96,1536]{2,1,0:T(8,128)(2,1)S(1)} %maximum_bitcast_fusion.2), channel_id=1, source_target_pairs={{0,2},{1,3},{2,0},{3,1},{4,6},{5,7},{6,4},{7,5},{8,10},{9,11},{10,... | collective-permute-start | bytes 884744 | tf_op jit(solution)/shard_map/ppermute | solution.py:87
  58.2 27.1 %collective-permute-start.9 = (bf16[4,96,1536]{2,1,0:T(8,128)(2,1)S(1)}, bf16[4,96,1536]{2,1,0:T(8,128)(2,1)S(1)}, u32[]{:S(2)}, u32[]{:S(2)}) collective-permute-start(bf16[4,96,1536]{2,1,0:T(8,128)(2,1)S(1)} %pad_maximum_fusion.8.refs_1_), channel_id=1, source_target_pairs={{0,1},{1,0},{2,3},{3,2},{4,5},{5,4},{6,7},{7,6},{8,9},{9,8},{10,11... | collective-permute-start | bytes 3538952 | tf_op jit(solution)/shard_map/ppermute | solution.py:68
  58.6 25.6 %collective-permute-start.8 = (bf16[2,96,1536]{2,1,0:T(8,128)(2,1)S(1)}, bf16[2,96,1536]{2,1,0:T(8,128)(2,1)S(1)}, u32[]{:S(2)}, u32[]{:S(2)}) collective-permute-start(bf16[2,96,1536]{2,1,0:T(8,128)(2,1)S(1)} %constant_dynamic-update-slice_fusion), channel_id=1, source_target_pairs={{0,4},{1,5},{2,6},{3,7},{4,0},{5,1},{6,2},{7,3},{8,12},{9,13},{10,... | collective-permute-start | bytes 1769480 | tf_op jit(solution)/shard_map/ppermute | solution.py:87
  62.7 22.9 %collective-permute-start.16 = (bf16[1,96,1536]{2,1,0:T(8,128)(2,1)S(1)}, bf16[1,96,1536]{2,1,0:T(8,128)(2,1)S(1)}, u32[]{:S(2)}, u32[]{:S(2)}) collective-permute-start(bf16[1,96,1536]{2,1,0:T(8,128)(2,1)S(1)} %maximum_bitcast_fusion.5), channel_id=1, source_target_pairs={{0,2},{1,3},{2,0},{3,1},{4,6},{5,7},{6,4},{7,5},{8,10},{9,11},{10,... | collective-permute-start | bytes 884744 | tf_op jit(solution)/shard_map/ppermute | solution.py:87
  85.3 26.1 %collective-permute-start.10 = (bf16[4,96,1536]{2,1,0:T(8,128)(2,1)S(1)}, bf16[4,96,1536]{2,1,0:T(8,128)(2,1)S(1)}, u32[]{:S(2)}, u32[]{:S(2)}) collective-permute-start(bf16[4,96,1536]{2,1,0:T(8,128)(2,1)S(1)} %constant_dynamic-update-slice_fusion.2.refs_1_), channel_id=1, source_target_pairs={{0,1},{1,0},{2,3},{3,2},{4,5},{5,4},{6,7},{7,6},{8,9},{9,8},{10,11... | collective-permute-start | bytes 3538952 | tf_op jit(solution)/shard_map/ppermute | solution.py:68
  87.5 36.5 %collective-permute-start.13 = (bf16[4,96,1536]{2,1,0:T(8,128)(2,1)S(1)}, bf16[4,96,1536]{2,1,0:T(8,128)(2,1)S(1)}, u32[]{:S(2)}, u32[]{:S(2)}) collective-permute-start(bf16[4,96,1536]{2,1,0:T(8,128)(2,1)S(1)} %pad_maximum_fusion.8.refs_1_), channel_id=1, source_target_pairs={{0,16},{8,24},{16,0},{24,8},{1,17},{9,25},{17,1},{25,9},{2,18},{10... | collective-permute-start | bytes 3538952 | tf_op jit(solution)/shard_map/ppermute | solution.py:55
  87.8 49.6 %collective-permute-start.14 = (bf16[4,96,1536]{2,1,0:T(8,128)(2,1)S(1)}, bf16[4,96,1536]{2,1,0:T(8,128)(2,1)S(1)}, u32[]{:S(2)}, u32[]{:S(2)}) collective-permute-start(bf16[4,96,1536]{2,1,0:T(8,128)(2,1)S(1)} %collective-permute-done.9.refs_2_), channel_id=1, source_target_pairs={{0,16},{8,24},{16,0},{24,8},{1,17},{9,25},{17,1},{25,9},{2,18},{10... | collective-permute-start | bytes 3538952 | tf_op jit(solution)/shard_map/ppermute | solution.py:55
  91.9 31.5 %collective-permute-start.18 = (bf16[2,96,1536]{2,1,0:T(8,128)(2,1)S(1)}, bf16[2,96,1536]{2,1,0:T(8,128)(2,1)S(1)}, u32[]{:S(2)}, u32[]{:S(2)}) collective-permute-start(bf16[2,96,1536]{2,1,0:T(8,128)(2,1)S(1)} %constant_dynamic-update-slice_fusion.4), channel_id=1, source_target_pairs={{0,4},{1,5},{2,6},{3,7},{4,0},{5,1},{6,2},{7,3},{8,12},{9,13},{10,... | collective-permute-start | bytes 1769480 | tf_op jit(solution)/shard_map/ppermute | solution.py:87
  111.7 29.2 %collective-permute-start.12 = (bf16[4,96,768]{2,1,0:T(8,128)(2,1)S(1)}, bf16[4,96,768]{2,1,0:T(8,128)(2,1)S(1)}, u32[]{:S(2)}, u32[]{:S(2)}) collective-permute-start(bf16[4,96,768]{2,1,0:T(8,128)(2,1)S(1)} %pad_maximum_fusion.15), channel_id=1, source_target_pairs={{0,8},{8,0},{16,24},{24,16},{1,9},{9,1},{17,25},{25,17},{2,10},{10... | collective-permute-start | bytes 1769480 | tf_op jit(solution)/shard_map/ppermute | solution.py:50
  123.2 18.6 %collective-permute-start.11 = (bf16[512,384]{1,0:T(8,128)(2,1)S(1)}, bf16[512,384]{1,0:T(8,128)(2,1)S(1)}, u32[]{:S(2)}, u32[]{:S(2)}) collective-permute-start(bf16[512,384]{1,0:T(8,128)(2,1)S(1)} %attend.2), channel_id=1, source_target_pairs={{0,8},{8,0},{16,24},{24,16},{1,9},{9,1},{17,25},{25,17},{2,10},{10... | collective-permute-start | bytes 1179656 | tf_op jit(solution)/shard_map/ppermute | solution.py:50
  123.4 37.1 %collective-permute-start.28 = (bf16[256,768]{1,0:T(8,128)(2,1)}, bf16[256,768]{1,0:T(8,128)(2,1)}, u32[]{:S(2)}, u32[]{:S(2)}) collective-permute-start(bf16[256,768]{1,0:T(8,128)(2,1)} %pad_maximum_fusion.25), channel_id=1, source_target_pairs={{0,8},{8,0},{16,24},{24,16},{1,9},{9,1},{17,25},{25,17},{2,10},{10... | collective-permute-start | bytes 1179656 | tf_op jit(solution)/shard_map/ppermute | solution.py:50
  124.0 38.0 %collective-permute-start.19 = (bf16[2,96,1536]{2,1,0:T(8,128)(2,1)S(1)}, bf16[2,96,1536]{2,1,0:T(8,128)(2,1)}, u32[]{:S(2)}, u32[]{:S(2)}) collective-permute-start(bf16[2,96,1536]{2,1,0:T(8,128)(2,1)S(1)} %pad_maximum_fusion.16), channel_id=1, source_target_pairs={{0,4},{1,5},{2,6},{3,7},{4,0},{5,1},{6,2},{7,3},{8,12},{9,13},{10,... | collective-permute-start | bytes 1769480 | tf_op jit(solution)/shard_map/ppermute | solution.py:87
  137.4 25.9 %collective-permute-start.20 = (bf16[4,96,1536]{2,1,0:T(8,128)(2,1)S(1)}, bf16[4,96,1536]{2,1,0:T(8,128)(2,1)}, u32[]{:S(2)}, u32[]{:S(2)}) collective-permute-start(bf16[4,96,1536]{2,1,0:T(8,128)(2,1)S(1)} %constant_dynamic-update-slice_fusion.6.refs_1_), channel_id=1, source_target_pairs={{0,1},{1,0},{2,3},{3,2},{4,5},{5,4},{6,7},{7,6},{8,9},{9,8},{10,11... | collective-permute-start | bytes 3538952 | tf_op jit(solution)/shard_map/ppermute | solution.py:68
  163.2 25.0 %collective-permute-start.21 = (bf16[4,96,1536]{2,1,0:T(8,128)(2,1)S(1)}, bf16[4,96,1536]{2,1,0:T(8,128)(2,1)S(1)}, u32[]{:S(2)}, u32[]{:S(2)}) collective-permute-start(bf16[4,96,1536]{2,1,0:T(8,128)(2,1)S(1)} %pad_maximum_fusion.9.refs_1_), channel_id=1, source_target_pairs={{0,1},{1,0},{2,3},{3,2},{4,5},{5,4},{6,7},{7,6},{8,9},{9,8},{10,11... | collective-permute-start | bytes 3538952 | tf_op jit(solution)/shard_map/ppermute | solution.py:68
  164.5 38.2 %collective-permute-start.24 = (bf16[4,96,1536]{2,1,0:T(8,128)(2,1)S(1)}, bf16[4,96,1536]{2,1,0:T(8,128)(2,1)S(1)}, u32[]{:S(2)}, u32[]{:S(2)}) collective-permute-start(bf16[4,96,1536]{2,1,0:T(8,128)(2,1)S(1)} %constant_dynamic-update-slice_fusion.6.refs_1_), channel_id=1, source_target_pairs={{0,16},{8,24},{16,0},{24,8},{1,17},{9,25},{17,1},{25,9},{2,18},{10... | collective-permute-start | bytes 3538952 | tf_op jit(solution)/shard_map/ppermute | solution.py:55
  164.8 50.6 %collective-permute-start.25 = (bf16[4,96,1536]{2,1,0:T(8,128)(2,1)}, bf16[4,96,1536]{2,1,0:T(8,128)(2,1)S(1)}, u32[]{:S(2)}, u32[]{:S(2)}) collective-permute-start(bf16[4,96,1536]{2,1,0:T(8,128)(2,1)} %collective-permute-done.20.refs_2_), channel_id=1, source_target_pairs={{0,16},{8,24},{16,0},{24,8},{1,17},{9,25},{17,1},{25,9},{2,18},{10... | collective-permute-start | bytes 3538952 | tf_op jit(solution)/shard_map/ppermute | solution.py:55
  188.3 31.7 %collective-permute-start.23 = (bf16[4,96,768]{2,1,0:T(8,128)(2,1)S(1)}, bf16[4,96,768]{2,1,0:T(8,128)(2,1)S(1)}, u32[]{:S(2)}, u32[]{:S(2)}) collective-permute-start(bf16[4,96,768]{2,1,0:T(8,128)(2,1)S(1)} %pad_maximum_fusion.17), channel_id=1, source_target_pairs={{0,8},{8,0},{16,24},{24,16},{1,9},{9,1},{17,25},{25,17},{2,10},{10... | collective-permute-start | bytes 1769480 | tf_op jit(solution)/shard_map/ppermute | solution.py:50
  201.2 20.2 %collective-permute-start.22 = (bf16[512,384]{1,0:T(8,128)(2,1)S(1)}, bf16[512,384]{1,0:T(8,128)(2,1)S(1)}, u32[]{:S(2)}, u32[]{:S(2)}) collective-permute-start(bf16[512,384]{1,0:T(8,128)(2,1)S(1)} %attend.3), channel_id=1, source_target_pairs={{0,8},{8,0},{16,24},{24,16},{1,9},{9,1},{17,25},{25,17},{2,10},{10... | collective-permute-start | bytes 1179656 | tf_op jit(solution)/shard_map/ppermute | solution.py:50
  234.4 19.4 %collective-permute-start.29 = (bf16[512,768]{1,0:T(8,128)(2,1)}, bf16[512,768]{1,0:T(8,128)(2,1)}, u32[]{:S(2)}, u32[]{:S(2)}) collective-permute-start(bf16[512,768]{1,0:T(8,128)(2,1)} %get-tuple-element.212), channel_id=1, source_target_pairs={{0,8},{8,0},{16,24},{24,16},{1,9},{9,1},{17,25},{25,17},{2,10},{10... | collective-permute-start | bytes 2359304 | tf_op jit(solution)/shard_map/ppermute | solution.py:50
  238.4 39.5 %collective-permute-start.57 = (bf16[8,48,1536]{2,1,0:T(8,128)(2,1)}, bf16[8,48,1536]{2,1,0:T(8,128)(2,1)}, u32[]{:S(2)}, u32[]{:S(2)}) collective-permute-start(bf16[8,48,1536]{2,1,0:T(8,128)(2,1)} %dynamic-slice_bitcast_fusion.1), channel_id=1, source_target_pairs={{0,16},{8,24},{16,0},{24,8},{1,17},{9,25},{17,1},{25,9},{2,18},{10... | collective-permute-start | bytes 3538952 | tf_op jit(solution)/shard_map/ppermute | solution.py:55
  246.0 45.4 %collective-permute-start.58 = (bf16[8,48,1536]{2,1,0:T(8,128)(2,1)}, bf16[8,48,1536]{2,1,0:T(8,128)(2,1)}, u32[]{:S(2)}, u32[]{:S(2)}) collective-permute-start(bf16[8,48,1536]{2,1,0:T(8,128)(2,1)} %pad_maximum_fusion.11), channel_id=1, source_target_pairs={{0,16},{8,24},{16,0},{24,8},{1,17},{9,25},{17,1},{25,9},{2,18},{10... | collective-permute-start | bytes 3538952 | tf_op jit(solution)/shard_map/ppermute | solution.py:55
  271.9 22.9 %collective-permute-start.30 = (bf16[512,768]{1,0:T(8,128)(2,1)S(1)}, bf16[512,768]{1,0:T(8,128)(2,1)S(1)}, u32[]{:S(2)}, u32[]{:S(2)}) collective-permute-start(bf16[512,768]{1,0:T(8,128)(2,1)S(1)} %get-tuple-element.214), channel_id=1, source_target_pairs={{0,8},{8,0},{16,24},{24,16},{1,9},{9,1},{17,25},{25,17},{2,10},{10... | collective-permute-start | bytes 2359304 | tf_op jit(solution)/shard_map/ppermute | solution.py:50
  274.3 45.1 %collective-permute-start.53 = (bf16[4,96,1536]{2,1,0:T(8,128)(2,1)}, bf16[4,96,1536]{2,1,0:T(8,128)(2,1)}, u32[]{:S(2)}, u32[]{:S(2)}) collective-permute-start(bf16[4,96,1536]{2,1,0:T(8,128)(2,1)} %dynamic-slice_bitcast_fusion.2), channel_id=1, source_target_pairs={{0,1},{1,0},{2,3},{3,2},{4,5},{5,4},{6,7},{7,6},{8,9},{9,8},{10,11... | collective-permute-start | bytes 3538952 | tf_op jit(solution)/shard_map/ppermute | solution.py:68
  294.4 61.2 %collective-permute-start.59 = (bf16[4,96,1536]{2,1,0:T(8,128)(2,1)}, bf16[4,96,1536]{2,1,0:T(8,128)(2,1)}, u32[]{:S(2)}, u32[]{:S(2)}) collective-permute-start(bf16[4,96,1536]{2,1,0:T(8,128)(2,1)} %dynamic-slice_bitcast_fusion), channel_id=1, source_target_pairs={{0,1},{1,0},{2,3},{3,2},{4,5},{5,4},{6,7},{7,6},{8,9},{9,8},{10,11... | collective-permute-start | bytes 3538952 | tf_op jit(solution)/shard_map/ppermute | solution.py:68
  306.6 53.3 %collective-permute-start.31 = (bf16[512,768]{1,0:T(8,128)(2,1)}, bf16[512,768]{1,0:T(8,128)(2,1)S(1)}, u32[]{:S(2)}, u32[]{:S(2)}) collective-permute-start(bf16[512,768]{1,0:T(8,128)(2,1)} %get-tuple-element.216), channel_id=1, source_target_pairs={{0,8},{8,0},{16,24},{24,16},{1,9},{9,1},{17,25},{25,17},{2,10},{10... | collective-permute-start | bytes 2359304 | tf_op jit(solution)/shard_map/ppermute | solution.py:50
  326.8 23.9 %collective-permute-start.55 = (bf16[96,1536]{1,0:T(8,128)(2,1)}, bf16[96,1536]{1,0:T(8,128)(2,1)}, u32[]{:S(2)}, u32[]{:S(2)}) collective-permute-start(bf16[96,1536]{1,0:T(8,128)(2,1)} %get-tuple-element.152), channel_id=1, source_target_pairs={{0,4},{1,5},{2,6},{3,7},{4,0},{5,1},{6,2},{7,3},{8,12},{9,13},{10,... | collective-permute-start | bytes 884744 | tf_op jit(solution)/shard_map/ppermute | solution.py:74
  326.8 26.7 %collective-permute-start.56 = (bf16[96,1536]{1,0:T(8,128)(2,1)}, bf16[96,1536]{1,0:T(8,128)(2,1)}, u32[]{:S(2)}, u32[]{:S(2)}) collective-permute-start(bf16[96,1536]{1,0:T(8,128)(2,1)} %get-tuple-element.151), channel_id=1, source_target_pairs={{0,6},{1,7},{2,0},{3,1},{4,2},{5,3},{6,4},{7,5},{8,14},{9,15},{10,... | collective-permute-start | bytes 884744 | tf_op jit(solution)/shard_map/ppermute | solution.py:74
  336.1 59.3 %collective-permute-start.45 = (bf16[8,48,1536]{2,1,0:T(8,128)(2,1)}, bf16[8,48,1536]{2,1,0:T(8,128)(2,1)}, u32[]{:S(2)}, u32[]{:S(2)}) collective-permute-start(bf16[8,48,1536]{2,1,0:T(8,128)(2,1)} %dynamic-slice_bitcast_fusion.4), channel_id=1, source_target_pairs={{0,16},{8,24},{16,0},{24,8},{1,17},{9,25},{17,1},{25,9},{2,18},{10... | collective-permute-start | bytes 3538952 | tf_op jit(solution)/shard_map/ppermute | solution.py:55
  358.2 29.2 %collective-permute-start.60 = (bf16[96,1536]{1,0:T(8,128)(2,1)}, bf16[96,1536]{1,0:T(8,128)(2,1)}, u32[]{:S(2)}, u32[]{:S(2)}) collective-permute-start(bf16[96,1536]{1,0:T(8,128)(2,1)} %get-tuple-element.153), channel_id=1, source_target_pairs={{0,2},{1,3},{2,4},{3,5},{4,6},{5,7},{6,0},{7,1},{8,10},{9,11},{10,... | collective-permute-start | bytes 884744 | tf_op jit(solution)/shard_map/ppermute | solution.py:74
  358.2 29.5 %collective-permute-start.61 = (bf16[96,1536]{1,0:T(8,128)(2,1)}, bf16[96,1536]{1,0:T(8,128)(2,1)}, u32[]{:S(2)}, u32[]{:S(2)}) collective-permute-start(bf16[96,1536]{1,0:T(8,128)(2,1)} %get-tuple-element.155), channel_id=1, source_target_pairs={{0,4},{1,5},{2,6},{3,7},{4,0},{5,1},{6,2},{7,3},{8,12},{9,13},{10,... | collective-permute-start | bytes 884744 | tf_op jit(solution)/shard_map/ppermute | solution.py:74
  358.4 33.5 %collective-permute-start.62 = (bf16[96,1536]{1,0:T(8,128)(2,1)}, bf16[96,1536]{1,0:T(8,128)(2,1)}, u32[]{:S(2)}, u32[]{:S(2)}) collective-permute-start(bf16[96,1536]{1,0:T(8,128)(2,1)} %get-tuple-element.154), channel_id=1, source_target_pairs={{0,6},{1,7},{2,0},{3,1},{4,2},{5,3},{6,4},{7,5},{8,14},{9,15},{10,... | collective-permute-start | bytes 884744 | tf_op jit(solution)/shard_map/ppermute | solution.py:74
  385.4 24.6 %collective-permute-start.46 = (bf16[8,48,1536]{2,1,0:T(8,128)(2,1)S(1)}, bf16[8,48,1536]{2,1,0:T(8,128)(2,1)S(1)}, u32[]{:S(2)}, u32[]{:S(2)}) collective-permute-start(bf16[8,48,1536]{2,1,0:T(8,128)(2,1)S(1)} %copy-done.71), channel_id=1, source_target_pairs={{0,16},{8,24},{16,0},{24,8},{1,17},{9,25},{17,1},{25,9},{2,18},{10... | collective-permute-start | bytes 3538952 | tf_op jit(solution)/shard_map/ppermute | solution.py:55
  387.4 63.9 %collective-permute-start.41 = (bf16[4,96,1536]{2,1,0:T(8,128)(2,1)}, bf16[4,96,1536]{2,1,0:T(8,128)(2,1)}, u32[]{:S(2)}, u32[]{:S(2)}) collective-permute-start(bf16[4,96,1536]{2,1,0:T(8,128)(2,1)} %dynamic-slice_bitcast_fusion.5), channel_id=1, source_target_pairs={{0,1},{1,0},{2,3},{3,2},{4,5},{5,4},{6,7},{7,6},{8,9},{9,8},{10,11... | collective-permute-start | bytes 3538952 | tf_op jit(solution)/shard_map/ppermute | solution.py:68
  387.7 23.9 %collective-permute-start.33 = (bf16[256,768]{1,0:T(8,128)(2,1)S(1)}, bf16[256,768]{1,0:T(8,128)(2,1)S(1)}, u32[]{:S(2)}, u32[]{:S(2)}) collective-permute-start(bf16[256,768]{1,0:T(8,128)(2,1)S(1)} %dynamic-slice_convert_fusion), channel_id=1, source_target_pairs={{0,8},{8,0},{16,24},{24,16},{1,9},{9,1},{17,25},{25,17},{2,10},{10... | collective-permute-start | bytes 1179656 | tf_op jit(solution)/shard_map/ppermute | solution.py:50
  394.3 54.4 %collective-permute-start.63 = (bf16[192,1536]{1,0:T(8,128)(2,1)}, bf16[192,1536]{1,0:T(8,128)(2,1)}, u32[]{:S(2)}, u32[]{:S(2)}) collective-permute-start(bf16[192,1536]{1,0:T(8,128)(2,1)} %pad_maximum_fusion.19), channel_id=1, source_target_pairs={{0,16},{8,24},{16,0},{24,8},{1,17},{9,25},{17,1},{25,9},{2,18},{10... | collective-permute-start | bytes 1769480 | tf_op jit(solution)/shard_map/ppermute | solution.py:55
  422.5 61.0 %collective-permute-start.47 = (bf16[4,96,1536]{2,1,0:T(8,128)(2,1)}, bf16[4,96,1536]{2,1,0:T(8,128)(2,1)}, u32[]{:S(2)}, u32[]{:S(2)}) collective-permute-start(bf16[4,96,1536]{2,1,0:T(8,128)(2,1)} %dynamic-slice_bitcast_fusion.3), channel_id=1, source_target_pairs={{0,1},{1,0},{2,3},{3,2},{4,5},{5,4},{6,7},{7,6},{8,9},{9,8},{10,11... | collective-permute-start | bytes 3538952 | tf_op jit(solution)/shard_map/ppermute | solution.py:68
  454.6 24.6 %collective-permute-start.43 = (bf16[96,1536]{1,0:T(8,128)(2,1)S(1)}, bf16[96,1536]{1,0:T(8,128)(2,1)S(1)}, u32[]{:S(2)}, u32[]{:S(2)}) collective-permute-start(bf16[96,1536]{1,0:T(8,128)(2,1)S(1)} %get-tuple-element.142), channel_id=1, source_target_pairs={{0,4},{1,5},{2,6},{3,7},{4,0},{5,1},{6,2},{7,3},{8,12},{9,13},{10,... | collective-permute-start | bytes 884744 | tf_op jit(solution)/shard_map/ppermute | solution.py:74
  456.2 26.5 %collective-permute-start.44 = (bf16[96,1536]{1,0:T(8,128)(2,1)S(1)}, bf16[96,1536]{1,0:T(8,128)(2,1)S(1)}, u32[]{:S(2)}, u32[]{:S(2)}) collective-permute-start(bf16[96,1536]{1,0:T(8,128)(2,1)S(1)} %get-tuple-element.141), channel_id=1, source_target_pairs={{0,6},{1,7},{2,0},{3,1},{4,2},{5,3},{6,4},{7,5},{8,14},{9,15},{10,... | collective-permute-start | bytes 884744 | tf_op jit(solution)/shard_map/ppermute | solution.py:74
  457.6 30.2 %collective-permute-start.64 = (bf16[288,1536]{1,0:T(8,128)(2,1)S(1)}, bf16[288,1536]{1,0:T(8,128)(2,1)S(1)}, u32[]{:S(2)}, u32[]{:S(2)}) collective-permute-start(bf16[288,1536]{1,0:T(8,128)(2,1)S(1)} %pad_maximum_fusion.13), channel_id=1, source_target_pairs={{0,8},{8,0},{16,24},{24,16},{1,9},{9,1},{17,25},{25,17},{2,10},{10... | collective-permute-start | bytes 2654216 | tf_op jit(solution)/shard_map/ppermute | solution.py:50
  486.1 25.5 %collective-permute-start.49 = (bf16[96,1536]{1,0:T(8,128)(2,1)}, bf16[96,1536]{1,0:T(8,128)(2,1)}, u32[]{:S(2)}, u32[]{:S(2)}) collective-permute-start(bf16[96,1536]{1,0:T(8,128)(2,1)} %get-tuple-element.145), channel_id=1, source_target_pairs={{0,4},{1,5},{2,6},{3,7},{4,0},{5,1},{6,2},{7,3},{8,12},{9,13},{10,... | collective-permute-start | bytes 884744 | tf_op jit(solution)/shard_map/ppermute | solution.py:74
  486.1 26.5 %collective-permute-start.50 = (bf16[96,1536]{1,0:T(8,128)(2,1)}, bf16[96,1536]{1,0:T(8,128)(2,1)}, u32[]{:S(2)}, u32[]{:S(2)}) collective-permute-start(bf16[96,1536]{1,0:T(8,128)(2,1)} %get-tuple-element.144), channel_id=1, source_target_pairs={{0,6},{1,7},{2,0},{3,1},{4,2},{5,3},{6,4},{7,5},{8,14},{9,15},{10,... | collective-permute-start | bytes 884744 | tf_op jit(solution)/shard_map/ppermute | solution.py:74
  515.0 14.7 %collective-permute-start.51 = (bf16[192,1536]{1,0:T(8,128)(2,1)}, bf16[192,1536]{1,0:T(8,128)(2,1)}, u32[]{:S(2)}, u32[]{:S(2)}) collective-permute-start(bf16[192,1536]{1,0:T(8,128)(2,1)} %pad_maximum_fusion.18), channel_id=1, source_target_pairs={{0,16},{8,24},{16,0},{24,8},{1,17},{9,25},{17,1},{25,9},{2,18},{10... | collective-permute-start | bytes 1769480 | tf_op jit(solution)/shard_map/ppermute | solution.py:55
  533.8 14.8 %collective-permute-start.52 = (bf16[288,1536]{1,0:T(8,128)(2,1)}, bf16[288,1536]{1,0:T(8,128)(2,1)}, u32[]{:S(2)}, u32[]{:S(2)}) collective-permute-start(bf16[288,1536]{1,0:T(8,128)(2,1)} %pad_maximum_fusion.12), channel_id=1, source_target_pairs={{0,8},{8,0},{16,24},{24,16},{1,9},{9,1},{17,25},{25,17},{2,10},{10... | collective-permute-start | bytes 2654216 | tf_op jit(solution)/shard_map/ppermute | solution.py:50
  (194 other events, 1836.3 us)

commit v3 on v2

v3 whole, which is shorter than its diff:
```python
import math

import jax
import jax.numpy as jnp
from jax import lax
from jax.experimental import pallas as pl
from jax.experimental.pallas import tpu as pltpu
from jax.sharding import PartitionSpec as P

HEAD_DIM = 64
LAYERS = 2
epsilon = 1e-05
BF = jnp.bfloat16
F32 = jnp.float32
VMEM_BYTES = 48 * 1024 * 1024

VECTORS = (
    "first_scale",
    "first_shift",
    "query_bias",
    "value_bias",
    "output_bias",
    "second_scale",
    "second_shift",
    "down_bias",
)
LINE_STEPS = (1, 2)


def lasting(microseconds):
    return pl.CostEstimate(
        flops=int(microseconds * 1.15e9),
        bytes_accessed=int(microseconds * 3.69e6),
        transcendentals=0,
    )


def matmul(left, right):
    return jnp.dot(left, right, preferred_element_type=F32)


def left_product(left, right):
    return lax.dot_general(left, right, (((0,), (0,)), ((), ())), preferred_element_type=F32)


def right_product(left, right):
    return lax.dot_general(left, right, (((1,), (1,)), ((), ())), preferred_element_type=F32)


def column_sums(values):
    return jnp.sum(values, axis=0, dtype=F32)


def swap_core(values):
    pairs = [(i, i ^ 1) for i in range(lax.axis_size("seq"))]
    return lax.ppermute(values, "seq", pairs)


def swap_row(values):
    pairs = [(i, i ^ 2) for i in range(lax.axis_size("seq"))]
    return lax.ppermute(values, "seq", pairs)


def by_core(core, mine, theirs, axis):
    return jnp.where(
        core == 0,
        jnp.concatenate([mine, theirs], axis),
        jnp.concatenate([theirs, mine], axis),
    )


def swap_pair(values):
    pairs = [(i, i ^ 1) for i in range(lax.axis_size("wt"))]
    return lax.ppermute(values, "wt", pairs)


def picked(values, index, axis):
    return lax.dynamic_index_in_dim(values, index, axis, keepdims=False)


def after(values, earlier):
    return lax.optimization_barrier((values, earlier))[0]


def swap_line(values, step):
    pairs = [(i, i ^ (2 * step)) for i in range(lax.axis_size("wt"))]
    return lax.ppermute(values, "wt", pairs)


def doubled(values, step):
    return jnp.concatenate([values, swap_line(values, step)], 0)


def place_kernel(fill, where_ref, *refs):
    fill(where_ref, *refs)


def place(fill, where, sources, spots, name):
    depth = sources[0][0].shape[0]
    rows = sources[0][0].shape[1]
    size = sum(math.prod(spot) for spot in spots) * depth

    def spot_index(spot):
        blank = (0,) * len(spot)
        return lambda k, w: (jnp.bitwise_xor(w[0], k),) + blank

    return pl.pallas_call(
        lambda *refs: place_kernel(fill, *refs),
        grid_spec=pltpu.PrefetchScalarGridSpec(
            num_scalar_prefetch=1,
            grid=(depth,),
            in_specs=[
                pl.BlockSpec((1, rows, width), lambda k, w, block=block: (k, 0, block))
                for _, width, block in sources
            ],
            out_specs=[pl.BlockSpec((1,) + spot, spot_index(spot)) for spot in spots],
        ),
        out_shape=[jax.ShapeDtypeStruct((depth,) + spot, BF) for spot in spots],
        compiler_params=pltpu.CompilerParams(vmem_limit_bytes=VMEM_BYTES),
        cost_estimate=lasting(3.0),
        name=name,
    )(where, *(array for array, _, _ in sources))


def piece_spots(where_ref, count):
    spots = [(0, where_ref[1]), (0, 1 - where_ref[1])]
    if count == 2:
        return spots
    return [spot + (where_ref[2],) for spot in spots] + [
        spot + (1 - where_ref[2],) for spot in spots
    ]


def fill_in(where_ref, *refs):
    sources, target = refs[:-1], refs[-1]
    for spot, source in zip(piece_spots(where_ref, len(sources)), sources):
        target[spot] = source[0]


def fill_out(where_ref, *refs):
    sources, target = refs[:-1], refs[-1]
    count = len(sources) // 2
    width = sources[0].shape[-1]
    here = pl.ds(pl.multiple_of(where_ref[3] * width, 128), width)
    there = pl.ds(pl.multiple_of((1 - where_ref[3]) * width, 128), width)
    for columns, group in ((here, sources[:count]), (there, sources[count:])):
        for spot, source in zip(piece_spots(where_ref, count), group):
            target[spot + (slice(None), columns)] = source[0]


def fill_wide(where_ref, near_ref, far_ref, near_there_ref, far_there_ref, up, down):
    rows = near_ref.shape[1] // 2
    features = down.shape[-1]
    for source, across, over in (
        (near_ref, where_ref[1], where_ref[2]),
        (far_ref, 1 - where_ref[1], where_ref[2]),
        (near_there_ref, where_ref[1], 1 - where_ref[2]),
        (far_there_ref, 1 - where_ref[1], 1 - where_ref[2]),
    ):
        up[0, across, over] = source[0, :rows]
        down[0, across, over, 0] = source[0, rows:, :features]
        down[0, across, over, 1] = source[0, rows:, features:]


class Reducer:
    def __init__(self):
        self.arrived = None
        self.stages = [None, None, None]
        self.totals = []

    def tick(self, values=None, gate=None, beside=None):
        owners = lax.axis_size("wt")
        if owners != 8:
            if values is not None:
                self.totals.append(
                    [
                        lax.psum_scatter(v, "wt", scatter_dimension=0, tiled=False).astype(F32)
                        for v in values
                    ]
                )
            return None if beside is None else swap_row(beside)
        own = lax.axis_index("wt")
        bits = (own % 2, own // 4, own // 2 % 2)
        moves = (swap_pair, lambda v: swap_line(v, 2), lambda v: swap_line(v, 1))
        axes = (1, 0, 0)
        if values is not None:
            self.stages[0] = [v.reshape((owners // 2, 2) + v.shape[1:]) for v in values]
        active = [i for i in range(3) if self.stages[i] is not None]
        sends = [[picked(v, 1 - bits[i], axes[i]) for v in self.stages[i]] for i in active]
        earlier = [v for v in (self.arrived, gate) if v is not None]
        if earlier:
            sends, beside = after((sends, beside), earlier)
        theirs = [[moves[i](v) for v in send] for i, send in zip(active, sends)]
        swapped = None if beside is None else swap_row(beside)
        self.arrived = (theirs, swapped)
        following = [None, None, None]
        for i, there in zip(active, theirs):
            kept = [picked(v, bits[i], axes[i]) for v in self.stages[i]]
            total = [k.astype(F32) + t.astype(F32) for k, t in zip(kept, there)]
            if i == 2:
                self.totals.append(total)
                continue
            total = [v.astype(k.dtype) for v, k in zip(total, kept)]
            if i == 0:
                total = [v.reshape((2, 2) + v.shape[1:]) for v in total]
            following[i + 1] = total
        self.stages = following
        return swapped

    def finish(self):
        while any(stage is not None for stage in self.stages):
            self.tick()


def attend_kernel(q_ref, k_ref, v_ref, o_ref):
    factor = 1.0 / math.sqrt(HEAD_DIM)
    for head in range(q_ref.shape[1] // HEAD_DIM):
        part = slice(head * HEAD_DIM, (head + 1) * HEAD_DIM)
        scores = right_product(q_ref[:, part], k_ref[:, part]) * factor
        raised = jnp.exp(scores - jnp.max(scores, axis=1, keepdims=True))
        chances = raised * (1.0 / jnp.sum(raised, axis=1, keepdims=True))
        o_ref[:, part] = matmul(chances.astype(BF), v_ref[:, part]).astype(BF)


def attend(qkv):
    rows, width = qkv.shape
    width //= 3
    block = 2 * HEAD_DIM
    steps = width // block
    return pl.pallas_call(
        attend_kernel,
        grid=(steps,),
        in_specs=[
            pl.BlockSpec((rows, block), lambda i: (0, i)),
            pl.BlockSpec((rows, block), lambda i: (0, steps + i)),
            pl.BlockSpec((rows, block), lambda i: (0, 2 * steps + i)),
        ],
        out_specs=pl.BlockSpec((rows, block), lambda i: (0, i)),
        out_shape=jax.ShapeDtypeStruct((rows, width), BF),
        compiler_params=pltpu.CompilerParams(vmem_limit_bytes=VMEM_BYTES),
        cost_estimate=lasting(6.0),
        name="attend",
    )(qkv, qkv, qkv)


def attend_back_kernel(q_ref, k_ref, v_ref, eo_ref, eq_ref, ek_ref, ev_ref):
    factor = 1.0 / math.sqrt(HEAD_DIM)
    for head in range(q_ref.shape[1] // HEAD_DIM):
        part = slice(head * HEAD_DIM, (head + 1) * HEAD_DIM)
        queries, keys, eo = q_ref[:, part], k_ref[:, part], eo_ref[:, part]
        scores = right_product(keys, queries) * factor
        raised = jnp.exp(scores - jnp.max(scores, axis=0, keepdims=True))
        chances = raised * (1.0 / jnp.sum(raised, axis=0, keepdims=True))
        ep = right_product(v_ref[:, part], eo)
        ev_ref[:, part] = matmul(chances.astype(BF), eo).astype(BF)
        inner = jnp.sum(ep * chances, axis=0, keepdims=True)
        es = (chances * (ep - inner)).astype(BF)
        ek_ref[:, part] = (matmul(es, queries) * factor).astype(BF)
        eq_ref[:, part] = (left_product(keys, es) * factor).T.astype(BF)


def attend_back(qkv, eo):
    rows, width = eo.shape
    block = 2 * HEAD_DIM
    steps = width // block
    return pl.pallas_call(
        attend_back_kernel,
        grid=(steps,),
        in_specs=[
            pl.BlockSpec((rows, block), lambda i: (0, i)),
            pl.BlockSpec((rows, block), lambda i: (0, steps + i)),
            pl.BlockSpec((rows, block), lambda i: (0, 2 * steps + i)),
            pl.BlockSpec((rows, block), lambda i: (0, i)),
        ],
        out_specs=[pl.BlockSpec((rows, block), lambda i: (0, i))] * 3,
        out_shape=[jax.ShapeDtypeStruct((rows, width), BF)] * 3,
        compiler_params=pltpu.CompilerParams(vmem_limit_bytes=VMEM_BYTES),
        cost_estimate=lasting(8.2),
        name="attend_back",
    )(qkv, qkv, qkv, eo)


def norm_parts(values):
    centred = values - jnp.mean(values, axis=-1, keepdims=True)
    spread = jnp.mean(centred * centred, axis=-1, keepdims=True)
    rate = lax.rsqrt(spread + epsilon)
    return centred * rate, rate


def pack_kernel(where_ref, *refs):
    *squares, up_ref, down_ref, branch_ref, wide_ref = refs
    side, core = where_ref[2], where_ref[3]
    shard, features = squares[0].shape[1:]
    half, part = features // 2, shard // 2
    unit_half = down_ref.shape[1] // 2
    columns = pl.ds(pl.multiple_of(core * half, 128), half)
    for position, square in enumerate(squares):
        branch_ref[:, position * half : (position + 1) * half] = square[0, :, columns]
    rows = up_ref[0, pl.ds(pl.multiple_of(side * part, 16), part), :]
    chosen = []
    for owner in range(up_ref.shape[2] // (2 * unit_half)):
        first = 2 * owner * unit_half
        low = rows[:, first : first + unit_half]
        high = rows[:, first + unit_half : first + 2 * unit_half]
        chosen.append(jnp.where(core == 0, low, high))
    wide_ref[:part, :] = jnp.concatenate(chosen, 1)
    for pair in range(2):
        first = pl.multiple_of(core * unit_half + side * shard, 16) + pair * part
        wide_ref[part:, pair * features : (pair + 1) * features] = down_ref[
            0, pl.ds(first, part), :
        ]


def pack(where, squares, up, down, layer):
    members = (*squares, up, down)
    shard, features = squares[0].shape[1:]
    shape = (shard, 2 * features)
    return pl.pallas_call(
        pack_kernel,
        grid=(1,),
        in_specs=[pl.BlockSpec(memory_space=pltpu.SMEM)]
        + [pl.BlockSpec((1,) + v.shape[1:], lambda i: (layer, 0, 0)) for v in members],
        out_specs=[pl.BlockSpec(shape, lambda i: (0, 0))] * 2,
        out_shape=[jax.ShapeDtypeStruct(shape, BF)] * 2,
        compiler_params=pltpu.CompilerParams(vmem_limit_bytes=VMEM_BYTES),
        cost_estimate=lasting(3.0),
        name="pack",
    )(where, *members)


def norm_next_kernel(base_ref, partial_ref, *refs):
    *theirs, bias_ref, scale_ref, shift_ref, value_ref, normed_ref = refs
    value = base_ref[...] + partial_ref[...] + bias_ref[...]
    for there in theirs:
        value = value + there[...].astype(F32)
    value_ref[...] = value
    flat, _ = norm_parts(value)
    normed_ref[...] = (flat * scale_ref[...] + shift_ref[...]).astype(BF)


def norm_next(base, parts, bias, scale, shift):
    rows, features = base.shape
    block = pl.BlockSpec((rows // 4, features), lambda i: (i, 0))
    line = pl.BlockSpec((1, features), lambda i: (0, 0))
    return pl.pallas_call(
        norm_next_kernel,
        grid=(4,),
        in_specs=[block] * (1 + len(parts)) + [line] * 3,
        out_specs=[block] * 2,
        out_shape=[
            jax.ShapeDtypeStruct((rows, features), F32),
            jax.ShapeDtypeStruct((rows, features), BF),
        ],
        compiler_params=pltpu.CompilerParams(vmem_limit_bytes=VMEM_BYTES),
        cost_estimate=lasting(2.9),
        name="norm_next",
    )(base, *parts, *(v.reshape(1, features) for v in (bias, scale, shift)))


def norm_back_kernel(offset_ref, partial_ref, there_ref, value_ref, scale_ref, base_ref, *outs):
    out_ref, low_ref, sums_ref = outs

    @pl.when(pl.program_id(0) == 0)
    def _():
        sums_ref[...] = jnp.zeros_like(sums_ref)

    grad = partial_ref[...] + there_ref[...].astype(F32)
    flat, rate = norm_parts(value_ref[...])
    inner = grad * scale_ref[...]
    mean_inner = jnp.mean(inner, axis=-1, keepdims=True)
    mean_cross = jnp.mean(inner * flat, axis=-1, keepdims=True)
    total = base_ref[...] + rate * (inner - mean_inner - flat * mean_cross)
    out_ref[...] = total
    low = total.astype(BF)
    low_ref[...] = low
    sums_ref[0:1] += jnp.sum(grad * flat, axis=0, keepdims=True)
    sums_ref[1:2] += jnp.sum(grad, axis=0, keepdims=True)
    sums_ref[2:3] += jnp.sum(low.astype(F32), axis=0, keepdims=True)


def norm_back(partial, there, value, scale, base, offset):
    rows, features = there.shape
    block = rows // 4
    steps = rows // block
    moved = pl.BlockSpec((block, features), lambda i, w: (w[0] * steps + i, 0))
    plain = pl.BlockSpec((block, features), lambda i, w: (i, 0))
    return pl.pallas_call(
        norm_back_kernel,
        grid_spec=pltpu.PrefetchScalarGridSpec(
            num_scalar_prefetch=1,
            grid=(steps,),
            in_specs=[
                moved,
                plain,
                moved,
                pl.BlockSpec((1, features), lambda i, w: (0, 0)),
                moved,
            ],
            out_specs=[plain, plain, pl.BlockSpec((8, features), lambda i, w: (0, 0))],
        ),
        out_shape=[
            jax.ShapeDtypeStruct((rows, features), F32),
            jax.ShapeDtypeStruct((rows, features), BF),
            jax.ShapeDtypeStruct((8, features), F32),
        ],
        compiler_params=pltpu.CompilerParams(vmem_limit_bytes=VMEM_BYTES),
        cost_estimate=lasting(3.8),
        name="norm_back",
    )(offset, partial, there, value, scale.reshape(1, features), base)


def gelu_parts(values):
    below = 0.5 * (1.0 + lax.erf(values * math.sqrt(0.5)))
    density = jnp.exp(-0.5 * values * values) * (1.0 / math.sqrt(2.0 * math.pi))
    return values * below, below + values * density


def settle_kernel(core_ref, mine_ref, mine_wide_ref, other_ref, other_wide_ref, *refs):
    *squares, up, down = refs[-6:]
    core = core_ref[0]
    shard, features = squares[0].shape[1:]
    half = features // 2
    unit_half = down.shape[1] // 2
    owners = up.shape[2] // (2 * unit_half)
    here = pl.ds(pl.multiple_of(core * half, 128), half)
    there = pl.ds(pl.multiple_of((1 - core) * half, 128), half)
    for position, target in enumerate(squares):
        columns = slice(position * half, (position + 1) * half)
        target[0, :, here] = mine_ref[:, columns].astype(F32)
        target[0, :, there] = other_ref[:, columns].astype(F32)
    mine, other = mine_wide_ref[:shard].astype(F32), other_wide_ref[:shard].astype(F32)
    low = jnp.where(core == 0, mine, other)
    high = jnp.where(core == 0, other, mine)
    for owner in range(owners):
        columns = slice(owner * unit_half, (owner + 1) * unit_half)
        up[0, :, 2 * owner * unit_half : 2 * (owner + 1) * unit_half] = jnp.concatenate(
            [low[:, columns], high[:, columns]], 1
        )
    for pair in range(2):
        columns = slice(pair * features, (pair + 1) * features)
        for source, where in ((mine_wide_ref, core), (other_wide_ref, 1 - core)):
            rows = pl.ds(pl.multiple_of(where * unit_half, 8) + pair * shard, shard)
            down[0, rows] = source[shard:, columns].astype(F32)


def settle(core, pieces, earlier, layer, shapes):
    size = sum(math.prod(shape[1:]) for shape in shapes)
    return pl.pallas_call(
        settle_kernel,
        grid=(1,),
        in_specs=[pl.BlockSpec(memory_space=pltpu.SMEM)]
        + [pl.BlockSpec(piece.shape, lambda i: (0, 0)) for piece in pieces]
        + [pl.BlockSpec(memory_space=pl.ANY)] * len(earlier),
        out_specs=[
            pl.BlockSpec((1,) + shape[1:], lambda i: (layer, 0, 0)) for shape in shapes
        ],
        out_shape=[jax.ShapeDtypeStruct(shape, F32) for shape in shapes],
        input_output_aliases={1 + len(pieces) + i: i for i in range(len(earlier))},
        compiler_params=pltpu.CompilerParams(vmem_limit_bytes=VMEM_BYTES),
        cost_estimate=lasting(2.0),
        name="settle",
    )(core, *pieces, *earlier)


def per_device(
    activations,
    upstream,
    first_scale,
    first_shift,
    query_weight,
    query_bias,
    key_weight,
    value_weight,
    value_bias,
    output_weight,
    output_bias,
    second_scale,
    second_shift,
    up_weight,
    up_bias,
    down_weight,
    down_bias,
):
    owners = lax.axis_size("wt")
    seat = lax.axis_index("seq")
    core, side = seat % 2, seat // 2
    frames_here, features = activations.shape[1:]
    half = features // 2
    shard = features // owners
    units = up_weight.shape[2]
    unit_shard = units // owners
    unit_half = unit_shard // 2

    def to_chip(values):
        kept = lax.dynamic_index_in_dim(values, side, 0, keepdims=False)
        sent = lax.dynamic_index_in_dim(values, 1 - side, 0, keepdims=False)
        mine = jnp.concatenate([kept, swap_row(sent)], 0)
        return by_core(core, mine, swap_core(mine), 0)

    def from_chip(mine):
        kept, sent = mine[:frames_here], mine[frames_here:]
        other = swap_row(sent)
        return jnp.where(side == 0, jnp.stack([kept, other]), jnp.stack([other, kept]))

    def own_rows(values):
        return lax.dynamic_slice_in_dim(values, core * 2 * frames_here, 2 * frames_here, 0)

    def half_columns(values):
        return lax.dynamic_slice_in_dim(values, core * half, half, 1)

    direct = owners == 8
    own = lax.axis_index("wt")
    line, across = own // 2, own % 2
    where = jnp.stack([line, across, side, core]).astype(jnp.int32)

    down_in = to_chip(upstream)
    shards = {}
    for layer in range(LAYERS):
        shards["branch", layer] = jnp.concatenate(
            [
                half_columns(query_weight[layer]),
                half_columns(key_weight[layer]),
                half_columns(value_weight[layer]),
                half_columns(output_weight[layer]),
            ],
            1,
        )
    for layer in range(LAYERS):
        shards["up", layer] = picked(
            up_weight[layer].reshape(shard, owners, 2, unit_half), core, 2
        ).reshape(shard, units // 2)
        shards["down", layer] = lax.dynamic_slice_in_dim(
            down_weight[layer], core * unit_half, unit_half, 0
        )
    members = dict(
        first_scale=first_scale,
        first_shift=first_shift,
        query_bias=query_bias,
        value_bias=value_bias,
        output_bias=output_bias,
        second_scale=second_scale,
        second_shift=second_shift,
        down_bias=down_bias,
    )
    narrow = len(VECTORS) * shard
    packed = jnp.concatenate([members[name] for name in VECTORS] + [up_bias], 1)
    gathered = {}
    if direct:

        squares = (query_weight, key_weight, value_weight, output_weight)
        branch_piece, wide_piece = zip(
            *(pack(where, squares, up_weight, down_weight, layer) for layer in range(LAYERS))
        )

        wide_hop = doubled(wide_piece[0][None], 1)
        hop = doubled(after(branch_piece[0], wide_hop)[None], 1)
        wide = [doubled(wide_hop, 2), None]
        packed = after(packed, wide[0])
        wide_near, hop, piece = after(
            (wide[0], hop, wide_piece[1][None]), (wide[0], down_in)
        )
        wide_far = [swap_pair(wide_near), None]
        wide_there = [swap_row(wide_near), None]
        branch = [doubled(hop, 2), None]
        wide_hop = doubled(piece, 1)
        near, far, hop, piece = after(
            (branch[0], wide_far[0], wide_hop, branch_piece[1]),
            (wide_far[0], wide_there[0], branch[0]),
        )
        branch_far = [swap_pair(near), None]
        wide_far_there = [swap_row(far), None]
        wide[1] = doubled(hop, 2)
        hop = doubled(piece[None], 1)
        near, hop = after((wide[1], hop), (branch_far[0], wide_far_there[0], wide[1]))
        wide_far[1] = swap_pair(near)
        wide_there[1] = swap_row(near)
        branch[1] = doubled(hop, 2)
        third = (wide_far[1], wide_there[1], branch[1])
        near, far = after((branch[1], wide_far[1]), third)
        branch_far[1], wide_far_there[1] = lax.optimization_barrier(
            (swap_pair(near), swap_row(far))
        )

        for layer in range(LAYERS):
            pieces = (branch[layer], branch_far[layer])
            (gathered["in", layer],) = place(
                fill_in,
                where,
                tuple((v, 3 * half, 0) for v in pieces),
                ((2, shard, 3 * half),),
                "place_in",
            )
            gathered["in", layer] = gathered["in", layer].reshape(features, 3 * half)
            swapped = swap_core(jnp.concatenate([v[:, :, 3 * half :] for v in pieces], 2))
            (gathered["out", layer],) = place(
                fill_out,
                where,
                tuple((v, half, 3) for v in pieces) + ((swapped, half, 0), (swapped, half, 1)),
                ((2, shard, features),),
                "place_out",
            )
            gathered["out", layer] = gathered["out", layer].reshape(features, features)
            width = 2 * features
            pieces = (wide[layer], wide_far[layer], wide_there[layer], wide_far_there[layer])
            gathered["up", layer], gathered["down", layer] = place(
                fill_wide,
                where,
                tuple((v, width, 0) for v in pieces),
                ((2, 2, shard // 2, width), (2, 2, 2, shard // 2, features)),
                "place_wide",
            )
            gathered["up", layer] = gathered["up", layer].reshape(features, units // 2)
            gathered["down", layer] = gathered["down", layer].reshape(units // 2, features)
    else:
        for layer in range(LAYERS):
            for kind in ("up", "down"):
                gathered[kind, layer] = lax.all_gather(
                    shards[kind, layer], "wt", axis=0, tiled=True
                )
            branch = lax.all_gather(shards["branch", layer], "wt", axis=0, tiled=True)
            gathered["in", layer] = branch[:, : 3 * half]
            out_half = branch[:, 3 * half :]
            gathered["out", layer] = by_core(core, out_half, swap_core(out_half), 1)
    if direct:
        reached = packed[None]
        for step in LINE_STEPS:
            reached = doubled(reached, step)
        other = swap_pair(reached)
        spread = jnp.stack([reached, other], 1)
        for bit in LINE_STEPS:
            turned = spread.reshape((owners // (4 * bit), 2, bit, 2) + packed.shape)
            spread = jnp.where((line & bit) == 0, turned, turned[:, ::-1]).reshape(spread.shape)
        spread = jnp.where(across == 0, spread, spread[:, ::-1]).reshape(
            (owners,) + packed.shape
        )
    else:
        spread = lax.all_gather(packed, "wt", axis=0, tiled=False)
    vector_rows = (
        spread[:, :, :narrow]
        .reshape(owners, LAYERS * len(VECTORS), shard)
        .swapaxes(0, 1)
        .reshape(LAYERS * len(VECTORS), features)
        .astype(F32)
    )
    vectors = [
        {
            name: vector_rows[layer * len(VECTORS) + position]
            for position, name in enumerate(VECTORS)
        }
        for layer in range(LAYERS)
    ]
    unit_rows = (
        picked(spread[:, :, narrow:].reshape(owners, LAYERS, 2, unit_half), core, 2)
        .swapaxes(0, 1)
        .reshape(LAYERS, units // 2)
        .astype(F32)
    )

    weights = [
        tuple(gathered[kind, layer] for kind in ("in", "out", "up", "down"))
        for layer in range(LAYERS)
    ]

    hidden = to_chip(activations).astype(F32)
    kept = []
    for layer in range(LAYERS):
        vec = vectors[layer]
        in_weight, out_weight, up, down = weights[layer]
        if layer == 0:
            flat, _ = norm_parts(hidden)
            normed = (flat * vec["first_scale"] + vec["first_shift"]).astype(BF)
        in_bias = jnp.concatenate(
            [
                lax.dynamic_slice_in_dim(vec["query_bias"], core * half, half, 0),
                jnp.zeros((half,), F32),
                lax.dynamic_slice_in_dim(vec["value_bias"], core * half, half, 0),
            ]
        )
        qkv = (matmul(normed, in_weight) + in_bias).astype(BF)
        mixture_half = attend(qkv)
        mixture = by_core(core, mixture_half, swap_core(mixture_half), 1)
        middle, second = norm_next(
            hidden,
            (matmul(mixture, out_weight),),
            vec["output_bias"],
            vec["second_scale"],
            vec["second_shift"],
        )
        upward = matmul(second, up) + unit_rows[layer]
        activated, slope = gelu_parts(upward)
        activated = activated.astype(BF)
        if direct and layer == 0:
            activated = after(activated, third)
        slope = slope.astype(BF)
        kept.append((hidden, normed, qkv, mixture, middle, second, activated, slope))
        partial = matmul(activated, down)
        if layer + 1 < LAYERS:
            hidden, normed = norm_next(
                middle,
                (partial, swap_core(partial.astype(BF))),
                vec["down_bias"],
                vectors[layer + 1]["first_scale"],
                vectors[layer + 1]["first_shift"],
            )
        else:
            theirs = lax.dynamic_slice_in_dim(
                partial, (1 - core) * 2 * frames_here, 2 * frames_here, 0
            )
            total = own_rows(partial) + swap_core(theirs.astype(BF))
            result_rows = (own_rows(middle) + vec["down_bias"] + total).astype(BF)

    grad_hidden = down_in.astype(F32)
    grad_down_bias = column_sums(down_in)[None]
    vector_grads = [None] * LAYERS
    settled = ()
    reducer = Reducer()
    row_core = core.reshape(1).astype(jnp.int32)
    no_offset = jnp.zeros((1,), jnp.int32)
    matrix_shapes = tuple(
        (LAYERS,) + shape
        for shape in ((shard, features),) * 4 + ((shard, units), (unit_shard, features))
    )
    for layer in reversed(range(LAYERS)):
        vec = vectors[layer]
        in_weight, out_weight, up, down = weights[layer]
        hidden, normed, qkv, mixture, middle, second, activated, slope = kept[layer]
        grad_down = left_product(activated, down_in).astype(BF)
        grad_upward = (slope.astype(F32) * right_product(down_in, down)).astype(BF)
        grad_up = left_product(second, grad_upward).astype(BF)
        if layer > 0:
            grad_up = grad_up.reshape(owners, shard, units // 2)
            reducer.tick([grad_down.reshape(owners, unit_half, features)])
        else:
            grad_up = grad_up.reshape(owners, 2, shard // 2, units // 2)
            grad_down = grad_down.reshape(owners, 2, 2, shard // 2, features)
            grad_down = jnp.concatenate([grad_down[:, :, 0], grad_down[:, :, 1]], -1)
            down_there = reducer.tick([grad_branch], beside=picked(grad_down, 1 - side, 1))
        grad_up_bias = column_sums(grad_upward)
        partial = right_product(grad_upward, up)
        there = swap_core(partial.astype(BF))
        grad_middle, branch_in, second_sums = norm_back(
            partial, there, middle, vec["second_scale"], grad_hidden, no_offset
        )
        grad_out = left_product(mixture, half_columns(branch_in))
        out_rows = lax.dynamic_slice_in_dim(out_weight, core * half, half, 0)
        grad_mixture = right_product(branch_in, out_rows).astype(BF)
        grad_qkv = jnp.concatenate(attend_back(qkv, grad_mixture), 1)
        grad_in = left_product(normed, grad_qkv).astype(BF)
        grad_branch = jnp.concatenate([grad_in, grad_out.astype(BF)], 1)
        grad_branch = grad_branch.reshape(owners, shard, 2 * features)
        if layer > 0:
            reducer.tick([grad_up], grad_branch)
        else:
            up_there = reducer.tick([grad_branch], beside=picked(grad_up, 1 - side, 1))
            grad_wide = jnp.concatenate(
                [
                    (picked(grad_up, side, 1).astype(F32) + up_there.astype(F32)).astype(BF),
                    (picked(grad_down, side, 1).astype(F32) + down_there.astype(F32)).astype(BF),
                ],
                1,
            )
        grad_in_bias = column_sums(grad_qkv)
        partial = right_product(grad_qkv, in_weight)
        below = grad_down_bias
        if layer > 0:
            there = swap_core(partial.astype(BF))
            grad_hidden, down_in, first_sums = norm_back(
                partial, there, hidden, vec["first_scale"], grad_middle, no_offset
            )
            grad_down_bias = first_sums[2:3]
        else:
            result_rows = after(result_rows, grad_qkv)
            result = from_chip(result_rows)
            theirs = lax.dynamic_slice_in_dim(
                partial, (1 - core) * 2 * frames_here, 2 * frames_here, 0
            )
            there = swap_core(theirs.astype(BF))
            before, _, first_sums = norm_back(
                partial, there, hidden, vec["first_scale"], grad_middle, row_core
            )
            input_grad = from_chip(before)

        twice = jnp.stack([grad_in_bias[:half], grad_in_bias[2 * half :]])
        rows = jnp.concatenate(
            [
                first_sums[:2],
                jnp.concatenate([twice, twice], 1),
                second_sums[2:3],
                second_sums[:2],
                below,
            ],
            0,
        )
        place_row = lax.broadcasted_iota(jnp.int32, rows.shape, 0)
        on_right = lax.broadcasted_iota(jnp.int32, rows.shape, 1) >= half
        counted = jnp.where((place_row == 2) | (place_row == 3), on_right == (core == 1), core == 0)
        if layer == 0:
            counted = counted | (place_row < 2)
        vector_grads[layer] = (jnp.where(counted, rows, 0.0), grad_up_bias)

    packed = jnp.stack([rows for rows, _ in vector_grads])
    packed = packed.reshape(LAYERS * len(VECTORS), owners, shard).swapaxes(0, 1)
    packed = packed.reshape(owners, LAYERS * narrow)
    from_units = jnp.stack([values for _, values in vector_grads])
    from_units = from_units.reshape(LAYERS, owners, unit_half).swapaxes(0, 1)
    from_units = from_units.reshape(owners, LAYERS * unit_half)
    packed = jnp.concatenate([packed, from_units], 1)
    reducer.tick([grad_wide, packed])
    reducer.finish()
    for layer in reversed(range(LAYERS)):
        if layer > 0:
            (grad_down,), (grad_up,), (grad_branch,) = reducer.totals[:3]
            grad_wide = jnp.concatenate(
                [grad_up, jnp.concatenate([grad_down[:shard], grad_down[shard:]], 1)], 0
            )
        else:
            (grad_branch,), (grad_wide, packed) = reducer.totals[3:]

        def over_sides(values):
            values = values.astype(BF)
            values = (values.astype(F32) + swap_row(values).astype(F32)).astype(BF)
            return values, swap_core(values)

        if layer > 0:
            mine, other = over_sides(jnp.concatenate([grad_branch, grad_wide], 0))
            mine, other = (mine[:shard], mine[shard:]), (other[:shard], other[shard:])
        else:
            grad_wide = grad_wide.astype(BF)
            there = swap_row(grad_wide)
            low = jnp.where(side == 0, grad_wide, there)
            high = jnp.where(side == 0, there, grad_wide)
            part = shard // 2
            low_down, high_down = low[part:], high[part:]
            grad_wide = jnp.concatenate(
                [
                    low[:part],
                    high[:part],
                    jnp.concatenate([low_down[:, :features], high_down[:, :features]], 1),
                    jnp.concatenate([low_down[:, features:], high_down[:, features:]], 1),
                ],
                0,
            )
            mine, other = zip(over_sides(grad_branch), (grad_wide, swap_core(grad_wide)))
        if direct:
            settled = settle(row_core, mine + other, settled, layer, matrix_shapes)
            continue
        low = [jnp.where(core == 0, m, o).astype(F32) for m, o in zip(mine, other)]
        high = [jnp.where(core == 0, o, m).astype(F32) for m, o in zip(mine, other)]
        done = []
        for position in range(4):
            part = slice(position * half, (position + 1) * half)
            done.append(jnp.concatenate([low[0][:, part], high[0][:, part]], 1))

        def up_part(values):
            return values[:shard].reshape(shard, owners, unit_half)

        def down_part(values):
            return jnp.concatenate([values[shard:, :features], values[shard:, features:]], 0)

        done.append(jnp.stack([up_part(low[1]), up_part(high[1])], 2).reshape(shard, units))
        done.append(jnp.concatenate([down_part(low[1]), down_part(high[1])], 0))
        if not settled:
            settled = tuple(jnp.zeros(shape, F32) for shape in matrix_shapes)
        settled = tuple(total.at[layer].set(part) for total, part in zip(settled, done))

    packed = packed + swap_row(packed)
    other = swap_core(packed)
    narrow_sum = (packed + other)[: LAYERS * narrow].reshape(LAYERS, len(VECTORS), shard)
    unit_mine = packed[LAYERS * narrow :].reshape(LAYERS, unit_half)
    unit_other = other[LAYERS * narrow :].reshape(LAYERS, unit_half)
    summed = {name: narrow_sum[:, position] for position, name in enumerate(VECTORS)}
    summed["up_bias"] = by_core(core, unit_mine, unit_other, 1)

    query, key, value, output, up, down = settled
    final = (
        summed["first_scale"],
        summed["first_shift"],
        query,
        summed["query_bias"],
        key,
        value,
        summed["value_bias"],
        output,
        summed["output_bias"],
        summed["second_scale"],
        summed["second_shift"],
        up,
        summed["up_bias"],
        down,
        summed["down_bias"],
    )
    return (result, input_grad) + final


def solution(mesh):
    rows, vector, matrix = P("wt", "seq", None), P(None, "wt"), P(None, "wt", None)
    parameters = (
        vector,
        vector,
        matrix,
        vector,
        matrix,
        matrix,
        vector,
        matrix,
        vector,
        vector,
        vector,
        matrix,
        vector,
        matrix,
        vector,
    )
    specs = (rows, rows) + parameters
    return jax.shard_map(
        per_device, mesh=mesh, in_specs=specs, out_specs=specs, check_vma=False
    )
```

time: 582 us -> 482 us (0.83)
  the two profiles are of different devices: /device:TPU:15 before, /device:TPU:0 now
where the time goes in v3:
time: 482 us; the launch traced here: 475 us
  waiting for transfers between devices  208 us (43%)
  Pallas kernels  74.4 us (15%)
  local copies, waits for them, and re-layouts  63.5 us (13%)
  starting transfers between devices  49.9 us (10%)
  matrix products  40.2 us (8%)
  other arithmetic  35.8 us (7%)
    ppermute x22, waiting for transfers between devices, swap_line(): return lax.ppermute(values, 'wt', pairs)  158 us
    ppermute x14, waiting for transfers between devices, swap_row(): return lax.ppermute(values, 'seq', pairs)  34.4 us
    unnamed x222, local copies, waits for them, and re-layouts  32.2 us
    ppermute x22, starting transfers between devices, swap_line(): return lax.ppermute(values, 'wt', pairs)  23.3 us
    pallas_call x6, Pallas kernels, place(): pl.pallas_call(lambda *refs: place_kernel(fill, *refs), grid_spec=pltpu.P...  21.1 us
    pallas_call x2, Pallas kernels, attend_back(): pl.pallas_call(attend_back_kernel, grid=(steps,), in_specs=[pl.BlockSpec(...  16.4 us
    pallas_call x4, Pallas kernels, norm_back(): pl.pallas_call(norm_back_kernel, grid_spec=pltpu.PrefetchScalarGridSpec(n...  15.3 us
    ppermute x11, waiting for transfers between devices, swap_pair(): return lax.ppermute(values, 'wt', pairs)  14.7 us
  transfers between devices with their start and end apart: 63, of which 29 were waited for; matrix products, arithmetic and copies ran while one was open for 20% of the time, Pallas kernels for 14%

profile of v3, /device:TPU:0, one launch (start us, length us, event | category | flops | bytes accessed | tf_op | source)
XLA Modules:
  0.0 475.3 jit_solution(17729405154984442778)
XLA Ops:
  2.4 3.0 collective-permute-start
  17.4 3.9 collective-permute-done.8
  22.5 2.7 collective-permute-start.3
  27.4 17.3 %collective-permute-done.7 = bf16[1,96,1536]{2,1,0:T(8,128)(2,1)S(1)} collective-permute-done((bf16[1,96,1536]{2,1,0:T(8,128)(2,1)S(1)}, bf16[1,96,1536]{2,1,0:T(8,128)(2,1)S(1)}, u32[]{:S(2)}, u32[]{:S(2)}) %collective-permute-start.7) | collective-permute-done | bytes 294944 | tf_op jit(solution)/shard_map/ppermute | solution.py:87
  45.6 6.1 %collective-permute-done.3 = bf16[2,96,1536]{2,1,0:T(8,128)(2,1)S(1)} collective-permute-done((bf16[2,96,1536]{2,1,0:T(8,128)(2,1)S(1)}, bf16[2,96,1536]{2,1,0:T(8,128)(2,1)S(1)}, u32[]{:S(2)}, u32[]{:S(2)}) %collective-permute-start.3) | collective-permute-done | bytes 589856 | tf_op jit(solution)/shard_map/ppermute | solution.py:87
  53.4 3.0 collective-permute-done.4
  69.3 13.6 %collective-permute-done.12 = bf16[1,96,1536]{2,1,0:T(8,128)(2,1)} collective-permute-done((bf16[1,96,1536]{2,1,0:T(8,128)(2,1)S(1)}, bf16[1,96,1536]{2,1,0:T(8,128)(2,1)}, u32[]{:S(2)}, u32[]{:S(2)}) %collective-permute-start.12) | collective-permute-done | bytes 294944 | tf_op jit(solution)/shard_map/ppermute | solution.py:87
  84.8 6.4 %collective-permute-done.10 = bf16[2,96,1536]{2,1,0:T(8,128)(2,1)} collective-permute-done((bf16[2,96,1536]{2,1,0:T(8,128)(2,1)}, bf16[2,96,1536]{2,1,0:T(8,128)(2,1)}, u32[]{:S(2)}, u32[]{:S(2)}) %collective-permute-start.10) | collective-permute-done | bytes 589856 | tf_op jit(solution)/shard_map/ppermute | solution.py:87
  100.2 12.7 %collective-permute-done.19 = bf16[1,96,1536]{2,1,0:T(8,128)(2,1)} collective-permute-done((bf16[1,96,1536]{2,1,0:T(8,128)(2,1)S(1)}, bf16[1,96,1536]{2,1,0:T(8,128)(2,1)}, u32[]{:S(2)}, u32[]{:S(2)}) %collective-permute-start.19) | collective-permute-done | bytes 294944 | tf_op jit(solution)/shard_map/ppermute | solution.py:87
  114.0 8.4 %collective-permute-done.18 = bf16[2,96,1536]{2,1,0:T(8,128)(2,1)} collective-permute-done((bf16[2,96,1536]{2,1,0:T(8,128)(2,1)}, bf16[2,96,1536]{2,1,0:T(8,128)(2,1)}, u32[]{:S(2)}, u32[]{:S(2)}) %collective-permute-start.18) | collective-permute-done | bytes 589856 | tf_op jit(solution)/shard_map/ppermute | solution.py:87
  127.8 3.2 place_in.2
  133.8 5.7 %attend.2 = bf16[512,384]{1,0:T(8,128)(2,1)S(1)} custom-call(bf16[512,1152]{1,0:T(8,128)(2,1)S(1)} %fusion.12.q_ref.k_ref.v_ref, bf16[512,1152]{1,0:T(8,128)(2,1)S(1)} %fusion.12.q_ref.k_ref.v_ref, bf16[512,1152]{1,0:T(8,128)(2,1)S(1)} %fusion.12.q_ref.k_ref.v_ref), custom_call_target="tpu_custom_call" | custom-call | flops 6899999744 | bytes 22140000 | tf_op jit(solution)/shard_map/attend/pallas_call | solution.py:230
  140.0 5.2 %place_wide.2 = (bf16[4,2,2,48,1536]{4,3,2,1,0:T(8,128)(2,1)}, bf16[4,2,2,2,48,768]{5,4,3,2,1,0:T(8,128)(2,1)}) custom-call(s32[4]{0:T(128)S(1)} %pad_add_fusion.where_ref.refs_0_, bf16[4,96,1536]{2,1,0:T(8,128)(2,1)S(1)} %pad_maximum_fusion.3.refs_1_, bf16[4,96,1536]{2,1,0:T(8,128)(2,1)} %collective-permute-done.11.refs_2_, ...), custom_call_target="tpu_custom_call" | custom-call | flops 3449999872 | bytes 11070000 | tf_op jit(solution)/shard_map/place_wide/pallas_call | solution.py:107
  145.2 2.5 place_out.2
  147.8 19.6 %collective-permute-done.22 = bf16[2,96,1536]{2,1,0:T(8,128)(2,1)S(1)} collective-permute-done((bf16[2,96,1536]{2,1,0:T(8,128)(2,1)S(1)}, bf16[2,96,1536]{2,1,0:T(8,128)(2,1)S(1)}, u32[]{:S(2)}, u32[]{:S(2)}) %collective-permute-start.22) | collective-permute-done | bytes 589856 | tf_op jit(solution)/shard_map/ppermute | solution.py:87
  170.7 3.1 multiply_convert_fusion.1
  174.9 2.8 fusion.67
  184.6 2.9 norm_next.4
  187.6 14.3 %collective-permute-done.24.refs_2_ = bf16[4,96,1536]{2,1,0:T(8,128)(2,1)} collective-permute-done((bf16[4,96,1536]{2,1,0:T(8,128)(2,1)S(1)}, bf16[4,96,1536]{2,1,0:T(8,128)(2,1)}, u32[]{:S(2)}, u32[]{:S(2)}) %collective-permute-start.24) | collective-permute-done | bytes 1179680 | tf_op jit(solution)/shard_map/ppermute | solution.py:74
  203.3 2.7 place_in.3
  208.5 5.7 %attend.3 = bf16[512,384]{1,0:T(8,128)(2,1)S(1)} custom-call(bf16[512,1152]{1,0:T(8,128)(2,1)S(1)} %fusion.13.q_ref.k_ref.v_ref, bf16[512,1152]{1,0:T(8,128)(2,1)S(1)} %fusion.13.q_ref.k_ref.v_ref, bf16[512,1152]{1,0:T(8,128)(2,1)S(1)} %fusion.13.q_ref.k_ref.v_ref), custom_call_target="tpu_custom_call" | custom-call | flops 6899999744 | bytes 22140000 | tf_op jit(solution)/shard_map/attend/pallas_call | solution.py:230
  214.2 4.9 %place_wide.3 = (bf16[4,2,2,48,1536]{4,3,2,1,0:T(8,128)(2,1)}, bf16[4,2,2,2,48,768]{5,4,3,2,1,0:T(8,128)(2,1)}) custom-call(s32[4]{0:T(128)S(1)} %pad_add_fusion.where_ref.refs_0_, bf16[4,96,1536]{2,1,0:T(8,128)(2,1)S(1)} %copy-done.3, bf16[4,96,1536]{2,1,0:T(8,128)(2,1)} %collective-permute-done.20.refs_2_, bf16[4,96,1536]{2,1,0:T(8,128)(2,1)S(1)} %copy-done.7, ...), custom_call_target="tpu_custom_call" | custom-call | flops 3449999872 | bytes 11070000 | tf_op jit(solution)/shard_map/place_wide/pallas_call | solution.py:107
  226.4 3.0 convert_reduce_fusion
  229.4 2.9 fusion.68
  232.3 2.8 convolution_convert_fusion.2
  247.2 3.9 norm_back.4
  253.5 8.2 %attend_back.2 = (bf16[512,384]{1,0:T(8,128)(2,1)S(1)}, bf16[512,384]{1,0:T(8,128)(2,1)S(1)}, bf16[512,384]{1,0:T(8,128)(2,1)S(1)}) custom-call(bf16[512,1152]{1,0:T(8,128)(2,1)S(1)} %copy-done.33, bf16[512,1152]{1,0:T(8,128)(2,1)S(1)} %copy-done.33, bf16[512,1152]{1,0:T(8,128)(2,1)S(1)} %copy-done.33, bf16[512,384]{1,0:T(8,128)(2,1)S(1)} %convolution_convert_fusion.9.eo_ref), custom_call_target="tpu_custom_call" | custom-call | flops 9429999616 | bytes 30258000 | tf_op jit(solution)/shard_map/attend_back/pallas_call | solution.py:266
  272.8 3.7 norm_back.5
  281.9 2.8 fusion.70
  284.8 2.8 convolution_convert_fusion.5
  290.9 2.5 dynamic-slice_bitcast_fusion.1
  294.5 7.0 %collective-permute-done.37 = bf16[2,192,768]{2,1,0:T(8,128)(2,1)} collective-permute-done((bf16[2,192,768]{2,1,0:T(8,128)(2,1)S(1)}, bf16[2,192,768]{2,1,0:T(8,128)(2,1)}, u32[]{:S(2)}, u32[]{:S(2)}) %collective-permute-start.37) | collective-permute-done | bytes 589856 | tf_op jit(solution)/shard_map/ppermute | solution.py:87
  309.2 3.7 norm_back.6
  315.3 8.2 %attend_back.3 = (bf16[512,384]{1,0:T(8,128)(2,1)S(1)}, bf16[512,384]{1,0:T(8,128)(2,1)S(1)}, bf16[512,384]{1,0:T(8,128)(2,1)S(1)}) custom-call(bf16[512,1152]{1,0:T(8,128)(2,1)S(1)} %copy-done.31, bf16[512,1152]{1,0:T(8,128)(2,1)S(1)} %copy-done.31, bf16[512,1152]{1,0:T(8,128)(2,1)S(1)} %copy-done.31, bf16[512,384]{1,0:T(8,128)(2,1)S(1)} %convolution_convert_fusion.8.eo_ref), custom_call_target="tpu_custom_call" | custom-call | flops 9429999616 | bytes 30258000 | tf_op jit(solution)/shard_map/attend_back/pallas_call | solution.py:266
  332.2 5.5 %collective-permute-done.32 = bf16[128,768]{1,0:T(8,128)(2,1)S(1)} collective-permute-done((bf16[128,768]{1,0:T(8,128)(2,1)S(1)}, bf16[128,768]{1,0:T(8,128)(2,1)S(1)}, u32[]{:S(2)}, u32[]{:S(2)}) %collective-permute-start.32) | collective-permute-done | bytes 196640 | tf_op jit(solution)/shard_map/ppermute | solution.py:61
  339.5 4.0 norm_back.7
  348.4 6.5 %collective-permute-done.34 = f32[128,768]{1,0:T(8,128)S(1)} collective-permute-done((f32[128,768]{1,0:T(8,128)S(1)}, f32[128,768]{1,0:T(8,128)S(1)}, u32[]{:S(2)}, u32[]{:S(2)}) %collective-permute-start.34) | collective-permute-done | bytes 393248 | tf_op jit(solution)/shard_map/ppermute | solution.py:61
  359.4 16.6 %collective-permute-done.44 = bf16[2,96,1536]{2,1,0:T(8,128)(2,1)S(1)} collective-permute-done((bf16[2,96,1536]{2,1,0:T(8,128)(2,1)S(1)}, bf16[2,96,1536]{2,1,0:T(8,128)(2,1)S(1)}, u32[]{:S(2)}, u32[]{:S(2)}) %collective-permute-start.44) | collective-permute-done | bytes 589856 | tf_op jit(solution)/shard_map/ppermute | solution.py:87
  376.8 6.2 %collective-permute-done.42 = bf16[8,48,1536]{2,1,0:T(8,128)(2,1)S(1)} collective-permute-done((bf16[8,48,1536]{2,1,0:T(8,128)(2,1)S(1)}, bf16[8,48,1536]{2,1,0:T(8,128)(2,1)S(1)}, u32[]{:S(2)}, u32[]{:S(2)}) %collective-permute-start.42) | collective-permute-done | bytes 1179680 | tf_op jit(solution)/shard_map/ppermute | solution.py:61
  391.6 15.2 %collective-permute-done.49 = bf16[96,1536]{1,0:T(8,128)(2,1)S(1)} collective-permute-done((bf16[96,1536]{1,0:T(8,128)(2,1)}, bf16[96,1536]{1,0:T(8,128)(2,1)S(1)}, u32[]{:S(2)}, u32[]{:S(2)}) %collective-permute-start.49) | collective-permute-done | bytes 294944 | tf_op jit(solution)/shard_map/ppermute | solution.py:87
  407.5 7.2 %collective-permute-done.48 = bf16[2,96,1536]{2,1,0:T(8,128)(2,1)} collective-permute-done((bf16[2,96,1536]{2,1,0:T(8,128)(2,1)S(1)}, bf16[2,96,1536]{2,1,0:T(8,128)(2,1)}, u32[]{:S(2)}, u32[]{:S(2)}) %collective-permute-start.48) | collective-permute-done | bytes 589856 | tf_op jit(solution)/shard_map/ppermute | solution.py:87
  417.7 2.9 collective-permute-start.51
  420.6 5.2 %collective-permute-done.61 = bf16[288,1536]{1,0:T(8,128)(2,1)S(1)} collective-permute-done((bf16[288,1536]{1,0:T(8,128)(2,1)S(1)}, bf16[288,1536]{1,0:T(8,128)(2,1)S(1)}, u32[]{:S(2)}, u32[]{:S(2)}) %collective-permute-start.61) | collective-permute-done | bytes 884768 | tf_op jit(solution)/shard_map/ppermute | solution.py:61
  429.1 2.5 collective-permute-start.52
  431.8 15.5 %collective-permute-done.51 = bf16[2,96,1536]{2,1,0:T(8,128)(2,1)S(1)} collective-permute-done((bf16[2,96,1536]{2,1,0:T(8,128)(2,1)S(1)}, bf16[2,96,1536]{2,1,0:T(8,128)(2,1)S(1)}, u32[]{:S(2)}, u32[]{:S(2)}) %collective-permute-start.51) | collective-permute-done | bytes 589856 | tf_op jit(solution)/shard_map/ppermute | solution.py:87
  447.4 2.7 collective-permute-done.52
  454.4 4.7 collective-permute-done.57
  461.3 5.8 %collective-permute-done.58 = bf16[96,1536]{1,0:T(8,128)(2,1)S(1)} collective-permute-done((bf16[96,1536]{1,0:T(8,128)(2,1)S(1)}, bf16[96,1536]{1,0:T(8,128)(2,1)S(1)}, u32[]{:S(2)}, u32[]{:S(2)}) %collective-permute-start.58) | collective-permute-done | bytes 294944 | tf_op jit(solution)/shard_map/ppermute | solution.py:61
  (518 shorter events, 170.2 us)
Async XLA Ops:
  2.4 13.0 %collective-permute-start = (bf16[128,768]{1,0:T(8,128)(2,1)}, bf16[128,768]{1,0:T(8,128)(2,1)S(1)}, u32[]{:S(2)}, u32[]{:S(2)}) collective-permute-start(bf16[128,768]{1,0:T(8,128)(2,1)} %get-tuple-element.210), channel_id=1, source_target_pairs={{0,16},{8,24},{16,0},{24,8},{1,17},{9,25},{17,1},{25,9},{2,18},{10... | collective-permute-start | bytes 589832 | tf_op jit(solution)/shard_map/ppermute | solution.py:61
  12.6 9.8 %collective-permute-start.2 = (bf16[1,96,1536]{2,1,0:T(8,128)(2,1)S(1)}, bf16[1,96,1536]{2,1,0:T(8,128)(2,1)S(1)}, u32[]{:S(2)}, u32[]{:S(2)}) collective-permute-start(bf16[1,96,1536]{2,1,0:T(8,128)(2,1)S(1)} %bitcast.237), channel_id=1, source_target_pairs={{0,2},{1,3},{2,0},{3,1},{4,6},{5,7},{6,4},{7,5},{8,10},{9,11},{10,... | collective-permute-start | bytes 884744 | tf_op jit(solution)/shard_map/ppermute | solution.py:87
  16.3 9.2 %collective-permute-start.1 = (bf16[256,768]{1,0:T(8,128)(2,1)}, bf16[256,768]{1,0:T(8,128)(2,1)}, u32[]{:S(2)}, u32[]{:S(2)}) collective-permute-start(bf16[256,768]{1,0:T(8,128)(2,1)} %pad_maximum_fusion.10), channel_id=1, source_target_pairs={{0,8},{8,0},{16,24},{24,16},{1,9},{9,1},{17,25},{25,17},{2,10},{10... | collective-permute-start | bytes 1179656 | tf_op jit(solution)/shard_map/ppermute | solution.py:56
  22.3 35.4 %collective-permute-start.9 = (bf16[256,768]{1,0:T(8,128)(2,1)S(1)}, bf16[256,768]{1,0:T(8,128)(2,1)S(1)}, u32[]{:S(2)}, u32[]{:S(2)}) collective-permute-start(bf16[256,768]{1,0:T(8,128)(2,1)S(1)} %pad_maximum_fusion.11), channel_id=1, source_target_pairs={{0,8},{8,0},{16,24},{24,16},{1,9},{9,1},{17,25},{25,17},{2,10},{10... | collective-permute-start | bytes 1179656 | tf_op jit(solution)/shard_map/ppermute | solution.py:56
  22.5 29.2 %collective-permute-start.3 = (bf16[2,96,1536]{2,1,0:T(8,128)(2,1)S(1)}, bf16[2,96,1536]{2,1,0:T(8,128)(2,1)S(1)}, u32[]{:S(2)}, u32[]{:S(2)}) collective-permute-start(bf16[2,96,1536]{2,1,0:T(8,128)(2,1)S(1)} %pad_maximum_fusion.4), channel_id=1, source_target_pairs={{0,4},{1,5},{2,6},{3,7},{4,0},{5,1},{6,2},{7,3},{8,12},{9,13},{10,... | collective-permute-start | bytes 1769480 | tf_op jit(solution)/shard_map/ppermute | solution.py:87
  25.1 19.6 %collective-permute-start.7 = (bf16[1,96,1536]{2,1,0:T(8,128)(2,1)S(1)}, bf16[1,96,1536]{2,1,0:T(8,128)(2,1)S(1)}, u32[]{:S(2)}, u32[]{:S(2)}) collective-permute-start(bf16[1,96,1536]{2,1,0:T(8,128)(2,1)S(1)} %bitcast.244), channel_id=1, source_target_pairs={{0,2},{1,3},{2,0},{3,1},{4,6},{5,7},{6,4},{7,5},{8,10},{9,11},{10,... | collective-permute-start | bytes 884744 | tf_op jit(solution)/shard_map/ppermute | solution.py:87
  64.6 26.6 %collective-permute-start.10 = (bf16[2,96,1536]{2,1,0:T(8,128)(2,1)}, bf16[2,96,1536]{2,1,0:T(8,128)(2,1)}, u32[]{:S(2)}, u32[]{:S(2)}) collective-permute-start(bf16[2,96,1536]{2,1,0:T(8,128)(2,1)} %pad_maximum_fusion.5), channel_id=1, source_target_pairs={{0,4},{1,5},{2,6},{3,7},{4,0},{5,1},{6,2},{7,3},{8,12},{9,13},{10,... | collective-permute-start | bytes 1769480 | tf_op jit(solution)/shard_map/ppermute | solution.py:87
  65.8 27.3 %collective-permute-start.11 = (bf16[4,96,1536]{2,1,0:T(8,128)(2,1)S(1)}, bf16[4,96,1536]{2,1,0:T(8,128)(2,1)}, u32[]{:S(2)}, u32[]{:S(2)}) collective-permute-start(bf16[4,96,1536]{2,1,0:T(8,128)(2,1)S(1)} %pad_maximum_fusion.3.refs_1_), channel_id=1, source_target_pairs={{0,1},{1,0},{2,3},{3,2},{4,5},{5,4},{6,7},{7,6},{8,9},{9,8},{10,11... | collective-permute-start | bytes 3538952 | tf_op jit(solution)/shard_map/ppermute | solution.py:74
  66.3 26.8 %collective-permute-start.13 = (bf16[4,96,1536]{2,1,0:T(8,128)(2,1)S(1)}, bf16[4,96,1536]{2,1,0:T(8,128)(2,1)}, u32[]{:S(2)}, u32[]{:S(2)}) collective-permute-start(bf16[4,96,1536]{2,1,0:T(8,128)(2,1)S(1)} %pad_maximum_fusion.3.refs_1_), channel_id=1, source_target_pairs={{0,16},{8,24},{16,0},{24,8},{1,17},{9,25},{17,1},{25,9},{2,18},{10... | collective-permute-start | bytes 3538952 | tf_op jit(solution)/shard_map/ppermute | solution.py:61
  66.8 16.2 %collective-permute-start.12 = (bf16[1,96,1536]{2,1,0:T(8,128)(2,1)S(1)}, bf16[1,96,1536]{2,1,0:T(8,128)(2,1)}, u32[]{:S(2)}, u32[]{:S(2)}) collective-permute-start(bf16[1,96,1536]{2,1,0:T(8,128)(2,1)S(1)} %bitcast.242), channel_id=1, source_target_pairs={{0,2},{1,3},{2,0},{3,1},{4,6},{5,7},{6,4},{7,5},{8,10},{9,11},{10,... | collective-permute-start | bytes 884744 | tf_op jit(solution)/shard_map/ppermute | solution.py:87
  93.1 30.5 %collective-permute-start.14 = (bf16[4,96,1536]{2,1,0:T(8,128)(2,1)}, bf16[4,96,1536]{2,1,0:T(8,128)(2,1)}, u32[]{:S(2)}, u32[]{:S(2)}) collective-permute-start(bf16[4,96,1536]{2,1,0:T(8,128)(2,1)} %constant_dynamic-update-slice_fusion.refs_1_), channel_id=1, source_target_pairs={{0,1},{1,0},{2,3},{3,2},{4,5},{5,4},{6,7},{7,6},{8,9},{9,8},{10,11... | collective-permute-start | bytes 3538952 | tf_op jit(solution)/shard_map/ppermute | solution.py:74
  93.6 29.9 %collective-permute-start.17 = (bf16[4,96,1536]{2,1,0:T(8,128)(2,1)}, bf16[4,96,1536]{2,1,0:T(8,128)(2,1)}, u32[]{:S(2)}, u32[]{:S(2)}) collective-permute-start(bf16[4,96,1536]{2,1,0:T(8,128)(2,1)} %collective-permute-done.11.refs_2_), channel_id=1, source_target_pairs={{0,16},{8,24},{16,0},{24,8},{1,17},{9,25},{17,1},{25,9},{2,18},{10... | collective-permute-start | bytes 3538952 | tf_op jit(solution)/shard_map/ppermute | solution.py:61
  94.8 27.7 %collective-permute-start.18 = (bf16[2,96,1536]{2,1,0:T(8,128)(2,1)}, bf16[2,96,1536]{2,1,0:T(8,128)(2,1)}, u32[]{:S(2)}, u32[]{:S(2)}) collective-permute-start(bf16[2,96,1536]{2,1,0:T(8,128)(2,1)} %pad_maximum_fusion.6), channel_id=1, source_target_pairs={{0,4},{1,5},{2,6},{3,7},{4,0},{5,1},{6,2},{7,3},{8,12},{9,13},{10,... | collective-permute-start | bytes 1769480 | tf_op jit(solution)/shard_map/ppermute | solution.py:87
  95.6 17.3 %collective-permute-start.19 = (bf16[1,96,1536]{2,1,0:T(8,128)(2,1)S(1)}, bf16[1,96,1536]{2,1,0:T(8,128)(2,1)}, u32[]{:S(2)}, u32[]{:S(2)}) collective-permute-start(bf16[1,96,1536]{2,1,0:T(8,128)(2,1)S(1)} %bitcast.240), channel_id=1, source_target_pairs={{0,2},{1,3},{2,0},{3,1},{4,6},{5,7},{6,4},{7,5},{8,10},{9,11},{10,... | collective-permute-start | bytes 884744 | tf_op jit(solution)/shard_map/ppermute | solution.py:87
  123.6 50.2 %collective-permute-start.20 = (bf16[4,96,1536]{2,1,0:T(8,128)(2,1)S(1)}, bf16[4,96,1536]{2,1,0:T(8,128)(2,1)}, u32[]{:S(2)}, u32[]{:S(2)}) collective-permute-start(bf16[4,96,1536]{2,1,0:T(8,128)(2,1)S(1)} %constant_dynamic-update-slice_fusion.2.refs_1_), channel_id=1, source_target_pairs={{0,1},{1,0},{2,3},{3,2},{4,5},{5,4},{6,7},{7,6},{8,9},{9,8},{10,11... | collective-permute-start | bytes 3538952 | tf_op jit(solution)/shard_map/ppermute | solution.py:74
  125.1 48.6 %collective-permute-start.21 = (bf16[4,96,1536]{2,1,0:T(8,128)(2,1)S(1)}, bf16[4,96,1536]{2,1,0:T(8,128)(2,1)S(1)}, u32[]{:S(2)}, u32[]{:S(2)}) collective-permute-start(bf16[4,96,1536]{2,1,0:T(8,128)(2,1)S(1)} %constant_dynamic-update-slice_fusion.2.refs_1_), channel_id=1, source_target_pairs={{0,16},{8,24},{16,0},{24,8},{1,17},{9,25},{17,1},{25,9},{2,18},{10... | collective-permute-start | bytes 3538952 | tf_op jit(solution)/shard_map/ppermute | solution.py:61
  127.7 17.5 %collective-permute-start.16 = (bf16[4,96,768]{2,1,0:T(8,128)(2,1)S(1)}, bf16[4,96,768]{2,1,0:T(8,128)(2,1)S(1)}, u32[]{:S(2)}, u32[]{:S(2)}) collective-permute-start(bf16[4,96,768]{2,1,0:T(8,128)(2,1)S(1)} %pad_maximum_fusion.7), channel_id=1, source_target_pairs={{0,8},{8,0},{16,24},{24,16},{1,9},{9,1},{17,25},{25,17},{2,10},{10... | collective-permute-start | bytes 1769480 | tf_op jit(solution)/shard_map/ppermute | solution.py:56
  139.4 28.0 %collective-permute-start.15 = (bf16[512,384]{1,0:T(8,128)(2,1)S(1)}, bf16[512,384]{1,0:T(8,128)(2,1)S(1)}, u32[]{:S(2)}, u32[]{:S(2)}) collective-permute-start(bf16[512,384]{1,0:T(8,128)(2,1)S(1)} %attend.2), channel_id=1, source_target_pairs={{0,8},{8,0},{16,24},{24,16},{1,9},{9,1},{17,25},{25,17},{2,10},{10... | collective-permute-start | bytes 1179656 | tf_op jit(solution)/shard_map/ppermute | solution.py:56
  140.0 27.4 %collective-permute-start.22 = (bf16[2,96,1536]{2,1,0:T(8,128)(2,1)S(1)}, bf16[2,96,1536]{2,1,0:T(8,128)(2,1)S(1)}, u32[]{:S(2)}, u32[]{:S(2)}) collective-permute-start(bf16[2,96,1536]{2,1,0:T(8,128)(2,1)S(1)} %pad_maximum_fusion.8), channel_id=1, source_target_pairs={{0,4},{1,5},{2,6},{3,7},{4,0},{5,1},{6,2},{7,3},{8,12},{9,13},{10,... | collective-permute-start | bytes 1769480 | tf_op jit(solution)/shard_map/ppermute | solution.py:87
  173.8 28.1 %collective-permute-start.24 = (bf16[4,96,1536]{2,1,0:T(8,128)(2,1)S(1)}, bf16[4,96,1536]{2,1,0:T(8,128)(2,1)}, u32[]{:S(2)}, u32[]{:S(2)}) collective-permute-start(bf16[4,96,1536]{2,1,0:T(8,128)(2,1)S(1)} %constant_dynamic-update-slice_fusion.4.refs_1_), channel_id=1, source_target_pairs={{0,1},{1,0},{2,3},{3,2},{4,5},{5,4},{6,7},{7,6},{8,9},{9,8},{10,11... | collective-permute-start | bytes 3538952 | tf_op jit(solution)/shard_map/ppermute | solution.py:74
  174.4 27.9 %collective-permute-start.25 = (bf16[4,96,1536]{2,1,0:T(8,128)(2,1)}, bf16[4,96,1536]{2,1,0:T(8,128)(2,1)}, u32[]{:S(2)}, u32[]{:S(2)}) collective-permute-start(bf16[4,96,1536]{2,1,0:T(8,128)(2,1)} %collective-permute-done.20.refs_2_), channel_id=1, source_target_pairs={{0,16},{8,24},{16,0},{24,8},{1,17},{9,25},{17,1},{25,9},{2,18},{10... | collective-permute-start | bytes 3538952 | tf_op jit(solution)/shard_map/ppermute | solution.py:61
  206.1 13.1 %collective-permute-start.27 = (bf16[4,96,768]{2,1,0:T(8,128)(2,1)S(1)}, bf16[4,96,768]{2,1,0:T(8,128)(2,1)S(1)}, u32[]{:S(2)}, u32[]{:S(2)}) collective-permute-start(bf16[4,96,768]{2,1,0:T(8,128)(2,1)S(1)} %pad_maximum_fusion.9), channel_id=1, source_target_pairs={{0,8},{8,0},{16,24},{24,16},{1,9},{9,1},{17,25},{25,17},{2,10},{10... | collective-permute-start | bytes 1769480 | tf_op jit(solution)/shard_map/ppermute | solution.py:56
  236.6 10.4 %collective-permute-start.29 = (bf16[512,768]{1,0:T(8,128)(2,1)}, bf16[512,768]{1,0:T(8,128)(2,1)}, u32[]{:S(2)}, u32[]{:S(2)}) collective-permute-start(bf16[512,768]{1,0:T(8,128)(2,1)} %get-tuple-element.242), channel_id=1, source_target_pairs={{0,8},{8,0},{16,24},{24,16},{1,9},{9,1},{17,25},{25,17},{2,10},{10... | collective-permute-start | bytes 2359304 | tf_op jit(solution)/shard_map/ppermute | solution.py:56
  240.3 28.2 %collective-permute-start.35 = (bf16[4,192,768]{2,1,0:T(8,128)(2,1)}, bf16[4,192,768]{2,1,0:T(8,128)(2,1)}, u32[]{:S(2)}, u32[]{:S(2)}) collective-permute-start(bf16[4,192,768]{2,1,0:T(8,128)(2,1)} %dynamic-slice_bitcast_fusion.2), channel_id=1, source_target_pairs={{0,1},{1,0},{2,3},{3,2},{4,5},{5,4},{6,7},{7,6},{8,9},{9,8},{10,11... | collective-permute-start | bytes 3538952 | tf_op jit(solution)/shard_map/ppermute | solution.py:74
  271.8 30.9 %collective-permute-start.36 = (bf16[4,96,1536]{2,1,0:T(8,128)(2,1)}, bf16[4,96,1536]{2,1,0:T(8,128)(2,1)}, u32[]{:S(2)}, u32[]{:S(2)}) collective-permute-start(bf16[4,96,1536]{2,1,0:T(8,128)(2,1)} %dynamic-slice_bitcast_fusion.3), channel_id=1, source_target_pairs={{0,1},{1,0},{2,3},{3,2},{4,5},{5,4},{6,7},{7,6},{8,9},{9,8},{10,11... | collective-permute-start | bytes 3538952 | tf_op jit(solution)/shard_map/ppermute | solution.py:74
  272.4 29.1 %collective-permute-start.37 = (bf16[2,192,768]{2,1,0:T(8,128)(2,1)S(1)}, bf16[2,192,768]{2,1,0:T(8,128)(2,1)}, u32[]{:S(2)}, u32[]{:S(2)}) collective-permute-start(bf16[2,192,768]{2,1,0:T(8,128)(2,1)S(1)} %dynamic-slice_bitcast_fusion.10), channel_id=1, source_target_pairs={{0,4},{1,5},{2,6},{3,7},{4,0},{5,1},{6,2},{7,3},{8,12},{9,13},{10,... | collective-permute-start | bytes 1769480 | tf_op jit(solution)/shard_map/ppermute | solution.py:87
  287.6 21.6 %collective-permute-start.31 = (bf16[512,768]{1,0:T(8,128)(2,1)}, bf16[512,768]{1,0:T(8,128)(2,1)S(1)}, u32[]{:S(2)}, u32[]{:S(2)}) collective-permute-start(bf16[512,768]{1,0:T(8,128)(2,1)} %get-tuple-element.246), channel_id=1, source_target_pairs={{0,8},{8,0},{16,24},{24,16},{1,9},{9,1},{17,25},{25,17},{2,10},{10... | collective-permute-start | bytes 2359304 | tf_op jit(solution)/shard_map/ppermute | solution.py:56
  305.4 42.8 %collective-permute-start.41 = (bf16[8,48,1536]{2,1,0:T(8,128)(2,1)}, bf16[8,48,1536]{2,1,0:T(8,128)(2,1)}, u32[]{:S(2)}, u32[]{:S(2)}) collective-permute-start(bf16[8,48,1536]{2,1,0:T(8,128)(2,1)} %fusion.24), channel_id=1, source_target_pairs={{0,16},{8,24},{16,0},{24,8},{1,17},{9,25},{17,1},{25,9},{2,18},{10... | collective-permute-start | bytes 3538952 | tf_op jit(solution)/shard_map/ppermute | solution.py:61
  305.9 40.2 %collective-permute-start.38 = (bf16[4,96,1536]{2,1,0:T(8,128)(2,1)}, bf16[4,96,1536]{2,1,0:T(8,128)(2,1)}, u32[]{:S(2)}, u32[]{:S(2)}) collective-permute-start(bf16[4,96,1536]{2,1,0:T(8,128)(2,1)} %dynamic-slice_bitcast_fusion.4), channel_id=1, source_target_pairs={{0,1},{1,0},{2,3},{3,2},{4,5},{5,4},{6,7},{7,6},{8,9},{9,8},{10,11... | collective-permute-start | bytes 3538952 | tf_op jit(solution)/shard_map/ppermute | solution.py:74
  307.4 37.3 %collective-permute-start.39 = (bf16[2,96,1536]{2,1,0:T(8,128)(2,1)}, bf16[2,96,1536]{2,1,0:T(8,128)(2,1)}, u32[]{:S(2)}, u32[]{:S(2)}) collective-permute-start(bf16[2,96,1536]{2,1,0:T(8,128)(2,1)} %dynamic-slice_bitcast_fusion.9), channel_id=1, source_target_pairs={{0,4},{1,5},{2,6},{3,7},{4,0},{5,1},{6,2},{7,3},{8,12},{9,13},{10,... | collective-permute-start | bytes 1769480 | tf_op jit(solution)/shard_map/ppermute | solution.py:87
  307.4 31.1 %collective-permute-start.40 = (bf16[192,768]{1,0:T(8,128)(2,1)S(1)}, bf16[192,768]{1,0:T(8,128)(2,1)S(1)}, u32[]{:S(2)}, u32[]{:S(2)}) collective-permute-start(bf16[192,768]{1,0:T(8,128)(2,1)S(1)} %dynamic-slice_bitcast_fusion.15), channel_id=1, source_target_pairs={{0,2},{1,3},{2,0},{3,1},{4,6},{5,7},{6,4},{7,5},{8,10},{9,11},{10,... | collective-permute-start | bytes 884744 | tf_op jit(solution)/shard_map/ppermute | solution.py:87
  328.1 9.7 %collective-permute-start.32 = (bf16[128,768]{1,0:T(8,128)(2,1)S(1)}, bf16[128,768]{1,0:T(8,128)(2,1)S(1)}, u32[]{:S(2)}, u32[]{:S(2)}) collective-permute-start(bf16[128,768]{1,0:T(8,128)(2,1)S(1)} %get-tuple-element.206), channel_id=1, source_target_pairs={{0,16},{8,24},{16,0},{24,8},{1,17},{9,25},{17,1},{25,9},{2,18},{10... | collective-permute-start | bytes 589832 | tf_op jit(solution)/shard_map/ppermute | solution.py:61
  343.6 11.2 %collective-permute-start.34 = (f32[128,768]{1,0:T(8,128)S(1)}, f32[128,768]{1,0:T(8,128)S(1)}, u32[]{:S(2)}, u32[]{:S(2)}) collective-permute-start(f32[128,768]{1,0:T(8,128)S(1)} %get-tuple-element.202), channel_id=1, source_target_pairs={{0,16},{8,24},{16,0},{24,8},{1,17},{9,25},{17,1},{25,9},{2,18},{10... | collective-permute-start | bytes 1179656 | tf_op jit(solution)/shard_map/ppermute | solution.py:61
  348.3 27.6 %collective-permute-start.44 = (bf16[2,96,1536]{2,1,0:T(8,128)(2,1)S(1)}, bf16[2,96,1536]{2,1,0:T(8,128)(2,1)S(1)}, u32[]{:S(2)}, u32[]{:S(2)}) collective-permute-start(bf16[2,96,1536]{2,1,0:T(8,128)(2,1)S(1)} %dynamic-slice_bitcast_fusion.8), channel_id=1, source_target_pairs={{0,4},{1,5},{2,6},{3,7},{4,0},{5,1},{6,2},{7,3},{8,12},{9,13},{10,... | collective-permute-start | bytes 1769480 | tf_op jit(solution)/shard_map/ppermute | solution.py:87
  355.8 27.2 %collective-permute-start.42 = (bf16[8,48,1536]{2,1,0:T(8,128)(2,1)S(1)}, bf16[8,48,1536]{2,1,0:T(8,128)(2,1)S(1)}, u32[]{:S(2)}, u32[]{:S(2)}) collective-permute-start(bf16[8,48,1536]{2,1,0:T(8,128)(2,1)S(1)} %copy-done.62), channel_id=1, source_target_pairs={{0,16},{8,24},{16,0},{24,8},{1,17},{9,25},{17,1},{25,9},{2,18},{10... | collective-permute-start | bytes 3538952 | tf_op jit(solution)/shard_map/ppermute | solution.py:61
  356.3 27.2 %collective-permute-start.43 = (bf16[4,96,1536]{2,1,0:T(8,128)(2,1)S(1)}, bf16[4,96,1536]{2,1,0:T(8,128)(2,1)S(1)}, u32[]{:S(2)}, u32[]{:S(2)}) collective-permute-start(bf16[4,96,1536]{2,1,0:T(8,128)(2,1)S(1)} %copy-done.63), channel_id=1, source_target_pairs={{0,1},{1,0},{2,3},{3,2},{4,5},{5,4},{6,7},{7,6},{8,9},{9,8},{10,11... | collective-permute-start | bytes 3538952 | tf_op jit(solution)/shard_map/ppermute | solution.py:74
  357.8 29.5 %collective-permute-start.45 = (bf16[96,1536]{1,0:T(8,128)(2,1)S(1)}, bf16[96,1536]{1,0:T(8,128)(2,1)S(1)}, u32[]{:S(2)}, u32[]{:S(2)}) collective-permute-start(bf16[96,1536]{1,0:T(8,128)(2,1)S(1)} %dynamic-slice_bitcast_fusion.14), channel_id=1, source_target_pairs={{0,2},{1,3},{2,0},{3,1},{4,6},{5,7},{6,4},{7,5},{8,10},{9,11},{10,... | collective-permute-start | bytes 884744 | tf_op jit(solution)/shard_map/ppermute | solution.py:87
  388.9 27.1 %collective-permute-start.47 = (bf16[4,96,1536]{2,1,0:T(8,128)(2,1)}, bf16[4,96,1536]{2,1,0:T(8,128)(2,1)}, u32[]{:S(2)}, u32[]{:S(2)}) collective-permute-start(bf16[4,96,1536]{2,1,0:T(8,128)(2,1)} %dynamic-slice_bitcast_fusion), channel_id=1, source_target_pairs={{0,1},{1,0},{2,3},{3,2},{4,5},{5,4},{6,7},{7,6},{8,9},{9,8},{10,11... | collective-permute-start | bytes 3538952 | tf_op jit(solution)/shard_map/ppermute | solution.py:74
  389.5 25.3 %collective-permute-start.48 = (bf16[2,96,1536]{2,1,0:T(8,128)(2,1)S(1)}, bf16[2,96,1536]{2,1,0:T(8,128)(2,1)}, u32[]{:S(2)}, u32[]{:S(2)}) collective-permute-start(bf16[2,96,1536]{2,1,0:T(8,128)(2,1)S(1)} %dynamic-slice_bitcast_fusion.7), channel_id=1, source_target_pairs={{0,4},{1,5},{2,6},{3,7},{4,0},{5,1},{6,2},{7,3},{8,12},{9,13},{10,... | collective-permute-start | bytes 1769480 | tf_op jit(solution)/shard_map/ppermute | solution.py:87
  389.5 17.3 %collective-permute-start.49 = (bf16[96,1536]{1,0:T(8,128)(2,1)}, bf16[96,1536]{1,0:T(8,128)(2,1)S(1)}, u32[]{:S(2)}, u32[]{:S(2)}) collective-permute-start(bf16[96,1536]{1,0:T(8,128)(2,1)} %dynamic-slice_bitcast_fusion.13), channel_id=1, source_target_pairs={{0,2},{1,3},{2,0},{3,1},{4,6},{5,7},{6,4},{7,5},{8,10},{9,11},{10,... | collective-permute-start | bytes 884744 | tf_op jit(solution)/shard_map/ppermute | solution.py:87
  407.0 18.8 %collective-permute-start.61 = (bf16[288,1536]{1,0:T(8,128)(2,1)S(1)}, bf16[288,1536]{1,0:T(8,128)(2,1)S(1)}, u32[]{:S(2)}, u32[]{:S(2)}) collective-permute-start(bf16[288,1536]{1,0:T(8,128)(2,1)S(1)} %maximum_maximum_fusion), channel_id=1, source_target_pairs={{0,16},{8,24},{16,0},{24,8},{1,17},{9,25},{17,1},{25,9},{2,18},{10... | collective-permute-start | bytes 2654216 | tf_op jit(solution)/shard_map/ppermute | solution.py:61
  417.7 14.0 %collective-permute-start.50 = (f32[2,1920]{1,0:T(2,128)S(1)}, f32[2,1920]{1,0:T(2,128)S(1)}, u32[]{:S(2)}, u32[]{:S(2)}) collective-permute-start(f32[2,1920]{1,0:T(2,128)S(1)} %dynamic-slice_bitcast_fusion.20), channel_id=1, source_target_pairs={{0,4},{1,5},{2,6},{3,7},{4,0},{5,1},{6,2},{7,3},{8,12},{9,13},{10,... | collective-permute-start | bytes 46088 | tf_op jit(solution)/shard_map/ppermute | solution.py:87
  417.7 29.5 %collective-permute-start.51 = (bf16[2,96,1536]{2,1,0:T(8,128)(2,1)S(1)}, bf16[2,96,1536]{2,1,0:T(8,128)(2,1)S(1)}, u32[]{:S(2)}, u32[]{:S(2)}) collective-permute-start(bf16[2,96,1536]{2,1,0:T(8,128)(2,1)S(1)} %dynamic-slice_bitcast_fusion.6), channel_id=1, source_target_pairs={{0,4},{1,5},{2,6},{3,7},{4,0},{5,1},{6,2},{7,3},{8,12},{9,13},{10,... | collective-permute-start | bytes 1769480 | tf_op jit(solution)/shard_map/ppermute | solution.py:87
  429.0 39.7 %collective-permute-start.62 = (bf16[288,1536]{1,0:T(8,128)(2,1)}, bf16[288,1536]{1,0:T(8,128)(2,1)}, u32[]{:S(2)}, u32[]{:S(2)}) collective-permute-start(bf16[288,1536]{1,0:T(8,128)(2,1)} %add_convert_fusion), channel_id=1, source_target_pairs={{0,8},{8,0},{16,24},{24,16},{1,9},{9,1},{17,25},{25,17},{2,10},{10... | collective-permute-start | bytes 2654216 | tf_op jit(solution)/shard_map/ppermute | solution.py:56
  429.1 21.0 %collective-permute-start.52 = (bf16[96,1536]{1,0:T(8,128)(2,1)S(1)}, bf16[96,1536]{1,0:T(8,128)(2,1)S(1)}, u32[]{:S(2)}, u32[]{:S(2)}) collective-permute-start(bf16[96,1536]{1,0:T(8,128)(2,1)S(1)} %dynamic-slice_bitcast_fusion.12), channel_id=1, source_target_pairs={{0,2},{1,3},{2,0},{3,1},{4,6},{5,7},{6,4},{7,5},{8,10},{9,11},{10,... | collective-permute-start | bytes 884744 | tf_op jit(solution)/shard_map/ppermute | solution.py:87
  450.1 8.9 %collective-permute-start.57 = (bf16[96,1536]{1,0:T(8,128)(2,1)S(1)}, bf16[96,1536]{1,0:T(8,128)(2,1)S(1)}, u32[]{:S(2)}, u32[]{:S(2)}) collective-permute-start(bf16[96,1536]{1,0:T(8,128)(2,1)S(1)} %dynamic-slice_bitcast_fusion.11), channel_id=1, source_target_pairs={{0,2},{1,3},{2,0},{3,1},{4,6},{5,7},{6,4},{7,5},{8,10},{9,11},{10,... | collective-permute-start | bytes 884744 | tf_op jit(solution)/shard_map/ppermute | solution.py:87
  452.2 8.4 %collective-permute-start.56 = (bf16[96,1536]{1,0:T(8,128)(2,1)S(1)}, bf16[96,1536]{1,0:T(8,128)(2,1)S(1)}, u32[]{:S(2)}, u32[]{:S(2)}) collective-permute-start(bf16[96,1536]{1,0:T(8,128)(2,1)S(1)} %fusion.34), channel_id=1, source_target_pairs={{0,16},{8,24},{16,0},{24,8},{1,17},{9,25},{17,1},{25,9},{2,18},{10... | collective-permute-start | bytes 884744 | tf_op jit(solution)/shard_map/ppermute | solution.py:61
  460.6 12.2 %collective-permute-start.59 = (bf16[96,1536]{1,0:T(8,128)(2,1)S(1)}, bf16[96,1536]{1,0:T(8,128)(2,1)S(1)}, u32[]{:S(2)}, u32[]{:S(2)}) collective-permute-start(bf16[96,1536]{1,0:T(8,128)(2,1)S(1)} %add_convert_fusion.3.mine_ref), channel_id=1, source_target_pairs={{0,8},{8,0},{16,24},{24,16},{1,9},{9,1},{17,25},{25,17},{2,10},{10... | collective-permute-start | bytes 884744 | tf_op jit(solution)/shard_map/ppermute | solution.py:56
  (120 other events, 648.4 us)

commit v4 on v3

--- a/solution.py
+++ b/solution.py
@@ -88,7 +88,8 @@
 
 
 def doubled(values, step):
-    return jnp.concatenate([values, swap_line(values, step)], 0)
+    there = swap_line(values, step)
+    return jnp.concatenate([values, there], 0), there
 
 
 def place_kernel(fill, where_ref, *refs):
@@ -102,7 +103,7 @@
 
     def spot_index(spot):
         blank = (0,) * len(spot)
-        return lambda k, w: (jnp.bitwise_xor(w[0], k),) + blank
+        return lambda k, w: (jnp.bitwise_xor(w[0], 2 * (k % 2) + k // 2),) + blank
 
     return pl.pallas_call(
         lambda *refs: place_kernel(fill, *refs),
@@ -180,16 +181,17 @@
                 )
             return None if beside is None else swap_row(beside)
         own = lax.axis_index("wt")
-        bits = (own % 2, own // 4, own // 2 % 2)
-        moves = (swap_pair, lambda v: swap_line(v, 2), lambda v: swap_line(v, 1))
-        axes = (1, 0, 0)
+        bits = (own % 2, own // 2 % 2, own // 4)
+        moves = (swap_pair, lambda v: swap_line(v, 1), lambda v: swap_line(v, 2))
+        axes = (1, 1, 0)
         if values is not None:
             self.stages[0] = [v.reshape((owners // 2, 2) + v.shape[1:]) for v in values]
         active = [i for i in range(3) if self.stages[i] is not None]
         sends = [[picked(v, 1 - bits[i], axes[i]) for v in self.stages[i]] for i in active]
         earlier = [v for v in (self.arrived, gate) if v is not None]
         if earlier:
-            sends, beside = after((sends, beside), earlier)
+            sends = [[after(v, earlier) for v in send] for send in sends]
+            beside = None if beside is None else after(beside, earlier)
         theirs = [[moves[i](v) for v in send] for i, send in zip(active, sends)]
         swapped = None if beside is None else swap_row(beside)
         self.arrived = (theirs, swapped)
@@ -322,7 +324,7 @@
         + [pl.BlockSpec((1,) + v.shape[1:], lambda i: (layer, 0, 0)) for v in members],
         out_specs=[pl.BlockSpec(shape, lambda i: (0, 0))] * 2,
         out_shape=[jax.ShapeDtypeStruct(shape, BF)] * 2,
-        compiler_params=pltpu.CompilerParams(vmem_limit_bytes=VMEM_BYTES),
+        compiler_params=pltpu.CompilerParams(vmem_limit_bytes=60 * 1024 * 1024),
         cost_estimate=lasting(3.0),
         name="pack",
     )(where, *members)
@@ -415,32 +417,40 @@
     return values * below, below + values * density
 
 
-def settle_kernel(core_ref, mine_ref, mine_wide_ref, other_ref, other_wide_ref, *refs):
+def settle_kernel(where_ref, *refs):
     *squares, up, down = refs[-6:]
-    core = core_ref[0]
+    side, core = where_ref[2], where_ref[3]
     shard, features = squares[0].shape[1:]
-    half = features // 2
+    half, part = features // 2, shard // 2
     unit_half = down.shape[1] // 2
     owners = up.shape[2] // (2 * unit_half)
+    pieces = 3 if refs[1].shape[0] == shard else 2
+    mine_ref, *mine_wide = refs[:pieces]
+    other_ref, *other_wide = refs[pieces : 2 * pieces]
     here = pl.ds(pl.multiple_of(core * half, 128), half)
     there = pl.ds(pl.multiple_of((1 - core) * half, 128), half)
     for position, target in enumerate(squares):
         columns = slice(position * half, (position + 1) * half)
         target[0, :, here] = mine_ref[:, columns].astype(F32)
         target[0, :, there] = other_ref[:, columns].astype(F32)
-    mine, other = mine_wide_ref[:shard].astype(F32), other_wide_ref[:shard].astype(F32)
-    low = jnp.where(core == 0, mine, other)
-    high = jnp.where(core == 0, other, mine)
-    for owner in range(owners):
-        columns = slice(owner * unit_half, (owner + 1) * unit_half)
-        up[0, :, 2 * owner * unit_half : 2 * (owner + 1) * unit_half] = jnp.concatenate(
-            [low[:, columns], high[:, columns]], 1
-        )
-    for pair in range(2):
-        columns = slice(pair * features, (pair + 1) * features)
-        for source, where in ((mine_wide_ref, core), (other_wide_ref, 1 - core)):
-            rows = pl.ds(pl.multiple_of(where * unit_half, 8) + pair * shard, shard)
-            down[0, rows] = source[shard:, columns].astype(F32)
+    spread = [0] if pieces == 2 else [side, 1 - side]
+    rows = shard if pieces == 2 else part
+    for where, mine_part, other_part in zip(spread, mine_wide, other_wide):
+        mine, other = mine_part[:rows].astype(F32), other_part[:rows].astype(F32)
+        low = jnp.where(core == 0, mine, other)
+        high = jnp.where(core == 0, other, mine)
+        target = pl.ds(where * rows if pieces == 2 else pl.multiple_of(where * rows, 8), rows)
+        for owner in range(owners):
+            columns = slice(owner * unit_half, (owner + 1) * unit_half)
+            up[0, target, 2 * owner * unit_half : 2 * (owner + 1) * unit_half] = jnp.concatenate(
+                [low[:, columns], high[:, columns]], 1
+            )
+        for pair in range(2):
+            columns = slice(pair * features, (pair + 1) * features)
+            for source, place_core in ((mine_part, core), (other_part, 1 - core)):
+                first = place_core * unit_half + where * shard
+                target = pl.ds(pl.multiple_of(first, 8) + pair * rows, rows)
+                down[0, target] = source[rows:, columns].astype(F32)
 
 
 def settle(core, pieces, earlier, layer, shapes):
@@ -497,10 +507,23 @@
         mine = jnp.concatenate([kept, swap_row(sent)], 0)
         return by_core(core, mine, swap_core(mine), 0)
 
-    def from_chip(mine):
-        kept, sent = mine[:frames_here], mine[frames_here:]
-        other = swap_row(sent)
+    def from_chip(mine, other):
+        kept = mine[:frames_here]
         return jnp.where(side == 0, jnp.stack([kept, other]), jnp.stack([other, kept]))
+
+    def by_side(mine, there):
+        low, high = jnp.where(side == 0, mine, there), jnp.where(side == 0, there, mine)
+        part = shard // 2
+        low_down, high_down = low[part:], high[part:]
+        return jnp.concatenate(
+            [
+                low[:part],
+                high[:part],
+                jnp.concatenate([low_down[:, :features], high_down[:, :features]], 1),
+                jnp.concatenate([low_down[:, features:], high_down[:, features:]], 1),
+            ],
+            0,
+        )
 
     def own_rows(values):
         return lax.dynamic_slice_in_dim(values, core * 2 * frames_here, 2 * frames_here, 0)
@@ -552,33 +575,37 @@
             *(pack(where, squares, up_weight, down_weight, layer) for layer in range(LAYERS))
         )
 
-        wide_hop = doubled(wide_piece[0][None], 1)
-        hop = doubled(after(branch_piece[0], wide_hop)[None], 1)
-        wide = [doubled(wide_hop, 2), None]
-        packed = after(packed, wide[0])
-        wide_near, hop, piece = after(
-            (wide[0], hop, wide_piece[1][None]), (wide[0], down_in)
-        )
-        wide_far = [swap_pair(wide_near), None]
-        wide_there = [swap_row(wide_near), None]
-        branch = [doubled(hop, 2), None]
-        wide_hop = doubled(piece, 1)
-        near, far, hop, piece = after(
-            (branch[0], wide_far[0], wide_hop, branch_piece[1]),
-            (wide_far[0], wide_there[0], branch[0]),
-        )
-        branch_far = [swap_pair(near), None]
-        wide_far_there = [swap_row(far), None]
-        wide[1] = doubled(hop, 2)
-        hop = doubled(piece[None], 1)
-        near, hop = after((wide[1], hop), (branch_far[0], wide_far_there[0], wide[1]))
-        wide_far[1] = swap_pair(near)
-        wide_there[1] = swap_row(near)
-        branch[1] = doubled(hop, 2)
-        third = (wide_far[1], wide_there[1], branch[1])
-        near, far = after((branch[1], wide_far[1]), third)
+        wide, branch = [None, None], [None, None]
+        wide_far, branch_far = [None, None], [None, None]
+        wide_there, wide_far_there = [None, None], [None, None]
+        wide_hop, first = doubled(wide_piece[0][None], 2)
+
+        wide[0], tied = doubled(after(wide_hop, first), 1)
+        branch_hop, also = doubled(after(branch_piece[0][None], first), 2)
+        packed_hop, _ = doubled(after(packed[None], first), 2)
+        earlier = (tied, also, down_in)
+
+        wide_far[0] = swap_pair(after(wide[0], earlier))
+        wide_there[0] = swap_row(after(wide[0], earlier))
+        branch[0], tied = doubled(after(branch_hop, earlier), 1)
+        wide_hop, also = doubled(after(wide_piece[1][None], earlier), 2)
+        packed_line, _ = doubled(after(packed_hop, earlier), 1)
+        earlier = (tied, also, wide_far[0], wide_there[0])
+
+        branch_far[0] = swap_pair(after(branch[0], earlier))
+        wide_far_there[0] = swap_row(after(wide_far[0], earlier))
+        wide[1], tied = doubled(after(wide_hop, earlier), 1)
+        branch_hop, also = doubled(after(branch_piece[1][None], earlier), 2)
+        packed_far = swap_pair(after(packed_line, earlier))
+        earlier = (tied, also, branch_far[0], wide_far_there[0])
+
+        wide_far[1] = swap_pair(after(wide[1], earlier))
+        wide_there[1] = swap_row(after(wide[1], earlier))
+        branch[1], tied = doubled(after(branch_hop, earlier), 1)
+        third = (wide_far[1], wide_there[1], tied)
+
         branch_far[1], wide_far_there[1] = lax.optimization_barrier(
-            (swap_pair(near), swap_row(far))
+            (swap_pair(after(branch[1], third)), swap_row(after(wide_far[1], third)))
         )
 
         for layer in range(LAYERS):
@@ -622,11 +649,9 @@
             out_half = branch[:, 3 * half :]
             gathered["out", layer] = by_core(core, out_half, swap_core(out_half), 1)
     if direct:
-        reached = packed[None]
-        for step in LINE_STEPS:
-            reached = doubled(reached, step)
-        other = swap_pair(reached)
-        spread = jnp.stack([reached, other], 1)
+        spread = jnp.stack([packed_line, packed_far], 1)
+        spread = spread.reshape((2, 2, 2) + packed.shape).swapaxes(0, 1)
+        spread = spread.reshape((owners // 2, 2) + packed.shape)
         for bit in LINE_STEPS:
             turned = spread.reshape((owners // (4 * bit), 2, bit, 2) + packed.shape)
             spread = jnp.where((line & bit) == 0, turned, turned[:, ::-1]).reshape(spread.shape)
@@ -749,7 +774,9 @@
         grad_branch = jnp.concatenate([grad_in, grad_out.astype(BF)], 1)
         grad_branch = grad_branch.reshape(owners, shard, 2 * features)
         if layer > 0:
-            reducer.tick([grad_up], grad_branch)
+            result_there = reducer.tick(
+                [grad_up], grad_branch, beside=result_rows[frames_here:]
+            )
         else:
             up_there = reducer.tick([grad_branch], beside=picked(grad_up, 1 - side, 1))
             grad_wide = jnp.concatenate(
@@ -769,8 +796,6 @@
             )
             grad_down_bias = first_sums[2:3]
         else:
-            result_rows = after(result_rows, grad_qkv)
-            result = from_chip(result_rows)
             theirs = lax.dynamic_slice_in_dim(
                 partial, (1 - core) * 2 * frames_here, 2 * frames_here, 0
             )
@@ -778,7 +803,6 @@
             before, _, first_sums = norm_back(
                 partial, there, hidden, vec["first_scale"], grad_middle, row_core
             )
-            input_grad = from_chip(before)
 
         twice = jnp.stack([grad_in_bias[:half], grad_in_bias[2 * half :]])
         rows = jnp.concatenate(
@@ -805,7 +829,10 @@
     from_units = from_units.reshape(LAYERS, owners, unit_half).swapaxes(0, 1)
     from_units = from_units.reshape(owners, LAYERS * unit_half)
     packed = jnp.concatenate([packed, from_units], 1)
+    before = after(before, (reducer.arrived, packed))
     reducer.tick([grad_wide, packed])
+    result = from_chip(result_rows, result_there)
+    input_grad = from_chip(before, swap_row(before[frames_here:]))
     reducer.finish()
     for layer in reversed(range(LAYERS)):
         if layer > 0:
@@ -818,32 +845,26 @@
 
         def over_sides(values):
             values = values.astype(BF)
-            values = (values.astype(F32) + swap_row(values).astype(F32)).astype(BF)
+            there = swap_row(values)
+            if layer > 0:
+                there = after(there, reducer.arrived)
+            values = (values.astype(F32) + there.astype(F32)).astype(BF)
             return values, swap_core(values)
 
         if layer > 0:
             mine, other = over_sides(jnp.concatenate([grad_branch, grad_wide], 0))
             mine, other = (mine[:shard], mine[shard:]), (other[:shard], other[shard:])
         else:
-            grad_wide = grad_wide.astype(BF)
-            there = swap_row(grad_wide)
-            low = jnp.where(side == 0, grad_wide, there)
-            high = jnp.where(side == 0, there, grad_wide)
-            part = shard // 2
-            low_down, high_down = low[part:], high[part:]
-            grad_wide = jnp.concatenate(
-                [
-                    low[:part],
-                    high[:part],
-                    jnp.concatenate([low_down[:, :features], high_down[:, :features]], 1),
-                    jnp.concatenate([low_down[:, features:], high_down[:, features:]], 1),
-                ],
-                0,
-            )
-            mine, other = zip(over_sides(grad_branch), (grad_wide, swap_core(grad_wide)))
+            mine, other = over_sides(grad_branch)
+            wide_mine = grad_wide.astype(BF)
+            wide_there = after(swap_row(wide_mine), settled)
+            mine = (mine, wide_mine, wide_there)
+            other = (other, swap_core(wide_mine), swap_core(wide_there))
         if direct:
-            settled = settle(row_core, mine + other, settled, layer, matrix_shapes)
+            settled = settle(where, mine + other, settled, layer, matrix_shapes)
             continue
+        if layer == 0:
+            mine, other = (mine[0], by_side(*mine[1:])), (other[0], by_side(*other[1:]))
         low = [jnp.where(core == 0, m, o).astype(F32) for m, o in zip(mine, other)]
         high = [jnp.where(core == 0, o, m).astype(F32) for m, o in zip(mine, other)]
         done = []

time: 482 us -> 424 us (0.88)
  waiting for transfers between devices: 208 us -> 160 us
  local copies, waits for them, and re-layouts: 63.5 us -> 45.9 us
  starting transfers between devices: 49.9 us -> 59.5 us
  other arithmetic: 35.8 us -> 29 us
    ppermute x22, waiting for transfers between devices: 158 us -> 93.1 us  [swap_line(): return lax.ppermute(values, 'wt', pairs)]
    ppermute x11, waiting for transfers between devices: 14.7 us -> 30.9 us  [swap_pair(): return lax.ppermute(values, 'wt', pairs)]
    unnamed x222 -> x191, local copies, waits for them, and re-layouts: 32.2 us -> 19.3 us
    ppermute x22, starting transfers between devices: 23.3 us -> 31.4 us  [swap_line(): return lax.ppermute(values, 'wt', pairs)]
    squeeze x17 -> x16, local copies, waits for them, and re-layouts: 11.8 us -> 13.5 us  [picked(): return lax.dynamic_index_in_dim(values, index, axis, keepdims=False)]
  transfers between devices with their start and end apart: 63 -> 64, of which waited for: 29 -> 26; matrix products, arithmetic and copies ran while one was open for 20% -> 21% of each run, Pallas kernels for 14% -> 17%
where the time goes in v4:
time: 424 us; the launch traced here: 418 us
  waiting for transfers between devices  160 us (38%)
  Pallas kernels  78.6 us (19%)
  starting transfers between devices  59.5 us (14%)
  local copies, waits for them, and re-layouts  45.9 us (11%)
  matrix products  41.4 us (10%)
  other arithmetic  29 us (7%)
    ppermute x22, waiting for transfers between devices, swap_line(): return lax.ppermute(values, 'wt', pairs)  93.1 us
    ppermute x14, waiting for transfers between devices, swap_row(): return lax.ppermute(values, 'seq', pairs)  36.1 us
    ppermute x22, starting transfers between devices, swap_line(): return lax.ppermute(values, 'wt', pairs)  31.4 us
    ppermute x11, waiting for transfers between devices, swap_pair(): return lax.ppermute(values, 'wt', pairs)  30.9 us
    pallas_call x6, Pallas kernels, place(): pl.pallas_call(lambda *refs: place_kernel(fill, *refs), grid_spec=pltpu.P...  20.8 us
    unnamed x191, local copies, waits for them, and re-layouts  19.3 us
    pallas_call x2, Pallas kernels, attend_back(): pl.pallas_call(attend_back_kernel, grid=(steps,), in_specs=[pl.BlockSpec(...  16.4 us
    pallas_call x4, Pallas kernels, norm_back(): pl.pallas_call(norm_back_kernel, grid_spec=pltpu.PrefetchScalarGridSpec(n...  15.2 us
  transfers between devices with their start and end apart: 64, of which 26 were waited for; matrix products, arithmetic and copies ran while one was open for 21% of the time, Pallas kernels for 17%

profile of v4, /device:TPU:0, one launch (start us, length us, event | category | flops | bytes accessed | tf_op | source)
XLA Modules:
  0.0 417.9 jit_solution(7383995154564587358)
XLA Ops:
  1.3 2.5 pack.2
  3.8 4.0 collective-permute-start.2
  10.2 2.5 pack.3
  12.8 3.0 collective-permute-done.6
  15.9 2.6 collective-permute-done
  18.6 2.8 collective-permute-done.2
  21.6 4.2 collective-permute-start.4
  28.4 16.1 %collective-permute-done.5 = bf16[1,96,1536]{2,1,0:T(8,128)(2,1)S(1)} collective-permute-done((bf16[1,96,1536]{2,1,0:T(8,128)(2,1)S(1)}, bf16[1,96,1536]{2,1,0:T(8,128)(2,1)S(1)}, u32[]{:S(2)}, u32[]{:S(2)}) %collective-permute-start.5) | collective-permute-done | bytes 294944 | tf_op jit(solution)/shard_map/ppermute | solution.py:87
  48.4 2.7 collective-permute-start.10
  53.2 17.6 %collective-permute-done.8 = bf16[2,2,1152]{2,1,0:T(2,128)(2,1)S(1)} collective-permute-done((bf16[2,2,1152]{2,1,0:T(2,128)(2,1)S(1)}, bf16[2,2,1152]{2,1,0:T(2,128)(2,1)S(1)}, u32[]{:S(2)}, u32[]{:S(2)}) %collective-permute-start.8) | collective-permute-done | bytes 9248 | tf_op jit(solution)/shard_map/ppermute | solution.py:87
  83.1 8.2 %collective-permute-done.19 = bf16[1,96,1536]{2,1,0:T(8,128)(2,1)} collective-permute-done((bf16[1,96,1536]{2,1,0:T(8,128)(2,1)S(1)}, bf16[1,96,1536]{2,1,0:T(8,128)(2,1)}, u32[]{:S(2)}, u32[]{:S(2)}) %collective-permute-start.19) | collective-permute-done | bytes 294944 | tf_op jit(solution)/shard_map/ppermute | solution.py:87
  95.5 8.5 %collective-permute-done.17.refs_4_ = bf16[4,96,1536]{2,1,0:T(8,128)(2,1)} collective-permute-done((bf16[4,96,1536]{2,1,0:T(8,128)(2,1)}, bf16[4,96,1536]{2,1,0:T(8,128)(2,1)}, u32[]{:S(2)}, u32[]{:S(2)}) %collective-permute-start.17) | collective-permute-done | bytes 1179680 | tf_op jit(solution)/shard_map/ppermute | solution.py:61
  110.9 3.2 place_in.2
  116.8 5.7 %attend.2 = bf16[512,384]{1,0:T(8,128)(2,1)S(1)} custom-call(bf16[512,1152]{1,0:T(8,128)(2,1)S(1)} %fusion.12.q_ref.k_ref.v_ref, bf16[512,1152]{1,0:T(8,128)(2,1)S(1)} %fusion.12.q_ref.k_ref.v_ref, bf16[512,1152]{1,0:T(8,128)(2,1)S(1)} %fusion.12.q_ref.k_ref.v_ref), custom_call_target="tpu_custom_call" | custom-call | flops 6899999744 | bytes 22140000 | tf_op jit(solution)/shard_map/attend/pallas_call | solution.py:232
  123.0 4.9 %place_wide.2 = (bf16[4,2,2,48,1536]{4,3,2,1,0:T(8,128)(2,1)}, bf16[4,2,2,2,48,768]{5,4,3,2,1,0:T(8,128)(2,1)}) custom-call(s32[4]{0:T(128)S(1)} %copy-done.4, bf16[4,96,1536]{2,1,0:T(8,128)(2,1)S(1)} %copy-done.3, bf16[4,96,1536]{2,1,0:T(8,128)(2,1)} %collective-permute-done.11.refs_2_, bf16[4,96,1536]{2,1,0:T(8,128)(2,1)S(1)} %copy-done.8, ...), custom_call_target="tpu_custom_call" | custom-call | flops 3449999872 | bytes 11070000 | tf_op jit(solution)/shard_map/place_wide/pallas_call | solution.py:108
  128.8 2.5 place_out.2
  135.0 3.0 multiply_convert_fusion.1
  140.5 2.8 fusion.64
  148.9 2.9 norm_next.4
  151.8 14.6 %collective-permute-done.25.refs_4_ = bf16[4,96,1536]{2,1,0:T(8,128)(2,1)} collective-permute-done((bf16[4,96,1536]{2,1,0:T(8,128)(2,1)}, bf16[4,96,1536]{2,1,0:T(8,128)(2,1)}, u32[]{:S(2)}, u32[]{:S(2)}) %collective-permute-start.25) | collective-permute-done | bytes 1179680 | tf_op jit(solution)/shard_map/ppermute | solution.py:61
  167.8 2.7 place_in.3
  172.9 5.7 %attend.3 = bf16[512,384]{1,0:T(8,128)(2,1)S(1)} custom-call(bf16[512,1152]{1,0:T(8,128)(2,1)S(1)} %fusion.13.q_ref.k_ref.v_ref, bf16[512,1152]{1,0:T(8,128)(2,1)S(1)} %fusion.13.q_ref.k_ref.v_ref, bf16[512,1152]{1,0:T(8,128)(2,1)S(1)} %fusion.13.q_ref.k_ref.v_ref), custom_call_target="tpu_custom_call" | custom-call | flops 6899999744 | bytes 22140000 | tf_op jit(solution)/shard_map/attend/pallas_call | solution.py:232
  178.6 4.9 %place_wide.3 = (bf16[4,2,2,48,1536]{4,3,2,1,0:T(8,128)(2,1)}, bf16[4,2,2,2,48,768]{5,4,3,2,1,0:T(8,128)(2,1)}) custom-call(s32[4]{0:T(128)S(1)} %copy-done.4, bf16[4,96,1536]{2,1,0:T(8,128)(2,1)S(1)} %copy-done.1, bf16[4,96,1536]{2,1,0:T(8,128)(2,1)} %collective-permute-done.20.refs_2_, bf16[4,96,1536]{2,1,0:T(8,128)(2,1)S(1)} %copy-done.6, ...), custom_call_target="tpu_custom_call" | custom-call | flops 3449999872 | bytes 11070000 | tf_op jit(solution)/shard_map/place_wide/pallas_call | solution.py:108
  183.6 2.5 place_out.3
  193.2 2.9 fusion.65
  196.1 2.9 convolution_convert_fusion.2
  205.0 2.5 dynamic-slice_bitcast_fusion.2
  209.0 3.9 norm_back.4
  215.3 8.2 %attend_back.2 = (bf16[512,384]{1,0:T(8,128)(2,1)S(1)}, bf16[512,384]{1,0:T(8,128)(2,1)S(1)}, bf16[512,384]{1,0:T(8,128)(2,1)S(1)}) custom-call(bf16[512,1152]{1,0:T(8,128)(2,1)S(1)} %copy-done.30, bf16[512,1152]{1,0:T(8,128)(2,1)S(1)} %copy-done.30, bf16[512,1152]{1,0:T(8,128)(2,1)S(1)} %copy-done.30, bf16[512,384]{1,0:T(8,128)(2,1)S(1)} %convolution_convert_fusion.9.eo_ref), custom_call_target="tpu_custom_call" | custom-call | flops 9429999616 | bytes 30258000 | tf_op jit(solution)/shard_map/attend_back/pallas_call | solution.py:268
  230.3 2.6 collective-permute-done.29
  236.4 2.9 collective-permute-done.31
  240.1 3.6 norm_back.5
  243.8 3.4 convolution_convert_fusion.1
  249.6 2.8 fusion.67
  252.4 2.8 convolution_convert_fusion
  258.0 2.6 dynamic-slice_bitcast_fusion.1
  270.3 3.7 norm_back.6
  276.4 8.2 %attend_back.3 = (bf16[512,384]{1,0:T(8,128)(2,1)S(1)}, bf16[512,384]{1,0:T(8,128)(2,1)S(1)}, bf16[512,384]{1,0:T(8,128)(2,1)S(1)}) custom-call(bf16[512,1152]{1,0:T(8,128)(2,1)S(1)} %copy-done.28, bf16[512,1152]{1,0:T(8,128)(2,1)S(1)} %copy-done.28, bf16[512,1152]{1,0:T(8,128)(2,1)S(1)} %copy-done.28, bf16[512,384]{1,0:T(8,128)(2,1)S(1)} %convolution_convert_fusion.8.eo_ref), custom_call_target="tpu_custom_call" | custom-call | flops 9429999616 | bytes 30258000 | tf_op jit(solution)/shard_map/attend_back/pallas_call | solution.py:268
  291.6 4.1 norm_back.7
  306.3 9.5 %collective-permute-done.43 = bf16[96,1536]{1,0:T(8,128)(2,1)S(1)} collective-permute-done((bf16[96,1536]{1,0:T(8,128)(2,1)S(1)}, bf16[96,1536]{1,0:T(8,128)(2,1)S(1)}, u32[]{:S(2)}, u32[]{:S(2)}) %collective-permute-start.43) | collective-permute-done | bytes 294944 | tf_op jit(solution)/shard_map/ppermute | solution.py:87
  315.8 9.0 %collective-permute-done.42 = bf16[2,96,1536]{2,1,0:T(8,128)(2,1)S(1)} collective-permute-done((bf16[2,96,1536]{2,1,0:T(8,128)(2,1)S(1)}, bf16[2,96,1536]{2,1,0:T(8,128)(2,1)S(1)}, u32[]{:S(2)}, u32[]{:S(2)}) %collective-permute-start.42) | collective-permute-done | bytes 589856 | tf_op jit(solution)/shard_map/ppermute | solution.py:87
  336.0 23.8 %collective-permute-done.46 = f32[4,1920]{1,0:T(4,128)S(1)} collective-permute-done((f32[4,1920]{1,0:T(4,128)S(1)}, f32[4,1920]{1,0:T(4,128)S(1)}, u32[]{:S(2)}, u32[]{:S(2)}) %collective-permute-start.46) | collective-permute-done | bytes 30752 | tf_op jit(solution)/shard_map/ppermute | solution.py:74
  369.0 17.2 %collective-permute-done.50 = f32[2,1920]{1,0:T(2,128)S(1)} collective-permute-done((f32[2,1920]{1,0:T(2,128)S(1)}, f32[2,1920]{1,0:T(2,128)S(1)}, u32[]{:S(2)}, u32[]{:S(2)}) %collective-permute-start.50) | collective-permute-done | bytes 15392 | tf_op jit(solution)/shard_map/ppermute | solution.py:87
  386.3 2.6 collective-permute-start.53
  393.4 8.4 %collective-permute-done.57 = bf16[96,1536]{1,0:T(8,128)(2,1)S(1)} collective-permute-done((bf16[96,1536]{1,0:T(8,128)(2,1)S(1)}, bf16[96,1536]{1,0:T(8,128)(2,1)S(1)}, u32[]{:S(2)}, u32[]{:S(2)}) %collective-permute-start.57) | collective-permute-done | bytes 294944 | tf_op jit(solution)/shard_map/ppermute | solution.py:87
  407.5 2.5 settle.2
  410.0 3.4 collective-permute-done.58.refs_2_
  414.9 2.5 settle.3
  (482 shorter events, 148.9 us)
Async XLA Ops:
  3.8 17.6 %collective-permute-start.2 = (bf16[1,96,1536]{2,1,0:T(8,128)(2,1)}, bf16[1,96,1536]{2,1,0:T(8,128)(2,1)S(1)}, u32[]{:S(2)}, u32[]{:S(2)}) collective-permute-start(bf16[1,96,1536]{2,1,0:T(8,128)(2,1)} %bitcast.291), channel_id=1, source_target_pairs={{0,4},{1,5},{2,6},{3,7},{4,0},{5,1},{6,2},{7,3},{8,12},{9,13},{10,... | collective-permute-start | bytes 884744 | tf_op jit(solution)/shard_map/ppermute | solution.py:87
  15.8 11.4 %collective-permute-start.7 = (bf16[256,768]{1,0:T(8,128)(2,1)S(1)}, bf16[256,768]{1,0:T(8,128)(2,1)S(1)}, u32[]{:S(2)}, u32[]{:S(2)}) collective-permute-start(bf16[256,768]{1,0:T(8,128)(2,1)S(1)} %pad_maximum_fusion.10), channel_id=1, source_target_pairs={{0,8},{8,0},{16,24},{24,16},{1,9},{9,1},{17,25},{25,17},{2,10},{10... | collective-permute-start | bytes 1179656 | tf_op jit(solution)/shard_map/ppermute | solution.py:56
  21.6 23.7 %collective-permute-start.4 = (bf16[2,96,1536]{2,1,0:T(8,128)(2,1)S(1)}, bf16[2,96,1536]{2,1,0:T(8,128)(2,1)S(1)}, u32[]{:S(2)}, u32[]{:S(2)}) collective-permute-start(bf16[2,96,1536]{2,1,0:T(8,128)(2,1)S(1)} %pad_maximum_fusion.3), channel_id=1, source_target_pairs={{0,2},{1,3},{2,0},{3,1},{4,6},{5,7},{6,4},{7,5},{8,10},{9,11},{10,... | collective-permute-start | bytes 1769480 | tf_op jit(solution)/shard_map/ppermute | solution.py:87
  25.7 18.8 %collective-permute-start.5 = (bf16[1,96,1536]{2,1,0:T(8,128)(2,1)S(1)}, bf16[1,96,1536]{2,1,0:T(8,128)(2,1)S(1)}, u32[]{:S(2)}, u32[]{:S(2)}) collective-permute-start(bf16[1,96,1536]{2,1,0:T(8,128)(2,1)S(1)} %bitcast.289), channel_id=1, source_target_pairs={{0,4},{1,5},{2,6},{3,7},{4,0},{5,1},{6,2},{7,3},{8,12},{9,13},{10,... | collective-permute-start | bytes 884744 | tf_op jit(solution)/shard_map/ppermute | solution.py:87
  45.3 27.2 %collective-permute-start.11 = (bf16[4,96,1536]{2,1,0:T(8,128)(2,1)S(1)}, bf16[4,96,1536]{2,1,0:T(8,128)(2,1)}, u32[]{:S(2)}, u32[]{:S(2)}) collective-permute-start(bf16[4,96,1536]{2,1,0:T(8,128)(2,1)S(1)} %constant_dynamic-update-slice_fusion.2.refs_1_), channel_id=1, source_target_pairs={{0,1},{1,0},{2,3},{3,2},{4,5},{5,4},{6,7},{7,6},{8,9},{9,8},{10,11... | collective-permute-start | bytes 3538952 | tf_op jit(solution)/shard_map/ppermute | solution.py:74
  46.9 26.8 %collective-permute-start.12 = (bf16[4,96,1536]{2,1,0:T(8,128)(2,1)S(1)}, bf16[4,96,1536]{2,1,0:T(8,128)(2,1)S(1)}, u32[]{:S(2)}, u32[]{:S(2)}) collective-permute-start(bf16[4,96,1536]{2,1,0:T(8,128)(2,1)S(1)} %constant_dynamic-update-slice_fusion.2.refs_1_), channel_id=1, source_target_pairs={{0,16},{8,24},{16,0},{24,8},{1,17},{9,25},{17,1},{25,9},{2,18},{10... | collective-permute-start | bytes 3538952 | tf_op jit(solution)/shard_map/ppermute | solution.py:61
  48.4 22.4 %collective-permute-start.10 = (bf16[1,96,1536]{2,1,0:T(8,128)(2,1)S(1)}, bf16[1,96,1536]{2,1,0:T(8,128)(2,1)S(1)}, u32[]{:S(2)}, u32[]{:S(2)}) collective-permute-start(bf16[1,96,1536]{2,1,0:T(8,128)(2,1)S(1)} %bitcast.287), channel_id=1, source_target_pairs={{0,4},{1,5},{2,6},{3,7},{4,0},{5,1},{6,2},{7,3},{8,12},{9,13},{10,... | collective-permute-start | bytes 884744 | tf_op jit(solution)/shard_map/ppermute | solution.py:87
  51.1 20.6 %collective-permute-start.9 = (bf16[2,96,1536]{2,1,0:T(8,128)(2,1)S(1)}, bf16[2,96,1536]{2,1,0:T(8,128)(2,1)S(1)}, u32[]{:S(2)}, u32[]{:S(2)}) collective-permute-start(bf16[2,96,1536]{2,1,0:T(8,128)(2,1)S(1)} %pad_maximum_fusion.4), channel_id=1, source_target_pairs={{0,2},{1,3},{2,0},{3,1},{4,6},{5,7},{6,4},{7,5},{8,10},{9,11},{10,... | collective-permute-start | bytes 1769480 | tf_op jit(solution)/shard_map/ppermute | solution.py:87
  51.1 19.7 %collective-permute-start.8 = (bf16[2,2,1152]{2,1,0:T(2,128)(2,1)S(1)}, bf16[2,2,1152]{2,1,0:T(2,128)(2,1)S(1)}, u32[]{:S(2)}, u32[]{:S(2)}) collective-permute-start(bf16[2,2,1152]{2,1,0:T(2,128)(2,1)S(1)} %pad_maximum_fusion.15), channel_id=1, source_target_pairs={{0,2},{1,3},{2,0},{3,1},{4,6},{5,7},{6,4},{7,5},{8,10},{9,11},{10,... | collective-permute-start | bytes 27656 | tf_op jit(solution)/shard_map/ppermute | solution.py:87
  73.7 19.9 %collective-permute-start.18 = (bf16[2,96,1536]{2,1,0:T(8,128)(2,1)}, bf16[2,96,1536]{2,1,0:T(8,128)(2,1)}, u32[]{:S(2)}, u32[]{:S(2)}) collective-permute-start(bf16[2,96,1536]{2,1,0:T(8,128)(2,1)} %pad_maximum_fusion.6), channel_id=1, source_target_pairs={{0,2},{1,3},{2,0},{3,1},{4,6},{5,7},{6,4},{7,5},{8,10},{9,11},{10,... | collective-permute-start | bytes 1769480 | tf_op jit(solution)/shard_map/ppermute | solution.py:87
  76.1 15.2 %collective-permute-start.19 = (bf16[1,96,1536]{2,1,0:T(8,128)(2,1)S(1)}, bf16[1,96,1536]{2,1,0:T(8,128)(2,1)}, u32[]{:S(2)}, u32[]{:S(2)}) collective-permute-start(bf16[1,96,1536]{2,1,0:T(8,128)(2,1)S(1)} %bitcast.285), channel_id=1, source_target_pairs={{0,4},{1,5},{2,6},{3,7},{4,0},{5,1},{6,2},{7,3},{8,12},{9,13},{10,... | collective-permute-start | bytes 884744 | tf_op jit(solution)/shard_map/ppermute | solution.py:87
  78.5 25.5 %collective-permute-start.17 = (bf16[4,96,1536]{2,1,0:T(8,128)(2,1)}, bf16[4,96,1536]{2,1,0:T(8,128)(2,1)}, u32[]{:S(2)}, u32[]{:S(2)}) collective-permute-start(bf16[4,96,1536]{2,1,0:T(8,128)(2,1)} %collective-permute-done.11.refs_2_), channel_id=1, source_target_pairs={{0,16},{8,24},{16,0},{24,8},{1,17},{9,25},{17,1},{25,9},{2,18},{10... | collective-permute-start | bytes 3538952 | tf_op jit(solution)/shard_map/ppermute | solution.py:61
  80.0 25.9 %collective-permute-start.14 = (bf16[4,96,1536]{2,1,0:T(8,128)(2,1)S(1)}, bf16[4,96,1536]{2,1,0:T(8,128)(2,1)}, u32[]{:S(2)}, u32[]{:S(2)}) collective-permute-start(bf16[4,96,1536]{2,1,0:T(8,128)(2,1)S(1)} %constant_dynamic-update-slice_fusion.4.refs_1_), channel_id=1, source_target_pairs={{0,1},{1,0},{2,3},{3,2},{4,5},{5,4},{6,7},{7,6},{8,9},{9,8},{10,11... | collective-permute-start | bytes 3538952 | tf_op jit(solution)/shard_map/ppermute | solution.py:74
  105.9 32.1 %collective-permute-start.20 = (bf16[4,96,1536]{2,1,0:T(8,128)(2,1)}, bf16[4,96,1536]{2,1,0:T(8,128)(2,1)}, u32[]{:S(2)}, u32[]{:S(2)}) collective-permute-start(bf16[4,96,1536]{2,1,0:T(8,128)(2,1)} %constant_dynamic-update-slice_fusion.6.refs_1_), channel_id=1, source_target_pairs={{0,1},{1,0},{2,3},{3,2},{4,5},{5,4},{6,7},{7,6},{8,9},{9,8},{10,11... | collective-permute-start | bytes 3538952 | tf_op jit(solution)/shard_map/ppermute | solution.py:74
  107.4 30.6 %collective-permute-start.21 = (bf16[4,96,1536]{2,1,0:T(8,128)(2,1)}, bf16[4,96,1536]{2,1,0:T(8,128)(2,1)S(1)}, u32[]{:S(2)}, u32[]{:S(2)}) collective-permute-start(bf16[4,96,1536]{2,1,0:T(8,128)(2,1)} %constant_dynamic-update-slice_fusion.6.refs_1_), channel_id=1, source_target_pairs={{0,16},{8,24},{16,0},{24,8},{1,17},{9,25},{17,1},{25,9},{2,18},{10... | collective-permute-start | bytes 3538952 | tf_op jit(solution)/shard_map/ppermute | solution.py:61
  107.7 23.7 %collective-permute-start.22 = (bf16[2,96,1536]{2,1,0:T(8,128)(2,1)S(1)}, bf16[2,96,1536]{2,1,0:T(8,128)(2,1)S(1)}, u32[]{:S(2)}, u32[]{:S(2)}) collective-permute-start(bf16[2,96,1536]{2,1,0:T(8,128)(2,1)S(1)} %pad_maximum_fusion.7), channel_id=1, source_target_pairs={{0,2},{1,3},{2,0},{3,1},{4,6},{5,7},{6,4},{7,5},{8,10},{9,11},{10,... | collective-permute-start | bytes 1769480 | tf_op jit(solution)/shard_map/ppermute | solution.py:87
  110.8 18.1 %collective-permute-start.16 = (bf16[4,96,768]{2,1,0:T(8,128)(2,1)S(1)}, bf16[4,96,768]{2,1,0:T(8,128)(2,1)S(1)}, u32[]{:S(2)}, u32[]{:S(2)}) collective-permute-start(bf16[4,96,768]{2,1,0:T(8,128)(2,1)S(1)} %pad_maximum_fusion.5), channel_id=1, source_target_pairs={{0,8},{8,0},{16,24},{24,16},{1,9},{9,1},{17,25},{25,17},{2,10},{10... | collective-permute-start | bytes 1769480 | tf_op jit(solution)/shard_map/ppermute | solution.py:56
  122.5 9.9 %collective-permute-start.15 = (bf16[512,384]{1,0:T(8,128)(2,1)S(1)}, bf16[512,384]{1,0:T(8,128)(2,1)S(1)}, u32[]{:S(2)}, u32[]{:S(2)}) collective-permute-start(bf16[512,384]{1,0:T(8,128)(2,1)S(1)} %attend.2), channel_id=1, source_target_pairs={{0,8},{8,0},{16,24},{24,16},{1,9},{9,1},{17,25},{25,17},{2,10},{10... | collective-permute-start | bytes 1179656 | tf_op jit(solution)/shard_map/ppermute | solution.py:56
  138.1 28.3 %collective-permute-start.25 = (bf16[4,96,1536]{2,1,0:T(8,128)(2,1)}, bf16[4,96,1536]{2,1,0:T(8,128)(2,1)}, u32[]{:S(2)}, u32[]{:S(2)}) collective-permute-start(bf16[4,96,1536]{2,1,0:T(8,128)(2,1)} %collective-permute-done.20.refs_2_), channel_id=1, source_target_pairs={{0,16},{8,24},{16,0},{24,8},{1,17},{9,25},{17,1},{25,9},{2,18},{10... | collective-permute-start | bytes 3538952 | tf_op jit(solution)/shard_map/ppermute | solution.py:61
  139.9 27.8 %collective-permute-start.24 = (bf16[4,96,1536]{2,1,0:T(8,128)(2,1)}, bf16[4,96,1536]{2,1,0:T(8,128)(2,1)S(1)}, u32[]{:S(2)}, u32[]{:S(2)}) collective-permute-start(bf16[4,96,1536]{2,1,0:T(8,128)(2,1)} %constant_dynamic-update-slice_fusion.8.refs_1_), channel_id=1, source_target_pairs={{0,1},{1,0},{2,3},{3,2},{4,5},{5,4},{6,7},{7,6},{8,9},{9,8},{10,11... | collective-permute-start | bytes 3538952 | tf_op jit(solution)/shard_map/ppermute | solution.py:74
  170.5 13.0 %collective-permute-start.27 = (bf16[4,96,768]{2,1,0:T(8,128)(2,1)S(1)}, bf16[4,96,768]{2,1,0:T(8,128)(2,1)S(1)}, u32[]{:S(2)}, u32[]{:S(2)}) collective-permute-start(bf16[4,96,768]{2,1,0:T(8,128)(2,1)S(1)} %pad_maximum_fusion.8), channel_id=1, source_target_pairs={{0,8},{8,0},{16,24},{24,16},{1,9},{9,1},{17,25},{25,17},{2,10},{10... | collective-permute-start | bytes 1769480 | tf_op jit(solution)/shard_map/ppermute | solution.py:56
  204.4 28.6 %collective-permute-start.29 = (bf16[4,192,768]{2,1,0:T(8,128)(2,1)}, bf16[4,192,768]{2,1,0:T(8,128)(2,1)}, u32[]{:S(2)}, u32[]{:S(2)}) collective-permute-start(bf16[4,192,768]{2,1,0:T(8,128)(2,1)} %dynamic-slice_bitcast_fusion.5), channel_id=1, source_target_pairs={{0,1},{1,0},{2,3},{3,2},{4,5},{5,4},{6,7},{7,6},{8,9},{9,8},{10,11... | collective-permute-start | bytes 3538952 | tf_op jit(solution)/shard_map/ppermute | solution.py:74
  226.4 13.7 %collective-permute-start.32 = (bf16[512,768]{1,0:T(8,128)(2,1)S(1)}, bf16[512,768]{1,0:T(8,128)(2,1)S(1)}, u32[]{:S(2)}, u32[]{:S(2)}) collective-permute-start(bf16[512,768]{1,0:T(8,128)(2,1)S(1)} %get-tuple-element.252), channel_id=1, source_target_pairs={{0,8},{8,0},{16,24},{24,16},{1,9},{9,1},{17,25},{25,17},{2,10},{10... | collective-permute-start | bytes 2359304 | tf_op jit(solution)/shard_map/ppermute | solution.py:56
  235.8 25.9 %collective-permute-start.36 = (bf16[2,192,768]{2,1,0:T(8,128)(2,1)}, bf16[2,192,768]{2,1,0:T(8,128)(2,1)}, u32[]{:S(2)}, u32[]{:S(2)}) collective-permute-start(bf16[2,192,768]{2,1,0:T(8,128)(2,1)} %dynamic-slice_bitcast_fusion.10), channel_id=1, source_target_pairs={{0,2},{1,3},{2,0},{3,1},{4,6},{5,7},{6,4},{7,5},{8,10},{9,11},{10,... | collective-permute-start | bytes 1769480 | tf_op jit(solution)/shard_map/ppermute | solution.py:87
  235.9 27.8 %collective-permute-start.35 = (bf16[4,96,1536]{2,1,0:T(8,128)(2,1)}, bf16[4,96,1536]{2,1,0:T(8,128)(2,1)}, u32[]{:S(2)}, u32[]{:S(2)}) collective-permute-start(bf16[4,96,1536]{2,1,0:T(8,128)(2,1)} %dynamic-slice_bitcast_fusion.2), channel_id=1, source_target_pairs={{0,1},{1,0},{2,3},{3,2},{4,5},{5,4},{6,7},{7,6},{8,9},{9,8},{10,11... | collective-permute-start | bytes 3538952 | tf_op jit(solution)/shard_map/ppermute | solution.py:74
  257.7 12.6 %collective-permute-start.33 = (bf16[512,768]{1,0:T(8,128)(2,1)}, bf16[512,768]{1,0:T(8,128)(2,1)S(1)}, u32[]{:S(2)}, u32[]{:S(2)}) collective-permute-start(bf16[512,768]{1,0:T(8,128)(2,1)} %get-tuple-element.254), channel_id=1, source_target_pairs={{0,8},{8,0},{16,24},{24,16},{1,9},{9,1},{17,25},{25,17},{2,10},{10... | collective-permute-start | bytes 2359304 | tf_op jit(solution)/shard_map/ppermute | solution.py:56
  263.7 33.9 %collective-permute-start.40 = (bf16[8,48,1536]{2,1,0:T(8,128)(2,1)}, bf16[8,48,1536]{2,1,0:T(8,128)(2,1)}, u32[]{:S(2)}, u32[]{:S(2)}) collective-permute-start(bf16[8,48,1536]{2,1,0:T(8,128)(2,1)} %fusion.24), channel_id=1, source_target_pairs={{0,16},{8,24},{16,0},{24,8},{1,17},{9,25},{17,1},{25,9},{2,18},{10... | collective-permute-start | bytes 3538952 | tf_op jit(solution)/shard_map/ppermute | solution.py:61
  264.9 26.1 %collective-permute-start.39 = (bf16[192,768]{1,0:T(8,128)(2,1)S(1)}, bf16[192,768]{1,0:T(8,128)(2,1)S(1)}, u32[]{:S(2)}, u32[]{:S(2)}) collective-permute-start(bf16[192,768]{1,0:T(8,128)(2,1)S(1)} %dynamic-slice_bitcast_fusion.15), channel_id=1, source_target_pairs={{0,4},{1,5},{2,6},{3,7},{4,0},{5,1},{6,2},{7,3},{8,12},{9,13},{10,... | collective-permute-start | bytes 884744 | tf_op jit(solution)/shard_map/ppermute | solution.py:87
  268.0 28.2 %collective-permute-start.38 = (bf16[2,96,1536]{2,1,0:T(8,128)(2,1)}, bf16[2,96,1536]{2,1,0:T(8,128)(2,1)}, u32[]{:S(2)}, u32[]{:S(2)}) collective-permute-start(bf16[2,96,1536]{2,1,0:T(8,128)(2,1)} %dynamic-slice_bitcast_fusion.9), channel_id=1, source_target_pairs={{0,2},{1,3},{2,0},{3,1},{4,6},{5,7},{6,4},{7,5},{8,10},{9,11},{10,... | collective-permute-start | bytes 1769480 | tf_op jit(solution)/shard_map/ppermute | solution.py:87
  269.7 27.9 %collective-permute-start.37 = (bf16[4,96,1536]{2,1,0:T(8,128)(2,1)}, bf16[4,96,1536]{2,1,0:T(8,128)(2,1)}, u32[]{:S(2)}, u32[]{:S(2)}) collective-permute-start(bf16[4,96,1536]{2,1,0:T(8,128)(2,1)} %dynamic-slice_bitcast_fusion.3), channel_id=1, source_target_pairs={{0,1},{1,0},{2,3},{3,2},{4,5},{5,4},{6,7},{7,6},{8,9},{9,8},{10,11... | collective-permute-start | bytes 3538952 | tf_op jit(solution)/shard_map/ppermute | solution.py:74
  297.6 28.6 %collective-permute-start.41 = (bf16[4,96,1536]{2,1,0:T(8,128)(2,1)}, bf16[4,96,1536]{2,1,0:T(8,128)(2,1)S(1)}, u32[]{:S(2)}, u32[]{:S(2)}) collective-permute-start(bf16[4,96,1536]{2,1,0:T(8,128)(2,1)} %dynamic-slice_bitcast_fusion.4), channel_id=1, source_target_pairs={{0,1},{1,0},{2,3},{3,2},{4,5},{5,4},{6,7},{7,6},{8,9},{9,8},{10,11... | collective-permute-start | bytes 3538952 | tf_op jit(solution)/shard_map/ppermute | solution.py:74
  299.2 28.3 %collective-permute-start.44 = (bf16[8,48,1536]{2,1,0:T(8,128)(2,1)}, bf16[8,48,1536]{2,1,0:T(8,128)(2,1)S(1)}, u32[]{:S(2)}, u32[]{:S(2)}) collective-permute-start(bf16[8,48,1536]{2,1,0:T(8,128)(2,1)} %dynamic-slice_bitcast_fusion.1), channel_id=1, source_target_pairs={{0,16},{8,24},{16,0},{24,8},{1,17},{9,25},{17,1},{25,9},{2,18},{10... | collective-permute-start | bytes 3538952 | tf_op jit(solution)/shard_map/ppermute | solution.py:61
  299.6 16.2 %collective-permute-start.43 = (bf16[96,1536]{1,0:T(8,128)(2,1)S(1)}, bf16[96,1536]{1,0:T(8,128)(2,1)S(1)}, u32[]{:S(2)}, u32[]{:S(2)}) collective-permute-start(bf16[96,1536]{1,0:T(8,128)(2,1)S(1)} %dynamic-slice_bitcast_fusion.14), channel_id=1, source_target_pairs={{0,4},{1,5},{2,6},{3,7},{4,0},{5,1},{6,2},{7,3},{8,12},{9,13},{10,... | collective-permute-start | bytes 884744 | tf_op jit(solution)/shard_map/ppermute | solution.py:87
  303.9 21.0 %collective-permute-start.42 = (bf16[2,96,1536]{2,1,0:T(8,128)(2,1)S(1)}, bf16[2,96,1536]{2,1,0:T(8,128)(2,1)S(1)}, u32[]{:S(2)}, u32[]{:S(2)}) collective-permute-start(bf16[2,96,1536]{2,1,0:T(8,128)(2,1)S(1)} %dynamic-slice_bitcast_fusion.8), channel_id=1, source_target_pairs={{0,2},{1,3},{2,0},{3,1},{4,6},{5,7},{6,4},{7,5},{8,10},{9,11},{10,... | collective-permute-start | bytes 1769480 | tf_op jit(solution)/shard_map/ppermute | solution.py:87
  327.5 35.9 %collective-permute-start.48 = (bf16[2,96,1536]{2,1,0:T(8,128)(2,1)}, bf16[2,96,1536]{2,1,0:T(8,128)(2,1)}, u32[]{:S(2)}, u32[]{:S(2)}) collective-permute-start(bf16[2,96,1536]{2,1,0:T(8,128)(2,1)} %dynamic-slice_bitcast_fusion.7), channel_id=1, source_target_pairs={{0,2},{1,3},{2,0},{3,1},{4,6},{5,7},{6,4},{7,5},{8,10},{9,11},{10,... | collective-permute-start | bytes 1769480 | tf_op jit(solution)/shard_map/ppermute | solution.py:87
  327.8 32.1 %collective-permute-start.49 = (bf16[96,1536]{1,0:T(8,128)(2,1)}, bf16[96,1536]{1,0:T(8,128)(2,1)}, u32[]{:S(2)}, u32[]{:S(2)}) collective-permute-start(bf16[96,1536]{1,0:T(8,128)(2,1)} %dynamic-slice_bitcast_fusion.13), channel_id=1, source_target_pairs={{0,4},{1,5},{2,6},{3,7},{4,0},{5,1},{6,2},{7,3},{8,12},{9,13},{10,... | collective-permute-start | bytes 884744 | tf_op jit(solution)/shard_map/ppermute | solution.py:87
  331.9 32.7 %collective-permute-start.47 = (bf16[4,96,1536]{2,1,0:T(8,128)(2,1)}, bf16[4,96,1536]{2,1,0:T(8,128)(2,1)}, u32[]{:S(2)}, u32[]{:S(2)}) collective-permute-start(bf16[4,96,1536]{2,1,0:T(8,128)(2,1)} %dynamic-slice_bitcast_fusion), channel_id=1, source_target_pairs={{0,1},{1,0},{2,3},{3,2},{4,5},{5,4},{6,7},{7,6},{8,9},{9,8},{10,11... | collective-permute-start | bytes 3538952 | tf_op jit(solution)/shard_map/ppermute | solution.py:74
  333.4 26.4 %collective-permute-start.46 = (f32[4,1920]{1,0:T(4,128)S(1)}, f32[4,1920]{1,0:T(4,128)S(1)}, u32[]{:S(2)}, u32[]{:S(2)}) collective-permute-start(f32[4,1920]{1,0:T(4,128)S(1)} %bitcast.301), channel_id=1, source_target_pairs={{0,1},{1,0},{2,3},{3,2},{4,5},{5,4},{6,7},{7,6},{8,9},{9,8},{10,11... | collective-permute-start | bytes 92168 | tf_op jit(solution)/shard_map/ppermute | solution.py:74
  334.7 27.7 %collective-permute-start.45 = (f32[128,768]{1,0:T(8,128)}, f32[128,768]{1,0:T(8,128)S(1)}, u32[]{:S(2)}, u32[]{:S(2)}) collective-permute-start(f32[128,768]{1,0:T(8,128)} %get-tuple-element.214), channel_id=1, source_target_pairs={{0,16},{8,24},{16,0},{24,8},{1,17},{9,25},{17,1},{25,9},{2,18},{10... | collective-permute-start | bytes 1179656 | tf_op jit(solution)/shard_map/ppermute | solution.py:61
  361.0 32.4 %collective-permute-start.59 = (bf16[288,1536]{1,0:T(8,128)(2,1)S(1)}, bf16[288,1536]{1,0:T(8,128)(2,1)S(1)}, u32[]{:S(2)}, u32[]{:S(2)}) collective-permute-start(bf16[288,1536]{1,0:T(8,128)(2,1)S(1)} %maximum_maximum_fusion), channel_id=1, source_target_pairs={{0,16},{8,24},{16,0},{24,8},{1,17},{9,25},{17,1},{25,9},{2,18},{10... | collective-permute-start | bytes 2654216 | tf_op jit(solution)/shard_map/ppermute | solution.py:61
  366.2 20.1 %collective-permute-start.51 = (bf16[2,96,1536]{2,1,0:T(8,128)(2,1)S(1)}, bf16[2,96,1536]{2,1,0:T(8,128)(2,1)S(1)}, u32[]{:S(2)}, u32[]{:S(2)}) collective-permute-start(bf16[2,96,1536]{2,1,0:T(8,128)(2,1)S(1)} %dynamic-slice_bitcast_fusion.6), channel_id=1, source_target_pairs={{0,2},{1,3},{2,0},{3,1},{4,6},{5,7},{6,4},{7,5},{8,10},{9,11},{10,... | collective-permute-start | bytes 1769480 | tf_op jit(solution)/shard_map/ppermute | solution.py:87
  368.1 18.2 %collective-permute-start.50 = (f32[2,1920]{1,0:T(2,128)S(1)}, f32[2,1920]{1,0:T(2,128)S(1)}, u32[]{:S(2)}, u32[]{:S(2)}) collective-permute-start(f32[2,1920]{1,0:T(2,128)S(1)} %bitcast.306), channel_id=1, source_target_pairs={{0,2},{1,3},{2,0},{3,1},{4,6},{5,7},{6,4},{7,5},{8,10},{9,11},{10,... | collective-permute-start | bytes 46088 | tf_op jit(solution)/shard_map/ppermute | solution.py:87
  368.4 17.9 %collective-permute-start.52 = (bf16[96,1536]{1,0:T(8,128)(2,1)S(1)}, bf16[96,1536]{1,0:T(8,128)(2,1)S(1)}, u32[]{:S(2)}, u32[]{:S(2)}) collective-permute-start(bf16[96,1536]{1,0:T(8,128)(2,1)S(1)} %dynamic-slice_bitcast_fusion.12), channel_id=1, source_target_pairs={{0,4},{1,5},{2,6},{3,7},{4,0},{5,1},{6,2},{7,3},{8,12},{9,13},{10,... | collective-permute-start | bytes 884744 | tf_op jit(solution)/shard_map/ppermute | solution.py:87
  389.2 12.6 %collective-permute-start.57 = (bf16[96,1536]{1,0:T(8,128)(2,1)S(1)}, bf16[96,1536]{1,0:T(8,128)(2,1)S(1)}, u32[]{:S(2)}, u32[]{:S(2)}) collective-permute-start(bf16[96,1536]{1,0:T(8,128)(2,1)S(1)} %dynamic-slice_bitcast_fusion.11), channel_id=1, source_target_pairs={{0,4},{1,5},{2,6},{3,7},{4,0},{5,1},{6,2},{7,3},{8,12},{9,13},{10,... | collective-permute-start | bytes 884744 | tf_op jit(solution)/shard_map/ppermute | solution.py:87
  389.7 12.4 %collective-permute-start.56 = (bf16[96,1536]{1,0:T(8,128)(2,1)S(1)}, bf16[96,1536]{1,0:T(8,128)(2,1)S(1)}, u32[]{:S(2)}, u32[]{:S(2)}) collective-permute-start(bf16[96,1536]{1,0:T(8,128)(2,1)S(1)} %fusion.34), channel_id=1, source_target_pairs={{0,16},{8,24},{16,0},{24,8},{1,17},{9,25},{17,1},{25,9},{2,18},{10... | collective-permute-start | bytes 884744 | tf_op jit(solution)/shard_map/ppermute | solution.py:61
  392.5 10.2 %collective-permute-start.54 = (f32[1920]{0:T(1024)S(1)}, f32[1920]{0:T(1024)S(1)}, u32[]{:S(2)}, u32[]{:S(2)}) collective-permute-start(f32[1920]{0:T(1024)S(1)} %add.328), channel_id=1, source_target_pairs={{0,16},{8,24},{16,0},{24,8},{1,17},{9,25},{17,1},{25,9},{2,18},{10... | collective-permute-start | bytes 23048 | tf_op jit(solution)/shard_map/ppermute | solution.py:61
  402.2 12.4 %collective-permute-start.61 = (bf16[96,1536]{1,0:T(8,128)(2,1)S(1)}, bf16[96,1536]{1,0:T(8,128)(2,1)S(1)}, u32[]{:S(2)}, u32[]{:S(2)}) collective-permute-start(bf16[96,1536]{1,0:T(8,128)(2,1)S(1)} %add_convert_fusion.3.refs_0_), channel_id=1, source_target_pairs={{0,8},{8,0},{16,24},{24,16},{1,9},{9,1},{17,25},{25,17},{2,10},{10... | collective-permute-start | bytes 884744 | tf_op jit(solution)/shard_map/ppermute | solution.py:56
  405.2 9.4 %collective-permute-start.62 = (bf16[96,1536]{1,0:T(8,128)(2,1)S(1)}, bf16[96,1536]{1,0:T(8,128)(2,1)S(1)}, u32[]{:S(2)}, u32[]{:S(2)}) collective-permute-start(bf16[96,1536]{1,0:T(8,128)(2,1)S(1)} %fusion.33.refs_1_), channel_id=1, source_target_pairs={{0,8},{8,0},{16,24},{24,16},{1,9},{9,1},{17,25},{25,17},{2,10},{10... | collective-permute-start | bytes 884744 | tf_op jit(solution)/shard_map/ppermute | solution.py:56
  (104 other events, 547.2 us)

commit v5 on v4

--- a/solution.py
+++ b/solution.py
@@ -12,7 +12,7 @@
 epsilon = 1e-05
 BF = jnp.bfloat16
 F32 = jnp.float32
-VMEM_BYTES = 48 * 1024 * 1024
+VMEM_BYTES = 32 * 1024 * 1024
 
 VECTORS = (
     "first_scale",
@@ -94,6 +94,42 @@
 
 def place_kernel(fill, where_ref, *refs):
     fill(where_ref, *refs)
+
+
+def last_kernel(where_ref, source_ref, *refs):
+    up, down = refs[-2:]
+    rows = source_ref.shape[1] // 2
+    features = down.shape[-1]
+    up[0, 0, 0] = source_ref[0, :rows]
+    down[0, 0, 0, 0] = source_ref[0, rows:, :features]
+    down[0, 0, 0, 1] = source_ref[0, rows:, features:]
+
+
+def place_last(where, source, earlier):
+    depth, rows, width = source.shape
+
+    def spot_index(w, k, blank):
+        line = jnp.bitwise_xor(w[0], 2 * (k % 2) + k // 2)
+        return (line, 1 - w[1], 1 - w[2]) + (0,) * blank
+
+    return pl.pallas_call(
+        last_kernel,
+        grid_spec=pltpu.PrefetchScalarGridSpec(
+            num_scalar_prefetch=1,
+            grid=(depth,),
+            in_specs=[pl.BlockSpec((1, rows, width), lambda k, w: (k, 0, 0))]
+            + [pl.BlockSpec(memory_space=pl.ANY)] * 2,
+            out_specs=[
+                pl.BlockSpec((1, 1, 1) + v.shape[3:], lambda k, w, n=v.ndim: spot_index(w, k, n - 3))
+                for v in earlier
+            ],
+        ),
+        out_shape=[jax.ShapeDtypeStruct(v.shape, BF) for v in earlier],
+        input_output_aliases={2: 0, 3: 1},
+        compiler_params=pltpu.CompilerParams(vmem_limit_bytes=VMEM_BYTES),
+        cost_estimate=lasting(1.5),
+        name="place_last",
+    )(where, source, *earlier)
 
 
 def place(fill, where, sources, spots, name):
@@ -149,14 +185,13 @@
             target[spot + (slice(None), columns)] = source[0]
 
 
-def fill_wide(where_ref, near_ref, far_ref, near_there_ref, far_there_ref, up, down):
+def fill_wide(where_ref, near_ref, far_ref, near_there_ref, up, down):
     rows = near_ref.shape[1] // 2
     features = down.shape[-1]
     for source, across, over in (
         (near_ref, where_ref[1], where_ref[2]),
         (far_ref, 1 - where_ref[1], where_ref[2]),
         (near_there_ref, where_ref[1], 1 - where_ref[2]),
-        (far_there_ref, 1 - where_ref[1], 1 - where_ref[2]),
     ):
         up[0, across, over] = source[0, :rows]
         down[0, across, over, 0] = source[0, rows:, :features]
@@ -179,7 +214,7 @@
                         for v in values
                     ]
                 )
-            return None if beside is None else swap_row(beside)
+            return None if beside is None else jax.tree.map(swap_row, beside)
         own = lax.axis_index("wt")
         bits = (own % 2, own // 2 % 2, own // 4)
         moves = (swap_pair, lambda v: swap_line(v, 1), lambda v: swap_line(v, 2))
@@ -193,7 +228,7 @@
             sends = [[after(v, earlier) for v in send] for send in sends]
             beside = None if beside is None else after(beside, earlier)
         theirs = [[moves[i](v) for v in send] for i, send in zip(active, sends)]
-        swapped = None if beside is None else swap_row(beside)
+        swapped = None if beside is None else jax.tree.map(swap_row, beside)
         self.arrived = (theirs, swapped)
         following = [None, None, None]
         for i, there in zip(active, theirs):
@@ -628,13 +663,16 @@
             )
             gathered["out", layer] = gathered["out", layer].reshape(features, features)
             width = 2 * features
-            pieces = (wide[layer], wide_far[layer], wide_there[layer], wide_far_there[layer])
-            gathered["up", layer], gathered["down", layer] = place(
+            pieces = (wide[layer], wide_far[layer], wide_there[layer])
+            placed = place(
                 fill_wide,
                 where,
                 tuple((v, width, 0) for v in pieces),
                 ((2, 2, shard // 2, width), (2, 2, 2, shard // 2, features)),
                 "place_wide",
+            )
+            gathered["up", layer], gathered["down", layer] = place_last(
+                where, wide_far_there[layer], placed
             )
             gathered["up", layer] = gathered["up", layer].reshape(features, units // 2)
             gathered["down", layer] = gathered["down", layer].reshape(units // 2, features)
@@ -711,11 +749,11 @@
             vec["second_scale"],
             vec["second_shift"],
         )
+        if direct and layer == 0:
+            second = after(second, third)
         upward = matmul(second, up) + unit_rows[layer]
         activated, slope = gelu_parts(upward)
         activated = activated.astype(BF)
-        if direct and layer == 0:
-            activated = after(activated, third)
         slope = slope.astype(BF)
         kept.append((hidden, normed, qkv, mixture, middle, second, activated, slope))
         partial = matmul(activated, down)
@@ -728,11 +766,7 @@
                 vectors[layer + 1]["first_shift"],
             )
         else:
-            theirs = lax.dynamic_slice_in_dim(
-                partial, (1 - core) * 2 * frames_here, 2 * frames_here, 0
-            )
-            total = own_rows(partial) + swap_core(theirs.astype(BF))
-            result_rows = (own_rows(middle) + vec["down_bias"] + total).astype(BF)
+            last_rows = (partial, middle)
 
     grad_hidden = down_in.astype(F32)
     grad_down_bias = column_sums(down_in)[None]
@@ -774,10 +808,9 @@
         grad_branch = jnp.concatenate([grad_in, grad_out.astype(BF)], 1)
         grad_branch = grad_branch.reshape(owners, shard, 2 * features)
         if layer > 0:
-            result_there = reducer.tick(
-                [grad_up], grad_branch, beside=result_rows[frames_here:]
-            )
+            reducer.tick([grad_up], grad_branch)
         else:
+            last_rows = after(last_rows, reducer.arrived) if direct else last_rows
             up_there = reducer.tick([grad_branch], beside=picked(grad_up, 1 - side, 1))
             grad_wide = jnp.concatenate(
                 [
@@ -829,11 +862,19 @@
     from_units = from_units.reshape(LAYERS, owners, unit_half).swapaxes(0, 1)
     from_units = from_units.reshape(owners, LAYERS * unit_half)
     packed = jnp.concatenate([packed, from_units], 1)
-    before = after(before, (reducer.arrived, packed))
-    reducer.tick([grad_wide, packed])
-    result = from_chip(result_rows, result_there)
-    input_grad = from_chip(before, swap_row(before[frames_here:]))
+    partial, middle = last_rows
+    theirs = lax.dynamic_slice_in_dim(
+        partial, (1 - core) * 2 * frames_here, 2 * frames_here, 0
+    )
+    total = own_rows(partial) + swap_core(theirs.astype(BF))
+    last_bias = vectors[LAYERS - 1]["down_bias"]
+    result_rows = (own_rows(middle) + last_bias + total).astype(BF)
+    chip_there = reducer.tick(
+        [grad_wide, packed], beside=(result_rows[frames_here:], before[frames_here:])
+    )
     reducer.finish()
+    result = from_chip(result_rows, chip_there[0])
+    input_grad = from_chip(before, chip_there[1])
     for layer in reversed(range(LAYERS)):
         if layer > 0:
             (grad_down,), (grad_up,), (grad_branch,) = reducer.totals[:3]

time: 424 us -> 403 us (0.950)
  waiting for transfers between devices: 160 us -> 139 us
  local copies, waits for them, and re-layouts: 45.9 us -> 51.9 us
    ppermute x22, waiting for transfers between devices: 93.1 us -> 77 us  [swap_line(): return lax.ppermute(values, 'wt', pairs)]
    ppermute x14, waiting for transfers between devices: 36.1 us -> 27.4 us  [swap_row(): return lax.ppermute(values, 'seq', pairs)]
    pallas_call x4, Pallas kernels: 15.2 us -> 9.27 us  [norm_back(): pl.pallas_call(norm_back_kernel, grid_spec=pltpu.PrefetchScalarGridSpec(n...]
    unnamed x191 -> x203, local copies, waits for them, and re-layouts: 19.3 us -> 25 us
    pallas_call x0 -> x2, Pallas kernels: none -> 5.34 us  [place_last(): pl.pallas_call(last_kernel, grid_spec=pltpu.PrefetchScalarGridSpec(num_sc...]
  transfers between devices with their start and end apart: 64 -> 64, of which waited for: 26 -> 25; matrix products, arithmetic and copies ran while one was open for 21% -> 22% of each run, Pallas kernels for 17% -> 16%
where the time goes in v5:
time: 403 us; the launch traced here: 399 us
  waiting for transfers between devices  139 us (34%)
  Pallas kernels  74.6 us (19%)
  starting transfers between devices  61.8 us (15%)
  local copies, waits for them, and re-layouts  51.9 us (13%)
  matrix products  42.2 us (10%)
  other arithmetic  26.1 us (6%)
    ppermute x22, waiting for transfers between devices, swap_line(): return lax.ppermute(values, 'wt', pairs)  77 us
    ppermute x11, waiting for transfers between devices, swap_pair(): return lax.ppermute(values, 'wt', pairs)  34 us
    ppermute x22, starting transfers between devices, swap_line(): return lax.ppermute(values, 'wt', pairs)  30.9 us
    ppermute x14, waiting for transfers between devices, swap_row(): return lax.ppermute(values, 'seq', pairs)  27.4 us
    unnamed x203, local copies, waits for them, and re-layouts  25 us
    ppermute x14, starting transfers between devices, swap_row(): return lax.ppermute(values, 'seq', pairs)  17.6 us
    pallas_call x6, Pallas kernels, place(): pl.pallas_call(lambda *refs: place_kernel(fill, *refs), grid_spec=pltpu.P...  17.5 us
    pallas_call x2, Pallas kernels, attend_back(): pl.pallas_call(attend_back_kernel, grid=(steps,), in_specs=[pl.BlockSpec(...  16.4 us
  transfers between devices with their start and end apart: 64, of which 25 were waited for; matrix products, arithmetic and copies ran while one was open for 22% of the time, Pallas kernels for 16%

profile of v5, /device:TPU:0, one launch (start us, length us, event | category | flops | bytes accessed | tf_op | source)
XLA Modules:
  0.0 398.8 jit_solution(18263612388029671321)
XLA Ops:
  1.3 2.5 pack.2
  3.8 4.0 %collective-permute-start.2 = (bf16[1,96,1536]{2,1,0:T(8,128)(2,1)}, bf16[1,96,1536]{2,1,0:T(8,128)(2,1)S(1)}, u32[]{:S(2)}, u32[]{:S(2)}) collective-permute-start(bf16[1,96,1536]{2,1,0:T(8,128)(2,1)} %bitcast.296), channel_id=1, source_target_pairs={{0,4},{1,5},{2,6},{3,7},{4,0},{5,1},{6,2},{7,3},{8,12},{9,13},{10,... | collective-permute-start | bytes 884744 | tf_op jit(solution)/shard_map/ppermute | solution.py:87
  10.2 2.5 pack.3
  12.8 3.0 collective-permute-done.6
  15.9 2.6 collective-permute-done
  18.6 2.8 collective-permute-done.2
  21.6 4.2 %collective-permute-start.4 = (bf16[2,96,1536]{2,1,0:T(8,128)(2,1)S(1)}, bf16[2,96,1536]{2,1,0:T(8,128)(2,1)S(1)}, u32[]{:S(2)}, u32[]{:S(2)}) collective-permute-start(bf16[2,96,1536]{2,1,0:T(8,128)(2,1)S(1)} %pad_maximum_fusion.3), channel_id=1, source_target_pairs={{0,2},{1,3},{2,0},{3,1},{4,6},{5,7},{6,4},{7,5},{8,10},{9,11},{10,... | collective-permute-start | bytes 1769480 | tf_op jit(solution)/shard_map/ppermute | solution.py:87
  28.4 16.1 %collective-permute-done.5 = bf16[1,96,1536]{2,1,0:T(8,128)(2,1)S(1)} collective-permute-done((bf16[1,96,1536]{2,1,0:T(8,128)(2,1)S(1)}, bf16[1,96,1536]{2,1,0:T(8,128)(2,1)S(1)}, u32[]{:S(2)}, u32[]{:S(2)}) %collective-permute-start.5) | collective-permute-done | bytes 294944 | tf_op jit(solution)/shard_map/ppermute | solution.py:87
  48.4 2.7 collective-permute-start.10
  53.2 17.6 %collective-permute-done.8 = bf16[2,2,1152]{2,1,0:T(2,128)(2,1)S(1)} collective-permute-done((bf16[2,2,1152]{2,1,0:T(2,128)(2,1)S(1)}, bf16[2,2,1152]{2,1,0:T(2,128)(2,1)S(1)}, u32[]{:S(2)}, u32[]{:S(2)}) %collective-permute-start.8) | collective-permute-done | bytes 9248 | tf_op jit(solution)/shard_map/ppermute | solution.py:87
  79.6 3.3 place_wide.2
  86.6 16.4 %collective-permute-done.13 = bf16[4,2,1152]{2,1,0:T(2,128)(2,1)S(1)} collective-permute-done((bf16[4,2,1152]{2,1,0:T(2,128)(2,1)S(1)}, bf16[4,2,1152]{2,1,0:T(2,128)(2,1)S(1)}, u32[]{:S(2)}, u32[]{:S(2)}) %collective-permute-start.13) | collective-permute-done | bytes 18464 | tf_op jit(solution)/shard_map/ppermute | solution.py:74
  110.6 2.7 place_in.2
  116.0 5.7 %attend.2 = bf16[512,384]{1,0:T(8,128)(2,1)S(1)} custom-call(bf16[512,1152]{1,0:T(8,128)(2,1)S(1)} %fusion.12.q_ref.k_ref.v_ref, bf16[512,1152]{1,0:T(8,128)(2,1)S(1)} %fusion.12.q_ref.k_ref.v_ref, bf16[512,1152]{1,0:T(8,128)(2,1)S(1)} %fusion.12.q_ref.k_ref.v_ref), custom_call_target="tpu_custom_call" | custom-call | flops 6899999744 | bytes 22140000 | tf_op jit(solution)/shard_map/attend/pallas_call | solution.py:267
  125.1 2.7 place_last.2
  128.8 2.6 place_out.2
  137.4 3.0 multiply_convert_fusion.1
  140.4 2.8 fusion.64
  148.8 3.0 place_wide.3
  151.8 2.7 norm_next.4
  154.5 8.3 %collective-permute-done.25.source_ref = bf16[4,96,1536]{2,1,0:T(8,128)(2,1)} collective-permute-done((bf16[4,96,1536]{2,1,0:T(8,128)(2,1)}, bf16[4,96,1536]{2,1,0:T(8,128)(2,1)}, u32[]{:S(2)}, u32[]{:S(2)}) %collective-permute-start.25) | collective-permute-done | bytes 1179680 | tf_op jit(solution)/shard_map/ppermute | solution.py:61
  164.1 3.0 place_in.3
  169.7 5.7 %attend.3 = bf16[512,384]{1,0:T(8,128)(2,1)S(1)} custom-call(bf16[512,1152]{1,0:T(8,128)(2,1)S(1)} %fusion.13.q_ref.k_ref.v_ref, bf16[512,1152]{1,0:T(8,128)(2,1)S(1)} %fusion.13.q_ref.k_ref.v_ref, bf16[512,1152]{1,0:T(8,128)(2,1)S(1)} %fusion.13.q_ref.k_ref.v_ref), custom_call_target="tpu_custom_call" | custom-call | flops 6899999744 | bytes 22140000 | tf_op jit(solution)/shard_map/attend/pallas_call | solution.py:267
  175.9 2.7 place_last.3
  178.6 2.8 place_out.3
  187.9 3.0 fusion.65
  190.9 2.8 convolution_convert_fusion.4
  199.2 2.6 dynamic-slice_bitcast_fusion.4
  201.8 4.1 %fusion.68 = f32[512,768]{1,0:T(8,128)} fusion(bf16[512,1536]{1,0:T(8,128)(2,1)} %copy-done.93, bf16[1536,768]{1,0:T(8,128)(2,1)S(1)} %bitcast.256), kind=kOutput, calls=%fused_computation.249 | convolution fusion | flops 1207959552 | bytes 5505024 | tf_op jit(solution)/shard_map/dot_general | solution.py:39
  205.9 3.3 norm_back.4
  210.4 8.2 %attend_back.2 = (bf16[512,384]{1,0:T(8,128)(2,1)S(1)}, bf16[512,384]{1,0:T(8,128)(2,1)S(1)}, bf16[512,384]{1,0:T(8,128)(2,1)S(1)}) custom-call(bf16[512,1152]{1,0:T(8,128)(2,1)S(1)} %copy-done.39, bf16[512,1152]{1,0:T(8,128)(2,1)S(1)} %copy-done.39, bf16[512,1152]{1,0:T(8,128)(2,1)S(1)} %copy-done.39, bf16[512,384]{1,0:T(8,128)(2,1)S(1)} %convolution_convert_fusion.9.eo_ref), custom_call_target="tpu_custom_call" | custom-call | flops 9429999616 | bytes 30258000 | tf_op jit(solution)/shard_map/attend_back/pallas_call | solution.py:303
  237.1 2.8 fusion.67
  239.9 2.8 convolution_convert_fusion
  245.5 2.5 dynamic-slice_bitcast_fusion.1
  251.2 6.4 %collective-permute-done.30 = bf16[4,96,1536]{2,1,0:T(8,128)(2,1)} collective-permute-done((bf16[4,96,1536]{2,1,0:T(8,128)(2,1)}, bf16[4,96,1536]{2,1,0:T(8,128)(2,1)}, u32[]{:S(2)}, u32[]{:S(2)}) %collective-permute-start.30) | collective-permute-done | bytes 1179680 | tf_op jit(solution)/shard_map/ppermute | solution.py:74
  266.8 8.2 %attend_back.3 = (bf16[512,384]{1,0:T(8,128)(2,1)S(1)}, bf16[512,384]{1,0:T(8,128)(2,1)S(1)}, bf16[512,384]{1,0:T(8,128)(2,1)S(1)}) custom-call(bf16[512,1152]{1,0:T(8,128)(2,1)S(1)} %copy-done.37, bf16[512,1152]{1,0:T(8,128)(2,1)S(1)} %copy-done.37, bf16[512,1152]{1,0:T(8,128)(2,1)S(1)} %copy-done.37, bf16[512,384]{1,0:T(8,128)(2,1)S(1)} %convolution_convert_fusion.8.eo_ref), custom_call_target="tpu_custom_call" | custom-call | flops 9429999616 | bytes 30258000 | tf_op jit(solution)/shard_map/attend_back/pallas_call | solution.py:303
  282.0 2.6 norm_back.7
  287.3 2.4 collective-permute-done.32
  298.3 8.0 %collective-permute-done.42 = bf16[96,1536]{1,0:T(8,128)(2,1)S(1)} collective-permute-done((bf16[96,1536]{1,0:T(8,128)(2,1)S(1)}, bf16[96,1536]{1,0:T(8,128)(2,1)S(1)}, u32[]{:S(2)}, u32[]{:S(2)}) %collective-permute-start.42) | collective-permute-done | bytes 294944 | tf_op jit(solution)/shard_map/ppermute | solution.py:87
  306.6 8.7 %collective-permute-done.41 = bf16[2,96,1536]{2,1,0:T(8,128)(2,1)S(1)} collective-permute-done((bf16[2,96,1536]{2,1,0:T(8,128)(2,1)S(1)}, bf16[2,96,1536]{2,1,0:T(8,128)(2,1)S(1)}, u32[]{:S(2)}, u32[]{:S(2)}) %collective-permute-start.41) | collective-permute-done | bytes 589856 | tf_op jit(solution)/shard_map/ppermute | solution.py:87
  326.7 9.9 %collective-permute-done.44 = bf16[128,768]{1,0:T(8,128)(2,1)S(1)} collective-permute-done((bf16[128,768]{1,0:T(8,128)(2,1)S(1)}, bf16[128,768]{1,0:T(8,128)(2,1)S(1)}, u32[]{:S(2)}, u32[]{:S(2)}) %collective-permute-start.44) | collective-permute-done | bytes 196640 | tf_op jit(solution)/shard_map/ppermute | solution.py:61
  343.6 5.8 %collective-permute-done.47 = bf16[4,96,1536]{2,1,0:T(8,128)(2,1)} collective-permute-done((bf16[4,96,1536]{2,1,0:T(8,128)(2,1)}, bf16[4,96,1536]{2,1,0:T(8,128)(2,1)}, u32[]{:S(2)}, u32[]{:S(2)}) %collective-permute-start.47) | collective-permute-done | bytes 1179680 | tf_op jit(solution)/shard_map/ppermute | solution.py:74
  354.1 15.3 %collective-permute-done.50 = f32[2,1920]{1,0:T(2,128)S(1)} collective-permute-done((f32[2,1920]{1,0:T(2,128)S(1)}, f32[2,1920]{1,0:T(2,128)S(1)}, u32[]{:S(2)}, u32[]{:S(2)}) %collective-permute-start.50) | collective-permute-done | bytes 15392 | tf_op jit(solution)/shard_map/ppermute | solution.py:87
  369.5 2.7 collective-permute-start.53
  377.7 5.9 %collective-permute-done.57 = bf16[96,1536]{1,0:T(8,128)(2,1)S(1)} collective-permute-done((bf16[96,1536]{1,0:T(8,128)(2,1)S(1)}, bf16[96,1536]{1,0:T(8,128)(2,1)S(1)}, u32[]{:S(2)}, u32[]{:S(2)}) %collective-permute-start.57) | collective-permute-done | bytes 294944 | tf_op jit(solution)/shard_map/ppermute | solution.py:87
  389.3 2.5 settle.2
  391.8 2.4 collective-permute-done.58.refs_2_
  395.8 2.5 settle.3
  (496 shorter events, 155.1 us)
Async XLA Ops:
  3.8 17.6 %collective-permute-start.2 = (bf16[1,96,1536]{2,1,0:T(8,128)(2,1)}, bf16[1,96,1536]{2,1,0:T(8,128)(2,1)S(1)}, u32[]{:S(2)}, u32[]{:S(2)}) collective-permute-start(bf16[1,96,1536]{2,1,0:T(8,128)(2,1)} %bitcast.296), channel_id=1, source_target_pairs={{0,4},{1,5},{2,6},{3,7},{4,0},{5,1},{6,2},{7,3},{8,12},{9,13},{10,... | collective-permute-start | bytes 884744 | tf_op jit(solution)/shard_map/ppermute | solution.py:87
  9.6 8.9 %collective-permute-start = (bf16[128,768]{1,0:T(8,128)(2,1)S(1)}, bf16[128,768]{1,0:T(8,128)(2,1)S(1)}, u32[]{:S(2)}, u32[]{:S(2)}) collective-permute-start(bf16[128,768]{1,0:T(8,128)(2,1)S(1)} %get-tuple-element.232), channel_id=1, source_target_pairs={{0,16},{8,24},{16,0},{24,8},{1,17},{9,25},{17,1},{25,9},{2,18},{10... | collective-permute-start | bytes 589832 | tf_op jit(solution)/shard_map/ppermute | solution.py:61
  15.8 11.4 %collective-permute-start.7 = (bf16[256,768]{1,0:T(8,128)(2,1)S(1)}, bf16[256,768]{1,0:T(8,128)(2,1)S(1)}, u32[]{:S(2)}, u32[]{:S(2)}) collective-permute-start(bf16[256,768]{1,0:T(8,128)(2,1)S(1)} %pad_maximum_fusion.10), channel_id=1, source_target_pairs={{0,8},{8,0},{16,24},{24,16},{1,9},{9,1},{17,25},{25,17},{2,10},{10... | collective-permute-start | bytes 1179656 | tf_op jit(solution)/shard_map/ppermute | solution.py:56
  21.6 23.7 %collective-permute-start.4 = (bf16[2,96,1536]{2,1,0:T(8,128)(2,1)S(1)}, bf16[2,96,1536]{2,1,0:T(8,128)(2,1)S(1)}, u32[]{:S(2)}, u32[]{:S(2)}) collective-permute-start(bf16[2,96,1536]{2,1,0:T(8,128)(2,1)S(1)} %pad_maximum_fusion.3), channel_id=1, source_target_pairs={{0,2},{1,3},{2,0},{3,1},{4,6},{5,7},{6,4},{7,5},{8,10},{9,11},{10,... | collective-permute-start | bytes 1769480 | tf_op jit(solution)/shard_map/ppermute | solution.py:87
  25.7 18.8 %collective-permute-start.5 = (bf16[1,96,1536]{2,1,0:T(8,128)(2,1)S(1)}, bf16[1,96,1536]{2,1,0:T(8,128)(2,1)S(1)}, u32[]{:S(2)}, u32[]{:S(2)}) collective-permute-start(bf16[1,96,1536]{2,1,0:T(8,128)(2,1)S(1)} %bitcast.294), channel_id=1, source_target_pairs={{0,4},{1,5},{2,6},{3,7},{4,0},{5,1},{6,2},{7,3},{8,12},{9,13},{10,... | collective-permute-start | bytes 884744 | tf_op jit(solution)/shard_map/ppermute | solution.py:87
  45.3 27.2 %collective-permute-start.11 = (bf16[4,96,1536]{2,1,0:T(8,128)(2,1)S(1)}, bf16[4,96,1536]{2,1,0:T(8,128)(2,1)}, u32[]{:S(2)}, u32[]{:S(2)}) collective-permute-start(bf16[4,96,1536]{2,1,0:T(8,128)(2,1)S(1)} %constant_dynamic-update-slice_fusion.2.refs_1_), channel_id=1, source_target_pairs={{0,1},{1,0},{2,3},{3,2},{4,5},{5,4},{6,7},{7,6},{8,9},{9,8},{10,11... | collective-permute-start | bytes 3538952 | tf_op jit(solution)/shard_map/ppermute | solution.py:74
  46.9 26.8 %collective-permute-start.12 = (bf16[4,96,1536]{2,1,0:T(8,128)(2,1)S(1)}, bf16[4,96,1536]{2,1,0:T(8,128)(2,1)S(1)}, u32[]{:S(2)}, u32[]{:S(2)}) collective-permute-start(bf16[4,96,1536]{2,1,0:T(8,128)(2,1)S(1)} %constant_dynamic-update-slice_fusion.2.refs_1_), channel_id=1, source_target_pairs={{0,16},{8,24},{16,0},{24,8},{1,17},{9,25},{17,1},{25,9},{2,18},{10... | collective-permute-start | bytes 3538952 | tf_op jit(solution)/shard_map/ppermute | solution.py:61
  48.4 22.4 %collective-permute-start.10 = (bf16[1,96,1536]{2,1,0:T(8,128)(2,1)S(1)}, bf16[1,96,1536]{2,1,0:T(8,128)(2,1)S(1)}, u32[]{:S(2)}, u32[]{:S(2)}) collective-permute-start(bf16[1,96,1536]{2,1,0:T(8,128)(2,1)S(1)} %bitcast.292), channel_id=1, source_target_pairs={{0,4},{1,5},{2,6},{3,7},{4,0},{5,1},{6,2},{7,3},{8,12},{9,13},{10,... | collective-permute-start | bytes 884744 | tf_op jit(solution)/shard_map/ppermute | solution.py:87
  51.1 19.8 %collective-permute-start.9 = (bf16[2,96,1536]{2,1,0:T(8,128)(2,1)S(1)}, bf16[2,96,1536]{2,1,0:T(8,128)(2,1)S(1)}, u32[]{:S(2)}, u32[]{:S(2)}) collective-permute-start(bf16[2,96,1536]{2,1,0:T(8,128)(2,1)S(1)} %pad_maximum_fusion.4), channel_id=1, source_target_pairs={{0,2},{1,3},{2,0},{3,1},{4,6},{5,7},{6,4},{7,5},{8,10},{9,11},{10,... | collective-permute-start | bytes 1769480 | tf_op jit(solution)/shard_map/ppermute | solution.py:87
  51.1 19.7 %collective-permute-start.8 = (bf16[2,2,1152]{2,1,0:T(2,128)(2,1)S(1)}, bf16[2,2,1152]{2,1,0:T(2,128)(2,1)S(1)}, u32[]{:S(2)}, u32[]{:S(2)}) collective-permute-start(bf16[2,2,1152]{2,1,0:T(2,128)(2,1)S(1)} %pad_maximum_fusion.15), channel_id=1, source_target_pairs={{0,2},{1,3},{2,0},{3,1},{4,6},{5,7},{6,4},{7,5},{8,10},{9,11},{10,... | collective-permute-start | bytes 27656 | tf_op jit(solution)/shard_map/ppermute | solution.py:87
  73.6 34.1 %collective-permute-start.19 = (bf16[4,96,1536]{2,1,0:T(8,128)(2,1)}, bf16[4,96,1536]{2,1,0:T(8,128)(2,1)}, u32[]{:S(2)}, u32[]{:S(2)}) collective-permute-start(bf16[4,96,1536]{2,1,0:T(8,128)(2,1)} %collective-permute-done.11.refs_2_), channel_id=1, source_target_pairs={{0,16},{8,24},{16,0},{24,8},{1,17},{9,25},{17,1},{25,9},{2,18},{10... | collective-permute-start | bytes 3538952 | tf_op jit(solution)/shard_map/ppermute | solution.py:61
  75.2 29.4 %collective-permute-start.18 = (bf16[1,96,1536]{2,1,0:T(8,128)(2,1)}, bf16[1,96,1536]{2,1,0:T(8,128)(2,1)}, u32[]{:S(2)}, u32[]{:S(2)}) collective-permute-start(bf16[1,96,1536]{2,1,0:T(8,128)(2,1)} %bitcast.20), channel_id=1, source_target_pairs={{0,4},{1,5},{2,6},{3,7},{4,0},{5,1},{6,2},{7,3},{8,12},{9,13},{10,... | collective-permute-start | bytes 884744 | tf_op jit(solution)/shard_map/ppermute | solution.py:87
  77.5 28.2 %collective-permute-start.17 = (bf16[2,96,1536]{2,1,0:T(8,128)(2,1)S(1)}, bf16[2,96,1536]{2,1,0:T(8,128)(2,1)}, u32[]{:S(2)}, u32[]{:S(2)}) collective-permute-start(bf16[2,96,1536]{2,1,0:T(8,128)(2,1)S(1)} %pad_maximum_fusion.6), channel_id=1, source_target_pairs={{0,2},{1,3},{2,0},{3,1},{4,6},{5,7},{6,4},{7,5},{8,10},{9,11},{10,... | collective-permute-start | bytes 1769480 | tf_op jit(solution)/shard_map/ppermute | solution.py:87
  77.5 30.1 %collective-permute-start.14 = (bf16[4,96,1536]{2,1,0:T(8,128)(2,1)S(1)}, bf16[4,96,1536]{2,1,0:T(8,128)(2,1)}, u32[]{:S(2)}, u32[]{:S(2)}) collective-permute-start(bf16[4,96,1536]{2,1,0:T(8,128)(2,1)S(1)} %constant_dynamic-update-slice_fusion.4.refs_1_), channel_id=1, source_target_pairs={{0,1},{1,0},{2,3},{3,2},{4,5},{5,4},{6,7},{7,6},{8,9},{9,8},{10,11... | collective-permute-start | bytes 3538952 | tf_op jit(solution)/shard_map/ppermute | solution.py:74
  78.1 24.9 %collective-permute-start.13 = (bf16[4,2,1152]{2,1,0:T(2,128)(2,1)S(1)}, bf16[4,2,1152]{2,1,0:T(2,128)(2,1)S(1)}, u32[]{:S(2)}, u32[]{:S(2)}) collective-permute-start(bf16[4,2,1152]{2,1,0:T(2,128)(2,1)S(1)} %constant_dynamic-update-slice_fusion), channel_id=1, source_target_pairs={{0,1},{1,0},{2,3},{3,2},{4,5},{5,4},{6,7},{7,6},{8,9},{9,8},{10,11... | collective-permute-start | bytes 55304 | tf_op jit(solution)/shard_map/ppermute | solution.py:74
  107.7 26.7 %collective-permute-start.20 = (bf16[4,96,1536]{2,1,0:T(8,128)(2,1)}, bf16[4,96,1536]{2,1,0:T(8,128)(2,1)}, u32[]{:S(2)}, u32[]{:S(2)}) collective-permute-start(bf16[4,96,1536]{2,1,0:T(8,128)(2,1)} %constant_dynamic-update-slice_fusion.6.refs_1_), channel_id=1, source_target_pairs={{0,1},{1,0},{2,3},{3,2},{4,5},{5,4},{6,7},{7,6},{8,9},{9,8},{10,11... | collective-permute-start | bytes 3538952 | tf_op jit(solution)/shard_map/ppermute | solution.py:74
  108.3 26.0 %collective-permute-start.21 = (bf16[4,96,1536]{2,1,0:T(8,128)(2,1)}, bf16[4,96,1536]{2,1,0:T(8,128)(2,1)S(1)}, u32[]{:S(2)}, u32[]{:S(2)}) collective-permute-start(bf16[4,96,1536]{2,1,0:T(8,128)(2,1)} %constant_dynamic-update-slice_fusion.6.refs_1_), channel_id=1, source_target_pairs={{0,16},{8,24},{16,0},{24,8},{1,17},{9,25},{17,1},{25,9},{2,18},{10... | collective-permute-start | bytes 3538952 | tf_op jit(solution)/shard_map/ppermute | solution.py:61
  108.8 19.0 %collective-permute-start.22 = (bf16[2,96,1536]{2,1,0:T(8,128)(2,1)S(1)}, bf16[2,96,1536]{2,1,0:T(8,128)(2,1)S(1)}, u32[]{:S(2)}, u32[]{:S(2)}) collective-permute-start(bf16[2,96,1536]{2,1,0:T(8,128)(2,1)S(1)} %pad_maximum_fusion.7), channel_id=1, source_target_pairs={{0,2},{1,3},{2,0},{3,1},{4,6},{5,7},{6,4},{7,5},{8,10},{9,11},{10,... | collective-permute-start | bytes 1769480 | tf_op jit(solution)/shard_map/ppermute | solution.py:87
  134.4 28.4 %collective-permute-start.25 = (bf16[4,96,1536]{2,1,0:T(8,128)(2,1)}, bf16[4,96,1536]{2,1,0:T(8,128)(2,1)}, u32[]{:S(2)}, u32[]{:S(2)}) collective-permute-start(bf16[4,96,1536]{2,1,0:T(8,128)(2,1)} %collective-permute-done.20.refs_2_), channel_id=1, source_target_pairs={{0,16},{8,24},{16,0},{24,8},{1,17},{9,25},{17,1},{25,9},{2,18},{10... | collective-permute-start | bytes 3538952 | tf_op jit(solution)/shard_map/ppermute | solution.py:61
  136.0 28.1 %collective-permute-start.24 = (bf16[4,96,1536]{2,1,0:T(8,128)(2,1)}, bf16[4,96,1536]{2,1,0:T(8,128)(2,1)}, u32[]{:S(2)}, u32[]{:S(2)}) collective-permute-start(bf16[4,96,1536]{2,1,0:T(8,128)(2,1)} %constant_dynamic-update-slice_fusion.8.refs_1_), channel_id=1, source_target_pairs={{0,1},{1,0},{2,3},{3,2},{4,5},{5,4},{6,7},{7,6},{8,9},{9,8},{10,11... | collective-permute-start | bytes 3538952 | tf_op jit(solution)/shard_map/ppermute | solution.py:74
  168.4 10.2 %collective-permute-start.27 = (bf16[4,96,768]{2,1,0:T(8,128)(2,1)S(1)}, bf16[4,96,768]{2,1,0:T(8,128)(2,1)S(1)}, u32[]{:S(2)}, u32[]{:S(2)}) collective-permute-start(bf16[4,96,768]{2,1,0:T(8,128)(2,1)S(1)} %pad_maximum_fusion.8), channel_id=1, source_target_pairs={{0,8},{8,0},{16,24},{24,16},{1,9},{9,1},{17,25},{25,17},{2,10},{10... | collective-permute-start | bytes 1769480 | tf_op jit(solution)/shard_map/ppermute | solution.py:56
  193.7 12.2 %collective-permute-start.28 = (bf16[512,768]{1,0:T(8,128)(2,1)}, bf16[512,768]{1,0:T(8,128)(2,1)}, u32[]{:S(2)}, u32[]{:S(2)}) collective-permute-start(bf16[512,768]{1,0:T(8,128)(2,1)} %get-tuple-element.262), channel_id=1, source_target_pairs={{0,8},{8,0},{16,24},{24,16},{1,9},{9,1},{17,25},{25,17},{2,10},{10... | collective-permute-start | bytes 2359304 | tf_op jit(solution)/shard_map/ppermute | solution.py:56
  197.7 28.7 %collective-permute-start.29 = (bf16[4,192,768]{2,1,0:T(8,128)(2,1)}, bf16[4,192,768]{2,1,0:T(8,128)(2,1)}, u32[]{:S(2)}, u32[]{:S(2)}) collective-permute-start(bf16[4,192,768]{2,1,0:T(8,128)(2,1)} %dynamic-slice_bitcast_fusion.3), channel_id=1, source_target_pairs={{0,1},{1,0},{2,3},{3,2},{4,5},{5,4},{6,7},{7,6},{8,9},{9,8},{10,11... | collective-permute-start | bytes 3538952 | tf_op jit(solution)/shard_map/ppermute | solution.py:74
  229.0 20.2 %collective-permute-start.31 = (bf16[2,192,768]{2,1,0:T(8,128)(2,1)S(1)}, bf16[2,192,768]{2,1,0:T(8,128)(2,1)}, u32[]{:S(2)}, u32[]{:S(2)}) collective-permute-start(bf16[2,192,768]{2,1,0:T(8,128)(2,1)S(1)} %dynamic-slice_bitcast_fusion.10), channel_id=1, source_target_pairs={{0,2},{1,3},{2,0},{3,1},{4,6},{5,7},{6,4},{7,5},{8,10},{9,11},{10,... | collective-permute-start | bytes 1769480 | tf_op jit(solution)/shard_map/ppermute | solution.py:87
  229.3 28.3 %collective-permute-start.30 = (bf16[4,96,1536]{2,1,0:T(8,128)(2,1)}, bf16[4,96,1536]{2,1,0:T(8,128)(2,1)}, u32[]{:S(2)}, u32[]{:S(2)}) collective-permute-start(bf16[4,96,1536]{2,1,0:T(8,128)(2,1)} %dynamic-slice_bitcast_fusion.4), channel_id=1, source_target_pairs={{0,1},{1,0},{2,3},{3,2},{4,5},{5,4},{6,7},{7,6},{8,9},{9,8},{10,11... | collective-permute-start | bytes 3538952 | tf_op jit(solution)/shard_map/ppermute | solution.py:74
  242.7 21.0 %collective-permute-start.38 = (bf16[512,768]{1,0:T(8,128)(2,1)}, bf16[512,768]{1,0:T(8,128)(2,1)S(1)}, u32[]{:S(2)}, u32[]{:S(2)}) collective-permute-start(bf16[512,768]{1,0:T(8,128)(2,1)} %get-tuple-element.266), channel_id=1, source_target_pairs={{0,8},{8,0},{16,24},{24,16},{1,9},{9,1},{17,25},{25,17},{2,10},{10... | collective-permute-start | bytes 2359304 | tf_op jit(solution)/shard_map/ppermute | solution.py:56
  257.6 29.7 %collective-permute-start.36 = (bf16[8,48,1536]{2,1,0:T(8,128)(2,1)}, bf16[8,48,1536]{2,1,0:T(8,128)(2,1)}, u32[]{:S(2)}, u32[]{:S(2)}) collective-permute-start(bf16[8,48,1536]{2,1,0:T(8,128)(2,1)} %fusion.24), channel_id=1, source_target_pairs={{0,16},{8,24},{16,0},{24,8},{1,17},{9,25},{17,1},{25,9},{2,18},{10... | collective-permute-start | bytes 3538952 | tf_op jit(solution)/shard_map/ppermute | solution.py:61
  258.1 23.3 %collective-permute-start.34 = (bf16[192,768]{1,0:T(8,128)(2,1)S(1)}, bf16[192,768]{1,0:T(8,128)(2,1)S(1)}, u32[]{:S(2)}, u32[]{:S(2)}) collective-permute-start(bf16[192,768]{1,0:T(8,128)(2,1)S(1)} %dynamic-slice_bitcast_fusion.15), channel_id=1, source_target_pairs={{0,4},{1,5},{2,6},{3,7},{4,0},{5,1},{6,2},{7,3},{8,12},{9,13},{10,... | collective-permute-start | bytes 884744 | tf_op jit(solution)/shard_map/ppermute | solution.py:87
  261.5 24.3 %collective-permute-start.33 = (bf16[2,96,1536]{2,1,0:T(8,128)(2,1)}, bf16[2,96,1536]{2,1,0:T(8,128)(2,1)}, u32[]{:S(2)}, u32[]{:S(2)}) collective-permute-start(bf16[2,96,1536]{2,1,0:T(8,128)(2,1)} %dynamic-slice_bitcast_fusion.9), channel_id=1, source_target_pairs={{0,2},{1,3},{2,0},{3,1},{4,6},{5,7},{6,4},{7,5},{8,10},{9,11},{10,... | collective-permute-start | bytes 1769480 | tf_op jit(solution)/shard_map/ppermute | solution.py:87
  263.2 26.5 %collective-permute-start.32 = (bf16[4,96,1536]{2,1,0:T(8,128)(2,1)}, bf16[4,96,1536]{2,1,0:T(8,128)(2,1)}, u32[]{:S(2)}, u32[]{:S(2)}) collective-permute-start(bf16[4,96,1536]{2,1,0:T(8,128)(2,1)} %dynamic-slice_bitcast_fusion.5), channel_id=1, source_target_pairs={{0,1},{1,0},{2,3},{3,2},{4,5},{5,4},{6,7},{7,6},{8,9},{9,8},{10,11... | collective-permute-start | bytes 3538952 | tf_op jit(solution)/shard_map/ppermute | solution.py:74
  289.7 26.5 %collective-permute-start.40 = (bf16[4,96,1536]{2,1,0:T(8,128)(2,1)}, bf16[4,96,1536]{2,1,0:T(8,128)(2,1)S(1)}, u32[]{:S(2)}, u32[]{:S(2)}) collective-permute-start(bf16[4,96,1536]{2,1,0:T(8,128)(2,1)} %dynamic-slice_bitcast_fusion.2), channel_id=1, source_target_pairs={{0,1},{1,0},{2,3},{3,2},{4,5},{5,4},{6,7},{7,6},{8,9},{9,8},{10,11... | collective-permute-start | bytes 3538952 | tf_op jit(solution)/shard_map/ppermute | solution.py:74
  290.3 27.1 %collective-permute-start.43 = (bf16[8,48,1536]{2,1,0:T(8,128)(2,1)S(1)}, bf16[8,48,1536]{2,1,0:T(8,128)(2,1)S(1)}, u32[]{:S(2)}, u32[]{:S(2)}) collective-permute-start(bf16[8,48,1536]{2,1,0:T(8,128)(2,1)S(1)} %copy-done.69), channel_id=1, source_target_pairs={{0,16},{8,24},{16,0},{24,8},{1,17},{9,25},{17,1},{25,9},{2,18},{10... | collective-permute-start | bytes 3538952 | tf_op jit(solution)/shard_map/ppermute | solution.py:61
  291.8 14.5 %collective-permute-start.42 = (bf16[96,1536]{1,0:T(8,128)(2,1)S(1)}, bf16[96,1536]{1,0:T(8,128)(2,1)S(1)}, u32[]{:S(2)}, u32[]{:S(2)}) collective-permute-start(bf16[96,1536]{1,0:T(8,128)(2,1)S(1)} %dynamic-slice_bitcast_fusion.14), channel_id=1, source_target_pairs={{0,4},{1,5},{2,6},{3,7},{4,0},{5,1},{6,2},{7,3},{8,12},{9,13},{10,... | collective-permute-start | bytes 884744 | tf_op jit(solution)/shard_map/ppermute | solution.py:87
  295.6 19.7 %collective-permute-start.41 = (bf16[2,96,1536]{2,1,0:T(8,128)(2,1)S(1)}, bf16[2,96,1536]{2,1,0:T(8,128)(2,1)S(1)}, u32[]{:S(2)}, u32[]{:S(2)}) collective-permute-start(bf16[2,96,1536]{2,1,0:T(8,128)(2,1)S(1)} %dynamic-slice_bitcast_fusion.8), channel_id=1, source_target_pairs={{0,2},{1,3},{2,0},{3,1},{4,6},{5,7},{6,4},{7,5},{8,10},{9,11},{10,... | collective-permute-start | bytes 1769480 | tf_op jit(solution)/shard_map/ppermute | solution.py:87
  296.1 10.2 %collective-permute-start.37 = (bf16[256,768]{1,0:T(8,128)(2,1)S(1)}, bf16[256,768]{1,0:T(8,128)(2,1)S(1)}, u32[]{:S(2)}, u32[]{:S(2)}) collective-permute-start(bf16[256,768]{1,0:T(8,128)(2,1)S(1)} %dynamic-slice_convert_fusion.1), channel_id=1, source_target_pairs={{0,8},{8,0},{16,24},{24,16},{1,9},{9,1},{17,25},{25,17},{2,10},{10... | collective-permute-start | bytes 1179656 | tf_op jit(solution)/shard_map/ppermute | solution.py:56
  317.3 25.1 %collective-permute-start.48 = (bf16[2,96,1536]{2,1,0:T(8,128)(2,1)}, bf16[2,96,1536]{2,1,0:T(8,128)(2,1)}, u32[]{:S(2)}, u32[]{:S(2)}) collective-permute-start(bf16[2,96,1536]{2,1,0:T(8,128)(2,1)} %dynamic-slice_bitcast_fusion.7), channel_id=1, source_target_pairs={{0,2},{1,3},{2,0},{3,1},{4,6},{5,7},{6,4},{7,5},{8,10},{9,11},{10,... | collective-permute-start | bytes 1769480 | tf_op jit(solution)/shard_map/ppermute | solution.py:87
  317.4 20.0 %collective-permute-start.49 = (bf16[96,1536]{1,0:T(8,128)(2,1)}, bf16[96,1536]{1,0:T(8,128)(2,1)}, u32[]{:S(2)}, u32[]{:S(2)}) collective-permute-start(bf16[96,1536]{1,0:T(8,128)(2,1)} %dynamic-slice_bitcast_fusion.13), channel_id=1, source_target_pairs={{0,4},{1,5},{2,6},{3,7},{4,0},{5,1},{6,2},{7,3},{8,12},{9,13},{10,... | collective-permute-start | bytes 884744 | tf_op jit(solution)/shard_map/ppermute | solution.py:87
  324.0 25.4 %collective-permute-start.47 = (bf16[4,96,1536]{2,1,0:T(8,128)(2,1)}, bf16[4,96,1536]{2,1,0:T(8,128)(2,1)}, u32[]{:S(2)}, u32[]{:S(2)}) collective-permute-start(bf16[4,96,1536]{2,1,0:T(8,128)(2,1)} %dynamic-slice_bitcast_fusion), channel_id=1, source_target_pairs={{0,1},{1,0},{2,3},{3,2},{4,5},{5,4},{6,7},{7,6},{8,9},{9,8},{10,11... | collective-permute-start | bytes 3538952 | tf_op jit(solution)/shard_map/ppermute | solution.py:74
  324.6 15.6 %collective-permute-start.45 = (f32[128,768]{1,0:T(8,128)}, f32[128,768]{1,0:T(8,128)}, u32[]{:S(2)}, u32[]{:S(2)}) collective-permute-start(f32[128,768]{1,0:T(8,128)} %get-tuple-element.171), channel_id=1, source_target_pairs={{0,16},{8,24},{16,0},{24,8},{1,17},{9,25},{17,1},{25,9},{2,18},{10... | collective-permute-start | bytes 1179656 | tf_op jit(solution)/shard_map/ppermute | solution.py:61
  326.1 10.6 %collective-permute-start.44 = (bf16[128,768]{1,0:T(8,128)(2,1)S(1)}, bf16[128,768]{1,0:T(8,128)(2,1)S(1)}, u32[]{:S(2)}, u32[]{:S(2)}) collective-permute-start(bf16[128,768]{1,0:T(8,128)(2,1)S(1)} %get-tuple-element.170), channel_id=1, source_target_pairs={{0,16},{8,24},{16,0},{24,8},{1,17},{9,25},{17,1},{25,9},{2,18},{10... | collective-permute-start | bytes 589832 | tf_op jit(solution)/shard_map/ppermute | solution.py:61
  338.6 39.1 %collective-permute-start.59 = (bf16[288,1536]{1,0:T(8,128)(2,1)S(1)}, bf16[288,1536]{1,0:T(8,128)(2,1)S(1)}, u32[]{:S(2)}, u32[]{:S(2)}) collective-permute-start(bf16[288,1536]{1,0:T(8,128)(2,1)S(1)} %maximum_maximum_fusion), channel_id=1, source_target_pairs={{0,16},{8,24},{16,0},{24,8},{1,17},{9,25},{17,1},{25,9},{2,18},{10... | collective-permute-start | bytes 2654216 | tf_op jit(solution)/shard_map/ppermute | solution.py:61
  351.1 18.4 %collective-permute-start.51 = (bf16[2,96,1536]{2,1,0:T(8,128)(2,1)S(1)}, bf16[2,96,1536]{2,1,0:T(8,128)(2,1)S(1)}, u32[]{:S(2)}, u32[]{:S(2)}) collective-permute-start(bf16[2,96,1536]{2,1,0:T(8,128)(2,1)S(1)} %dynamic-slice_bitcast_fusion.6), channel_id=1, source_target_pairs={{0,2},{1,3},{2,0},{3,1},{4,6},{5,7},{6,4},{7,5},{8,10},{9,11},{10,... | collective-permute-start | bytes 1769480 | tf_op jit(solution)/shard_map/ppermute | solution.py:87
  352.9 16.5 %collective-permute-start.50 = (f32[2,1920]{1,0:T(2,128)S(1)}, f32[2,1920]{1,0:T(2,128)S(1)}, u32[]{:S(2)}, u32[]{:S(2)}) collective-permute-start(f32[2,1920]{1,0:T(2,128)S(1)} %bitcast.311), channel_id=1, source_target_pairs={{0,2},{1,3},{2,0},{3,1},{4,6},{5,7},{6,4},{7,5},{8,10},{9,11},{10,... | collective-permute-start | bytes 46088 | tf_op jit(solution)/shard_map/ppermute | solution.py:87
  353.2 16.3 %collective-permute-start.52 = (bf16[96,1536]{1,0:T(8,128)(2,1)S(1)}, bf16[96,1536]{1,0:T(8,128)(2,1)S(1)}, u32[]{:S(2)}, u32[]{:S(2)}) collective-permute-start(bf16[96,1536]{1,0:T(8,128)(2,1)S(1)} %dynamic-slice_bitcast_fusion.12), channel_id=1, source_target_pairs={{0,4},{1,5},{2,6},{3,7},{4,0},{5,1},{6,2},{7,3},{8,12},{9,13},{10,... | collective-permute-start | bytes 884744 | tf_op jit(solution)/shard_map/ppermute | solution.py:87
  372.4 11.2 %collective-permute-start.57 = (bf16[96,1536]{1,0:T(8,128)(2,1)S(1)}, bf16[96,1536]{1,0:T(8,128)(2,1)S(1)}, u32[]{:S(2)}, u32[]{:S(2)}) collective-permute-start(bf16[96,1536]{1,0:T(8,128)(2,1)S(1)} %dynamic-slice_bitcast_fusion.11), channel_id=1, source_target_pairs={{0,4},{1,5},{2,6},{3,7},{4,0},{5,1},{6,2},{7,3},{8,12},{9,13},{10,... | collective-permute-start | bytes 884744 | tf_op jit(solution)/shard_map/ppermute | solution.py:87
  372.8 11.1 %collective-permute-start.56 = (bf16[96,1536]{1,0:T(8,128)(2,1)S(1)}, bf16[96,1536]{1,0:T(8,128)(2,1)S(1)}, u32[]{:S(2)}, u32[]{:S(2)}) collective-permute-start(bf16[96,1536]{1,0:T(8,128)(2,1)S(1)} %fusion.34), channel_id=1, source_target_pairs={{0,16},{8,24},{16,0},{24,8},{1,17},{9,25},{17,1},{25,9},{2,18},{10... | collective-permute-start | bytes 884744 | tf_op jit(solution)/shard_map/ppermute | solution.py:61
  384.0 11.5 %collective-permute-start.61 = (bf16[96,1536]{1,0:T(8,128)(2,1)S(1)}, bf16[96,1536]{1,0:T(8,128)(2,1)S(1)}, u32[]{:S(2)}, u32[]{:S(2)}) collective-permute-start(bf16[96,1536]{1,0:T(8,128)(2,1)S(1)} %add_convert_fusion.3.refs_0_), channel_id=1, source_target_pairs={{0,8},{8,0},{16,24},{24,16},{1,9},{9,1},{17,25},{25,17},{2,10},{10... | collective-permute-start | bytes 884744 | tf_op jit(solution)/shard_map/ppermute | solution.py:56
  384.8 9.4 %collective-permute-start.58 = (bf16[96,1536]{1,0:T(8,128)(2,1)S(1)}, bf16[96,1536]{1,0:T(8,128)(2,1)S(1)}, u32[]{:S(2)}, u32[]{:S(2)}) collective-permute-start(bf16[96,1536]{1,0:T(8,128)(2,1)S(1)} %fusion.33.refs_1_), channel_id=1, source_target_pairs={{0,16},{8,24},{16,0},{24,8},{1,17},{9,25},{17,1},{25,9},{2,18},{10... | collective-permute-start | bytes 884744 | tf_op jit(solution)/shard_map/ppermute | solution.py:61
  (110 other events, 555.5 us)
